TPU v7x, 32 devices: a whole 2x2x4 slice. The times are simulated.
32 devices in a mesh: row: 8 (over z, core), col: 4 (over y, x).
Axes of the slice: x: 2, y: 2, z: 4, core: 2. Of those that a mesh axis runs over, the one named last changes fastest.
Arguments:
- buoy: bfloat16 [512, 512, 384], P('row', 'col'), may hold values from -6 to 6
- vel_w: bfloat16 [512, 512, 384], P('row', 'col'), may hold values from -6 to 6
- strat: float32 [576], P('col'), may hold values from 0.3 to 3
- eig_val: float32 [384], replicated, may hold values from 0.1 to 8
- eig_left: bfloat16 [384, 384], replicated, may hold values from -0.3125 to 0.3125
- eig_right: bfloat16 [384, 384], replicated, may hold values from -0.3125 to 0.3125
Outputs:
- new_buoy: bfloat16 [512, 512, 384], P('row', 'col')
- new_vel: bfloat16 [512, 512, 384], P('row', 'col')
All inputs are finite; a program needn't handle non-finite values.
Results may differ from a plain program's by a relative error of at most 0.019.
The roundings to bfloat16 on the way count: a program that leaves them out, or rounds other values in their place, can miss the bound.
Values may be sent and summed in bfloat16 or wider, within the bound.
No kernel may reach another device: no remote copies, remote signals or barrier semaphores. Data moves between devices by JAX's collectives and lax.ppermute only.
A program may use at most 192 MiB of HBM per device.

v0:
```python
import math

import jax
import jax.numpy as jnp
from jax import lax
from jax.sharding import PartitionSpec as P

KX = 512
KY = 512
NZ = 384
XG = 768
YG = 768
ZG = 576


explicit_step = 0.5
diffuse_buoy = 0.5
diffuse_vel = 0.25
couple_buoy = 0.7
couple_vel = 0.7


def fourier_trig(modes, points):
    order = jnp.arange(modes, dtype=jnp.int32)
    freq = ((order + 1) // 2).astype(jnp.float32)
    place = jnp.arange(points, dtype=jnp.float32)
    angle = 2.0 * math.pi / points * freq[:, None] * place[None, :]
    return (order, jnp.where((order % 2 == 0)[:, None], jnp.cos(angle), jnp.sin(angle)))


def fourier_eval(modes, points):
    order, values = fourier_trig(modes, points)
    return (values * math.sqrt(2.0 / modes)).astype(jnp.bfloat16)


def fourier_proj(modes, points):
    order, values = fourier_trig(modes, points)
    weight = jnp.where(order == 0, 1.0 / points, 2.0 / points).astype(jnp.float32)
    return jnp.transpose(values * weight[:, None] * math.sqrt(modes / 2.0)).astype(jnp.bfloat16)


def cheb_tables(degree, points):
    order = jnp.arange(degree, dtype=jnp.float32)
    theta = math.pi * (jnp.arange(points, dtype=jnp.float32) + 0.5) / points
    angle = order[:, None] * theta[None, :]
    norm = math.sqrt(2.0 / degree)
    levels = jnp.cos(angle) * norm
    slopes = -(order[:, None] / degree) * jnp.sin(angle) * norm
    weight = jnp.where(order == 0, 1.0 / points, 2.0 / points).astype(jnp.float32)
    projector = jnp.transpose(jnp.cos(angle) * weight[:, None] * math.sqrt(degree / 2.0))
    return (
        levels.astype(jnp.bfloat16),
        slopes.astype(jnp.bfloat16),
        projector.astype(jnp.bfloat16),
    )


def wave_squares(modes, offset, count):
    order = offset + jnp.arange(count, dtype=jnp.int32)
    freq = ((order + 1) // 2).astype(jnp.float32) * (2.0 / modes)
    return freq * freq


def lift_depth(coeffs, lookup, col_count):
    values = jnp.einsum("akn,nz->zak", coeffs, lookup, preferred_element_type=jnp.float32)
    return values.astype(jnp.bfloat16).reshape(col_count, values.shape[0] // col_count, -1)


def spread_rows(arrived, along_y, modes_x, modes_y, col_count, row_count):
    fields = arrived.shape[0]
    depth_part = arrived.shape[2]
    parts = arrived.reshape(fields, depth_part, col_count, modes_x, modes_y)
    result = jnp.einsum("fzcak,ckbi->fbaiz", parts, along_y, preferred_element_type=jnp.float32)
    return result.astype(jnp.bfloat16).reshape(fields, row_count, modes_x, -1)


def finish_grid(arrived, along_x):
    fields = arrived.shape[0]
    flat = arrived.reshape(fields, arrived.shape[2], arrived.shape[3])
    return jnp.einsum("fap,ax->fpx", flat, along_x, preferred_element_type=jnp.float32).astype(
        jnp.bfloat16
    )


def make_fluxes(vel_grid, slope_grid, strata_tiled):
    velocity = vel_grid.astype(jnp.float32)
    gradient = slope_grid.astype(jnp.float32)
    flux_buoy = -(velocity * gradient) - strata_tiled[:, None] * velocity
    flux_vel = -(velocity * jnp.abs(velocity))
    return jnp.stack([flux_buoy, flux_vel]).astype(jnp.bfloat16)


def fold_x(fluxes, back_x, row_count):
    values = jnp.einsum("fpx,xa->fap", fluxes, back_x, preferred_element_type=jnp.float32)
    fields, total_x, points = values.shape
    return values.astype(jnp.bfloat16).reshape(fields, row_count, total_x // row_count, points)


def fold_y(arrived, back_y, span_y, depth_part, col_count):
    fields, row_count, modes_x, points = arrived.shape
    parts = arrived.reshape(fields, row_count, modes_x, span_y, depth_part)
    values = jnp.einsum("fbaiz,bick->fczak", parts, back_y, preferred_element_type=jnp.float32)
    return values.astype(jnp.bfloat16).reshape(fields, col_count, depth_part, -1)


def fold_depth(arrived, projector, modes_x, modes_y):
    fields = arrived.shape[0]
    parts = arrived.reshape(fields, arrived.shape[1] * arrived.shape[2], modes_x, modes_y)
    return jnp.einsum("fzak,zn->fakn", parts, projector, preferred_element_type=jnp.float32)


def per_device(buoy, vel_w, strat, eig_val, eig_left, eig_right):
    row_count = lax.axis_size("row")
    col_count = lax.axis_size("col")
    modes_x, modes_y, degree = buoy.shape
    depth_part = ZG // col_count
    span_y = YG // row_count
    levels, slopes, projector = cheb_tables(NZ, ZG)
    along_y = fourier_eval(KY, YG).reshape(col_count, modes_y, row_count, span_y)
    along_x = fourier_eval(KX, XG)
    back_x = fourier_proj(KX, XG)
    back_y = fourier_proj(KY, YG).reshape(row_count, span_y, col_count, modes_y)
    strata_tiled = jnp.tile(strat, span_y)
    grid_list = []
    for coeffs, lookup in ((vel_w, levels), (buoy, slopes)):
        single = lift_depth(coeffs, lookup, col_count)[None]
        arrived = lax.all_to_all(single, "col", split_axis=1, concat_axis=3, tiled=True)
        spread = spread_rows(arrived, along_y, modes_x, modes_y, col_count, row_count)
        grid_list.append(
            finish_grid(
                lax.all_to_all(spread, "row", split_axis=1, concat_axis=2, tiled=True), along_x
            )[0]
        )
    fluxes = make_fluxes(grid_list[0], grid_list[1], strata_tiled)
    tend_list = []
    for member in range(2):
        folded = lax.all_to_all(
            fold_x(fluxes[member : member + 1], back_x, row_count),
            "row",
            split_axis=1,
            concat_axis=1,
            tiled=True,
        )
        returned = lax.all_to_all(
            fold_y(folded, back_y, span_y, depth_part, col_count),
            "col",
            split_axis=1,
            concat_axis=1,
            tiled=True,
        )
        tend_list.append(fold_depth(returned, projector, modes_x, modes_y)[0])
    tend_buoy = tend_list[0]
    tend_vel = tend_list[1]
    rhs_buoy = (buoy.astype(jnp.float32) + explicit_step * tend_buoy).astype(jnp.bfloat16)
    rhs_vel = (vel_w.astype(jnp.float32) + explicit_step * tend_vel).astype(jnp.bfloat16)
    modal_buoy = jnp.einsum("akn,nj->akj", rhs_buoy, eig_left, preferred_element_type=jnp.float32)
    modal_vel = jnp.einsum("akn,nj->akj", rhs_vel, eig_left, preferred_element_type=jnp.float32)
    wave_x = wave_squares(KX, lax.axis_index("row") * modes_x, modes_x)
    wave_y = wave_squares(KY, lax.axis_index("col") * modes_y, modes_y)
    lapl = 4.0 * (wave_x[:, None, None] + wave_y[None, :, None]) + eig_val[None, None, :]
    diag_buoy = 1.0 + diffuse_buoy * lapl
    diag_vel = 1.0 + diffuse_vel * lapl
    determ = diag_buoy * diag_vel + couple_buoy * couple_vel
    solved_buoy = ((diag_vel * modal_buoy - couple_buoy * modal_vel) / determ).astype(jnp.bfloat16)
    solved_vel = ((diag_buoy * modal_vel + couple_vel * modal_buoy) / determ).astype(jnp.bfloat16)
    new_buoy = jnp.einsum(
        "akj,jn->akn", solved_buoy, eig_right, preferred_element_type=jnp.float32
    ).astype(jnp.bfloat16)
    new_vel = jnp.einsum(
        "akj,jn->akn", solved_vel, eig_right, preferred_element_type=jnp.float32
    ).astype(jnp.bfloat16)
    return (new_buoy, new_vel)


def solution(mesh):
    in_specs = (P("row", "col", None), P("row", "col", None), P("col"), P(), P(), P())
    out_specs = (P("row", "col", None), P("row", "col", None))
    return jax.shard_map(
        per_device, mesh=mesh, in_specs=in_specs, out_specs=out_specs, check_vma=False
    )
```

profile of v0, /device:TPU:0, one launch (start us, length us, event | category | flops | bytes accessed | tf_op | source)
XLA Modules:
  0.0 1929.1 jit_solution(14926153851121471544)
XLA Ops:
  0.6 0.0 copy-start
  0.7 0.0 copy-start.1
  0.7 14.3 convolution_convert_fusion.3
  15.0 13.4 copy.36
  28.3 14.8 broadcast_in_dim_reshape.6
  43.1 6.0 all-to-all-start
  49.2 0.0 copy-done.1
  49.2 14.2 convolution_convert_fusion.2
  63.4 13.4 copy.41
  76.8 14.8 broadcast_in_dim_reshape.7
  91.6 62.7 %all-to-all-done = bf16[1,4,144,8192]{3,2,0,1:T(8,128)(2,1)} async-done(((bf16[1,4,144,8192]{3,2,0,1:T(8,128)(2,1)}), bf16[1,4,144,8192]{3,2,0,1:T(8,128)(2,1)}, u32[]{:S(2)}, u32[]{:S(2)}) %all-to-all-start) | async-done | bytes 9437216 | tf_op jit(solution)/shard_map/all_to_all | solution.py:127
  154.3 5.8 all-to-all-start.2
  160.1 0.0 copy-start.10
  160.1 0.0 copy-start.5
  160.1 0.0 copy-start.3
  160.2 10.4 copy.70
  170.6 103.5 %fusion.20 = bf16[1,8,64,96,144]{3,4,2,1,0:T(8,128)(2,1)} fusion(bf16[144,4,64,128]{3,2,0,1:T(8,128)(2,1)} %bitcast.179, f32[8,96]{1,0:T(8,128)S(1)} %multiply_add_fusion, f32[4,128]{1,0:T(4,128)S(1)} %fusion.122, pred[4,128]{1,0:T(4,128)(4,1)S(1)} %fusion.119), kind=kOutput, calls=%fused_computation.22 | convolution fusion | flops 7256408064 | bytes 23598592 | tf_op jit(solution)/shard_map/fzcak,ckbi->fbaiz/dot_general | solution.py:73
  274.1 29.0 %copy.39 = bf16[1,8,64,96,144]{4,3,2,1,0:T(8,128)(2,1)} copy(bf16[1,8,64,96,144]{3,4,2,1,0:T(8,128)(2,1)} %fusion.20) | data formatting | bytes 28311552 | tf_op jit(solution)/shard_map/convert_element_type | solution.py:74
  303.1 42.3 %reshape.304 = bf16[1,8,64,13824]{3,2,1,0:T(8,128)(2,1)} reshape(bf16[1,8,64,96,144]{4,3,2,1,0:T(8,128)(2,1)} %copy.39) | data formatting | bytes 28311552 | tf_op jit(solution)/shard_map/reshape | solution.py:74
  345.5 0.0 all-to-all-done.2
  345.5 5.5 all-to-all-start.1
  350.9 10.4 copy.71
  361.4 0.0 copy-done.10
  361.4 0.0 copy-done.5
  361.4 0.0 copy-done.3
  361.4 89.1 %fusion.21 = bf16[1,8,64,96,144]{3,4,2,1,0:T(8,128)(2,1)} fusion(bf16[144,4,64,128]{3,2,0,1:T(8,128)(2,1)} %bitcast.180, f32[8,96]{1,0:T(8,128)S(1)} %multiply_add_fusion, f32[4,128]{1,0:T(4,128)S(1)} %fusion.122, pred[4,128]{1,0:T(4,128)(4,1)S(1)} %fusion.119), kind=kOutput, calls=%fused_computation.23 | convolution fusion | flops 7256408064 | bytes 23598592 | tf_op jit(solution)/shard_map/fzcak,ckbi->fbaiz/dot_general | solution.py:73
  450.5 29.0 %copy.44 = bf16[1,8,64,96,144]{4,3,2,1,0:T(8,128)(2,1)} copy(bf16[1,8,64,96,144]{3,4,2,1,0:T(8,128)(2,1)} %fusion.21) | data formatting | bytes 28311552 | tf_op jit(solution)/shard_map/convert_element_type | solution.py:74
  479.5 42.3 %reshape.307 = bf16[1,8,64,13824]{3,2,1,0:T(8,128)(2,1)} reshape(bf16[1,8,64,96,144]{4,3,2,1,0:T(8,128)(2,1)} %copy.44) | data formatting | bytes 28311552 | tf_op jit(solution)/shard_map/reshape | solution.py:74
  521.9 136.6 %all-to-all-done.1 = bf16[1,8,64,13824]{3,2,0,1:T(8,128)(2,1)} async-done(((bf16[1,8,64,13824]{3,2,0,1:T(8,128)(2,1)}), bf16[1,8,64,13824]{3,2,0,1:T(8,128)(2,1)}, u32[]{:S(2)}, u32[]{:S(2)}) %all-to-all-start.1) | async-done | bytes 14155808 | tf_op jit(solution)/shard_map/all_to_all | solution.py:131
  658.4 5.5 all-to-all-start.3
  663.9 25.9 %convolution_convert_fusion.1 = bf16[13824,768]{1,0:T(8,128)(2,1)} fusion(bf16[512,13824]{1,0:T(8,128)(2,1)} %bitcast.14, f32[512]{0:T(512)S(1)} %get-tuple-element.2, pred[512]{0:T(512)(128)(4,1)S(1)} %fusion.123), kind=kOutput, calls=%fused_computation.16 | convolution fusion | flops 10883825664 | bytes 35392000 | tf_op jit(solution)/shard_map/fap,ax->fpx/dot_general | solution.py:80
  689.8 35.4 %fusion.17 = bf16[512,13824]{1,0:T(8,128)(2,1)} fusion(bf16[13824,768]{1,0:T(8,128)(2,1)} %convolution_convert_fusion.1, f32[512]{0:T(512)S(1)} %get-tuple-element.3, f32[512]{0:T(512)S(1)} %get-tuple-element.2, pred[512]{0:T(512)(128)(4,1)S(1)} %fusion.123), kind=kOutput, calls=%fused_computation.21 | convolution fusion | flops 10933764096 | bytes 35394048 | tf_op jit(solution)/shard_map/fpx,xa->fap/dot_general | solution.py:94
  725.2 246.2 %all-to-all-done.3 = bf16[1,8,64,13824]{3,2,0,1:T(8,128)(2,1)} async-done(((bf16[1,8,64,13824]{3,2,0,1:T(8,128)(2,1)}), bf16[1,8,64,13824]{3,2,0,1:T(8,128)(2,1)}, u32[]{:S(2)}, u32[]{:S(2)}) %all-to-all-start.3) | async-done | bytes 14155808 | tf_op jit(solution)/shard_map/all_to_all | solution.py:131
  971.4 5.6 all-to-all-start.6
  977.0 0.0 copy-done.7
  977.0 0.1 mul.391
  977.2 6.2 multiply_convert_fusion.16
  983.4 54.3 %fusion.14 = bf16[512,13824]{1,0:T(8,128)(2,1)} fusion(bf16[13824,768]{1,0:T(8,128)(2,1)} %convolution_convert_fusion.1, f32[13824]{0:T(1024)S(1)} %mul.391, bf16[512,13824]{1,0:T(8,128)(2,1)} %bitcast.26, f32[512]{0:T(512)S(1)} %get-tuple-element.2, pred[512]{0:T(512)(128)(4,1)S(1)} %fusion.123, bf16[768,512]{1,0:T(8,128)(2,1)S(1)} %multiply_convert_fusion.16), kind=kOutput, calls=%fused_computation.20 | convolution fusion | flops 21836857344 | bytes 50389504 | tf_op jit(solution)/shard_map/fpx,xa->fap/dot_general | solution.py:94
  1037.6 246.9 %all-to-all-done.6 = bf16[1,8,64,13824]{3,2,0,1:T(8,128)(2,1)} async-done(((bf16[1,8,64,13824]{3,2,0,1:T(8,128)(2,1)}), bf16[1,8,64,13824]{3,2,0,1:T(8,128)(2,1)}, u32[]{:S(2)}, u32[]{:S(2)}) %all-to-all-start.6) | async-done | bytes 14155808 | tf_op jit(solution)/shard_map/all_to_all | solution.py:137
  1284.5 5.7 all-to-all-start.4
  1290.2 0.0 copy-start.4
  1290.2 0.0 copy-start.6
  1290.2 0.0 copy-start.11
  1290.2 44.2 %reshape.314 = bf16[8,64,96,144]{3,2,1,0:T(8,128)(2,1)} reshape(bf16[1,8,64,13824]{3,2,0,1:T(8,128)(2,1)} %all-to-all-done.6) | data formatting | bytes 28311552 | tf_op jit(solution)/shard_map/reshape.47
  1334.4 0.0 copy-done.4
  1334.4 0.0 copy-done.6
  1334.5 0.0 copy-done.11
  1334.5 26.3 %fusion.35 = bf16[1,4,64,18,8,128]{5,4,3,2,1,0:T(8,128)(2,1)} fusion(bf16[8,64,96,144]{3,2,1,0:T(8,128)(2,1)} %reshape.314, f32[4,128]{1,0:T(4,128)S(1)} %fusion.137, f32[8,96]{1,0:T(8,128)S(1)} %copy-done.4, f32[4,128]{1,0:T(4,128)S(1)} %copy-done.6, pred[4,128]{1,0:T(4,128)(4,1)S(1)} %copy-done.11), kind=kOutput, calls=%fused_computation.43 | convolution fusion | flops 7254441984 | bytes 23600640 | tf_op jit(solution)/shard_map/fbaiz,bick->fczak/dot_general | solution.py:102
  1360.7 9.8 copy.96
  1370.5 227.1 %all-to-all-done.4 = bf16[1,8,64,13824]{3,2,0,1:T(8,128)(2,1)} async-done(((bf16[1,8,64,13824]{3,2,0,1:T(8,128)(2,1)}), bf16[1,8,64,13824]{3,2,0,1:T(8,128)(2,1)}, u32[]{:S(2)}, u32[]{:S(2)}) %all-to-all-start.4) | async-done | bytes 14155808 | tf_op jit(solution)/shard_map/all_to_all | solution.py:137
  1597.6 6.3 all-to-all-start.7
  1603.9 44.2 %reshape.310 = bf16[8,64,96,144]{3,2,1,0:T(8,128)(2,1)} reshape(bf16[1,8,64,13824]{3,2,0,1:T(8,128)(2,1)} %all-to-all-done.4) | data formatting | bytes 28311552 | tf_op jit(solution)/shard_map/reshape.39
  1648.2 26.3 %fusion.34 = bf16[1,4,64,18,8,128]{5,4,3,2,1,0:T(8,128)(2,1)} fusion(bf16[8,64,96,144]{3,2,1,0:T(8,128)(2,1)} %reshape.310, f32[4,128]{1,0:T(4,128)S(1)} %fusion.137, f32[8,96]{1,0:T(8,128)S(1)} %copy-done.4, f32[4,128]{1,0:T(4,128)S(1)} %copy-done.6, pred[4,128]{1,0:T(4,128)(4,1)S(1)} %copy-done.11), kind=kOutput, calls=%fused_computation.42 | convolution fusion | flops 7254441984 | bytes 23600640 | tf_op jit(solution)/shard_map/fbaiz,bick->fczak/dot_general | solution.py:102
  1674.4 10.0 copy.97
  1684.4 23.5 %all-to-all-done.7 = bf16[1,4,144,8192]{3,2,0,1:T(8,128)(2,1)} async-done(((bf16[1,4,144,8192]{3,2,0,1:T(8,128)(2,1)}), bf16[1,4,144,8192]{3,2,0,1:T(8,128)(2,1)}, u32[]{:S(2)}, u32[]{:S(2)}) %all-to-all-start.7) | async-done | bytes 9437216 | tf_op jit(solution)/shard_map/all_to_all | solution.py:144
  1707.9 6.0 all-to-all-start.5
  1713.9 0.1 add_multiply_fusion.2
  1714.0 10.4 copy.73
  1724.4 92.4 %all-to-all-done.5 = bf16[1,4,144,8192]{3,2,0,1:T(8,128)(2,1)} async-done(((bf16[1,4,144,8192]{3,2,0,1:T(8,128)(2,1)}), bf16[1,4,144,8192]{3,2,0,1:T(8,128)(2,1)}, u32[]{:S(2)}, u32[]{:S(2)}) %all-to-all-start.5) | async-done | bytes 9437216 | tf_op jit(solution)/shard_map/all_to_all | solution.py:144
  1816.8 10.4 copy.72
  1827.2 37.5 %fusion.49 = f32[64,128,384]{2,1,0:T(8,128)} fusion(bf16[64,128,384]{2,1,0:T(8,128)(2,1)} %param.7, bf16[576,64,128]{2,1,0:T(8,128)(2,1)} %bitcast.177, f32[384]{0:T(512)S(1)} %fusion.142, f32[576]{0:T(1024)S(1)} %copy-done.2, bf16[384,384]{1,0:T(8,128)(2,1)S(1)} %copy-done), kind=kOutput, calls=%fused_computation.57 | convolution fusion | flops 6053265408 | bytes 28610304 | tf_op jit(solution)/shard_map/akn,nj->akj/dot_general | solution.py:157
  1864.7 37.3 %fusion.48 = f32[64,128,384]{2,1,0:T(8,128)} fusion(bf16[64,128,384]{2,1,0:T(8,128)(2,1)} %param.6, bf16[576,64,128]{2,1,0:T(8,128)(2,1)} %bitcast.178, f32[384]{0:T(512)S(1)} %fusion.142, f32[576]{0:T(1024)S(1)} %copy-done.2, bf16[384,384]{1,0:T(8,128)(2,1)S(1)} %copy-done), kind=kOutput, calls=%fused_computation.56 | convolution fusion | flops 6053265408 | bytes 28610304 | tf_op jit(solution)/shard_map/akn,nj->akj/dot_general | solution.py:156
  1902.1 13.4 fusion.56
  1915.5 13.2 fusion.59
  (20 shorter events, 0.1 us)
Async XLA Ops:
  0.6 1826.6 %copy-start = (bf16[384,384]{1,0:T(8,128)(2,1)S(1)}, bf16[384,384]{1,0:T(8,128)(2,1)}, u32[]{:S(2)}) copy-start(bf16[384,384]{1,0:T(8,128)(2,1)} %param.10) | copy-start | bytes 884740
  0.7 48.5 %copy-start.1 = (f32[576]{0:T(1024)}, f32[576]{0:T(1024)S(1)}, u32[]{:S(2)}) copy-start(f32[576]{0:T(1024)S(1)} %add_multiply_fusion.3) | copy-start | bytes 6916
  43.1 111.2 %all-to-all-start = ((bf16[1,4,144,8192]{3,2,0,1:T(8,128)(2,1)}), bf16[1,4,144,8192]{3,2,0,1:T(8,128)(2,1)}, u32[]{:S(2)}, u32[]{:S(2)}) async-start(bf16[1,4,144,8192]{3,2,0,1:T(8,128)(2,1)} %bitcast.174), calls=%async_computation | async-start | bytes 18874368 | tf_op jit(solution)/shard_map/all_to_all | solution.py:127
  154.3 191.2 %all-to-all-start.2 = ((bf16[1,4,144,8192]{3,2,0,1:T(8,128)(2,1)}), bf16[1,4,144,8192]{3,2,0,1:T(8,128)(2,1)}, u32[]{:S(2)}, u32[]{:S(2)}) async-start(bf16[1,4,144,8192]{3,2,0,1:T(8,128)(2,1)} %bitcast.172), calls=%async_computation.2 | async-start | bytes 18874368 | tf_op jit(solution)/shard_map/all_to_all | solution.py:127
  160.1 201.3 %copy-start.10 = (pred[4,128]{1,0:T(4,128)(4,1)}, pred[4,128]{1,0:T(4,128)(4,1)S(1)}, u32[]{:S(2)}) copy-start(pred[4,128]{1,0:T(4,128)(4,1)S(1)} %fusion.119) | copy-start | bytes 1540
  160.1 201.3 %copy-start.5 = (f32[4,128]{1,0:T(4,128)}, f32[4,128]{1,0:T(4,128)S(1)}, u32[]{:S(2)}) copy-start(f32[4,128]{1,0:T(4,128)S(1)} %fusion.122) | copy-start | bytes 6148
  160.1 201.3 %copy-start.3 = (f32[8,96]{1,0:T(8,128)}, f32[8,96]{1,0:T(8,128)S(1)}, u32[]{:S(2)}) copy-start(f32[8,96]{1,0:T(8,128)S(1)} %multiply_add_fusion) | copy-start | bytes 9220
  345.5 313.0 %all-to-all-start.1 = ((bf16[1,8,64,13824]{3,2,0,1:T(8,128)(2,1)}), bf16[1,8,64,13824]{3,2,0,1:T(8,128)(2,1)}, u32[]{:S(2)}, u32[]{:S(2)}) async-start(bf16[1,8,64,13824]{3,2,0,1:T(8,128)(2,1)} %bitcast.169), calls=%async_computation.1 | async-start | bytes 28311552 | tf_op jit(solution)/shard_map/all_to_all | solution.py:131
  658.4 313.0 %all-to-all-start.3 = ((bf16[1,8,64,13824]{3,2,0,1:T(8,128)(2,1)}), bf16[1,8,64,13824]{3,2,0,1:T(8,128)(2,1)}, u32[]{:S(2)}, u32[]{:S(2)}) async-start(bf16[1,8,64,13824]{3,2,0,1:T(8,128)(2,1)} %bitcast.170), calls=%async_computation.3 | async-start | bytes 28311552 | tf_op jit(solution)/shard_map/all_to_all | solution.py:131
  971.4 5.6 copy-start.7
  971.4 313.1 %all-to-all-start.6 = ((bf16[1,8,64,13824]{3,2,0,1:T(8,128)(2,1)}), bf16[1,8,64,13824]{3,2,0,1:T(8,128)(2,1)}, u32[]{:S(2)}, u32[]{:S(2)}) async-start(bf16[1,8,64,13824]{3,2,0,1:T(8,128)(2,1)} %bitcast.176), calls=%async_computation.6 | async-start | bytes 28311552 | tf_op jit(solution)/shard_map/all_to_all | solution.py:137
  1284.5 313.2 %all-to-all-start.4 = ((bf16[1,8,64,13824]{3,2,0,1:T(8,128)(2,1)}), bf16[1,8,64,13824]{3,2,0,1:T(8,128)(2,1)}, u32[]{:S(2)}, u32[]{:S(2)}) async-start(bf16[1,8,64,13824]{3,2,0,1:T(8,128)(2,1)} %bitcast.175), calls=%async_computation.4 | async-start | bytes 28311552 | tf_op jit(solution)/shard_map/all_to_all | solution.py:137
  1290.2 44.3 %copy-start.4 = (f32[8,96]{1,0:T(8,128)S(1)}, f32[8,96]{1,0:T(8,128)}, u32[]{:S(2)}) copy-start(f32[8,96]{1,0:T(8,128)} %copy-done.3) | copy-start | bytes 9220
  1290.2 44.3 %copy-start.6 = (f32[4,128]{1,0:T(4,128)S(1)}, f32[4,128]{1,0:T(4,128)}, u32[]{:S(2)}) copy-start(f32[4,128]{1,0:T(4,128)} %copy-done.5) | copy-start | bytes 6148
  1290.2 44.2 %copy-start.11 = (pred[4,128]{1,0:T(4,128)(4,1)S(1)}, pred[4,128]{1,0:T(4,128)(4,1)}, u32[]{:S(2)}) copy-start(pred[4,128]{1,0:T(4,128)(4,1)} %copy-done.10) | copy-start | bytes 1540
  1597.6 110.2 %all-to-all-start.7 = ((bf16[1,4,144,8192]{3,2,0,1:T(8,128)(2,1)}), bf16[1,4,144,8192]{3,2,0,1:T(8,128)(2,1)}, u32[]{:S(2)}, u32[]{:S(2)}) async-start(bf16[1,4,144,8192]{3,2,0,1:T(8,128)(2,1)} %bitcast.173), calls=%async_computation.7 | async-start | bytes 18874368 | tf_op jit(solution)/shard_map/all_to_all | solution.py:144
  1707.9 109.0 %all-to-all-start.5 = ((bf16[1,4,144,8192]{3,2,0,1:T(8,128)(2,1)}), bf16[1,4,144,8192]{3,2,0,1:T(8,128)(2,1)}, u32[]{:S(2)}, u32[]{:S(2)}) async-start(bf16[1,4,144,8192]{3,2,0,1:T(8,128)(2,1)} %bitcast.171), calls=%async_computation.5 | async-start | bytes 18874368 | tf_op jit(solution)/shard_map/all_to_all | solution.py:144
  1816.8 10.4 copy-start.2
  1864.7 37.3 %copy-start.8 = (bf16[384,384]{1,0:T(8,128)(2,1)S(1)}, bf16[384,384]{1,0:T(8,128)(2,1)}, u32[]{:S(2)}) copy-start(bf16[384,384]{1,0:T(8,128)(2,1)} %param.11) | copy-start | bytes 884740
  1864.7 37.3 %copy-start.9 = (f32[384]{0:T(512)S(1)}, f32[384]{0:T(512)}, u32[]{:S(2)}) copy-start(f32[384]{0:T(512)} %param.9) | copy-start | bytes 4612
where the time goes:
time: 1940 us; the launch traced here: 1930 us
  waiting for transfers between devices  1040 us (54%)
  matrix products  491 us (25%)
  local copies, waits for them, and re-layouts  349 us (18%)
  starting transfers between devices  46.3 us (2%)
    all_to_all x2, waiting for transfers between devices, per_device(): lax.all_to_all(fold_x(fluxes[member:member + 1], back_x, row_count), 'row...  474 us
    all_to_all x2, waiting for transfers between devices, per_device(): lax.all_to_all(spread, 'row', split_axis=1, concat_axis=2, tiled=True)  383 us
    dot_general x2, matrix products, spread_rows(): jnp.einsum('fzcak,ckbi->fbaiz', parts, along_y, preferred_element_type=jn...  193 us
    all_to_all x2, waiting for transfers between devices, per_device(): lax.all_to_all(fold_y(folded, back_y, span_y, depth_part, col_count), 'co...  116 us
    dot_general x2, matrix products, fold_x(): jnp.einsum('fpx,xa->fap', fluxes, back_x, preferred_element_type=jnp.floa...  89.7 us
    another operation x2, local copies, waits for them, and re-layouts  88.5 us
    reshape x2, local copies, waits for them, and re-layouts, spread_rows(): return result.astype(jnp.bfloat16).reshape(fields, row_count, modes_x, -1)  84.7 us
    all_to_all x2, waiting for transfers between devices, per_device(): lax.all_to_all(single, 'col', split_axis=1, concat_axis=3, tiled=True)  62.7 us
  transfers between devices with their start and end apart: 8, of which 7 were waited for; matrix products, arithmetic and copies ran while one was open for 36% of the time, Pallas kernels for 0%

commit v1 on v0

v1 whole, which is shorter than its diff:
```python
import math

import jax
import jax.numpy as jnp
import numpy as np
from jax import lax
from jax.experimental import pallas as pl
from jax.experimental.pallas import tpu as pltpu
from jax.sharding import PartitionSpec as P

explicit_step = 0.5
diffuse_buoy = 0.5
diffuse_vel = 0.25
couple_buoy = 0.7
couple_vel = 0.7

CHUNKS = 4
BF16 = jnp.bfloat16
F32 = jnp.float32
VMEM_BYTES = 56 * 1024 * 1024


def fourier_trig(modes, points):
    order = np.arange(modes, dtype=np.int32)
    freq = ((order + 1) // 2).astype(np.float32)
    place = np.arange(points, dtype=np.float32)
    angle = np.float32(2.0 * math.pi / points) * freq[:, None] * place[None, :]
    return (order, np.where((order % 2 == 0)[:, None], np.cos(angle), np.sin(angle)))


def fourier_eval(modes, points):
    order, values = fourier_trig(modes, points)
    return (values * np.float32(math.sqrt(2.0 / modes))).astype(BF16)


def fourier_proj(modes, points):
    order, values = fourier_trig(modes, points)
    weight = np.where(order == 0, 1.0 / points, 2.0 / points).astype(np.float32)
    return np.transpose(values * weight[:, None] * np.float32(math.sqrt(modes / 2.0))).astype(BF16)


def cheb_tables(degree, points):
    order = np.arange(degree, dtype=np.float32)
    theta = np.float32(math.pi) * (np.arange(points, dtype=np.float32) + np.float32(0.5)) / np.float32(points)
    angle = order[:, None] * theta[None, :]
    norm = np.float32(math.sqrt(2.0 / degree))
    levels = np.cos(angle) * norm
    slopes = -(order[:, None] / np.float32(degree)) * np.sin(angle) * norm
    weight = np.where(order == 0, 1.0 / points, 2.0 / points).astype(np.float32)
    projector = np.transpose(np.cos(angle) * weight[:, None] * np.float32(math.sqrt(degree / 2.0)))
    return (levels.astype(BF16), slopes.astype(BF16), projector.astype(BF16))


def wave_squares(modes, offset, count):
    order = offset + jnp.arange(count, dtype=jnp.int32)
    freq = ((order + 1) // 2).astype(F32) * (2.0 / modes)
    return freq * freq


def largest_divisor(count, limit):
    return max(size for size in range(1, limit + 1) if count % size == 0)


def params(grid_rank):
    return pltpu.CompilerParams(
        dimension_semantics=("arbitrary",) * grid_rank, vmem_limit_bytes=VMEM_BYTES
    )


def whole(shape):
    return pl.BlockSpec(shape, lambda *_: (0,) * len(shape))


def lift_kernel(vel_ref, buoy_ref, table_ref, out_ref):
    blocks, fields, depth, span, lanes = out_ref.shape
    for field, source in enumerate((vel_ref, buoy_ref)):
        coeffs = source[...].reshape(span * lanes, source.shape[-1])
        values = lax.dot_general(
            table_ref[field], coeffs, (((1,), (1,)), ((), ())), preferred_element_type=F32
        )
        values = values.reshape(blocks * depth, span, lanes).astype(BF16)
        out_ref[:, field] = values.reshape(blocks, depth, span, lanes)


def lift(kernels, vel_w, buoy, table, blocks):
    modes_x, modes_y, degree = vel_w.shape
    depth = table.shape[1] // blocks
    shape = (blocks, 2, depth, modes_x, modes_y)
    if not kernels:
        fields = jnp.stack([vel_w, buoy])
        values = jnp.einsum("fzn,fakn->fzak", table, fields, preferred_element_type=F32)
        values = values.astype(BF16).reshape(2, blocks, depth, modes_x, modes_y)
        return jnp.transpose(values, (1, 0, 2, 3, 4))
    span = 16
    return pl.pallas_call(
        lift_kernel,
        grid=(modes_x // span,),
        in_specs=[
            pl.BlockSpec((span, modes_y, degree), lambda a: (a, 0, 0)),
            pl.BlockSpec((span, modes_y, degree), lambda a: (a, 0, 0)),
            whole(table.shape),
        ],
        out_specs=pl.BlockSpec((blocks, 2, depth, span, modes_y), lambda a: (0, 0, 0, a, 0)),
        out_shape=jax.ShapeDtypeStruct(shape, BF16),
        compiler_params=params(1),
        cost_estimate=pl.CostEstimate(
            flops=2 * math.prod(shape) * degree,
            bytes_accessed=2 * (2 * vel_w.size + math.prod(shape)),
            transcendentals=0,
        ),
        name="lift",
    )(vel_w, buoy, table)


def spread_kernel(in_ref, table_ref, *out_refs):
    blocks, _, depth, modes_x, lanes = in_ref.shape
    parts = [in_ref[:, 0, level].reshape(blocks * modes_x, lanes) for level in range(depth)]
    values = jnp.dot(
        table_ref[...], jnp.concatenate(parts, axis=1), preferred_element_type=F32
    ).astype(BF16)
    rows = out_refs[0].shape[2]
    for position, out_ref in enumerate(out_refs):
        for level in range(depth):
            out_ref[0, level] = values[
                position * rows : (position + 1) * rows, level * lanes : (level + 1) * lanes
            ]


def spread(kernels, arrived, table, col_count):
    blocks, fields, depth, modes_x, modes_y = arrived.shape
    rows = table.shape[0] // col_count
    if not kernels:
        values = jnp.einsum(
            "xpa,pfzak->fzxk",
            table.reshape(-1, blocks, modes_x),
            arrived,
            preferred_element_type=F32,
        ).astype(BF16)
        return [values[:, :, c * rows : (c + 1) * rows] for c in range(col_count)]
    step = largest_divisor(depth, 6)
    shape = (fields, depth, rows, modes_y)
    return pl.pallas_call(
        spread_kernel,
        grid=(fields, depth // step),
        in_specs=[
            pl.BlockSpec((blocks, 1, step, modes_x, modes_y), lambda f, z: (0, f, z, 0, 0)),
            whole(table.shape),
        ],
        out_specs=[pl.BlockSpec((1, step, rows, modes_y), lambda f, z: (f, z, 0, 0))] * col_count,
        out_shape=[jax.ShapeDtypeStruct(shape, BF16)] * col_count,
        compiler_params=params(2),
        cost_estimate=pl.CostEstimate(
            flops=2 * fields * depth * modes_y * table.size,
            bytes_accessed=2 * (arrived.size + col_count * math.prod(shape)),
            transcendentals=0,
        ),
        name="spread",
    )(arrived, table)


def flux_kernel(count, strat_ref, along_ref, back_ref, *refs):
    in_refs, out_refs = refs[:count], refs[count:]
    _, depth, rows, lanes = in_refs[0].shape
    grids = []
    for field in range(2):
        parts = [ref[field].reshape(depth * rows, lanes) for ref in in_refs]
        grids.append(
            jnp.dot(
                jnp.concatenate(parts, axis=1), along_ref[...], preferred_element_type=F32
            ).astype(BF16)
        )
    first = pl.program_id(0) * depth
    buoy_parts, vel_parts = [], []
    for level in range(depth):
        velocity = grids[0][level * rows : (level + 1) * rows].astype(F32)
        gradient = grids[1][level * rows : (level + 1) * rows].astype(F32)
        flux_buoy = -(velocity * gradient) - strat_ref[first + level] * velocity
        buoy_parts.append(flux_buoy.astype(BF16))
        vel_parts.append((-(velocity * jnp.abs(velocity))).astype(BF16))
    for field, parts in enumerate((buoy_parts, vel_parts)):
        values = jnp.dot(
            jnp.concatenate(parts, axis=0), back_ref[...], preferred_element_type=F32
        ).astype(BF16)
        for position, ref in enumerate(out_refs):
            ref[field] = values[:, position * lanes : (position + 1) * lanes].reshape(
                depth, rows, lanes
            )


def make_fluxes(kernels, arrived, strat, along_y, back_y):
    count = len(arrived)
    fields, depth, rows, lanes = arrived[0].shape
    if not kernels:
        values = jnp.concatenate(arrived, axis=-1)
        grids = jnp.einsum("fzxk,ky->fzxy", values, along_y, preferred_element_type=F32)
        grids = grids.astype(BF16).astype(F32)
        flux_buoy = -(grids[0] * grids[1]) - strat[:, None, None] * grids[0]
        flux_vel = -(grids[0] * jnp.abs(grids[0]))
        fluxes = jnp.stack([flux_buoy, flux_vel]).astype(BF16)
        values = jnp.einsum("fzxy,yk->fzxk", fluxes, back_y, preferred_element_type=F32)
        return jnp.split(values.astype(BF16), count, axis=-1)
    step = largest_divisor(depth, 3)
    block = pl.BlockSpec((fields, step, rows, lanes), lambda z: (0, z, 0, 0))
    return pl.pallas_call(
        lambda *refs: flux_kernel(count, *refs),
        grid=(depth // step,),
        in_specs=[pl.BlockSpec(memory_space=pltpu.SMEM), whole(along_y.shape), whole(back_y.shape)]
        + [block] * count,
        out_specs=[block] * count,
        out_shape=[jax.ShapeDtypeStruct(arrived[0].shape, BF16)] * count,
        compiler_params=params(1),
        cost_estimate=pl.CostEstimate(
            flops=4 * fields * depth * rows * along_y.size,
            bytes_accessed=4 * count * arrived[0].size,
            transcendentals=0,
        ),
        name="fluxes",
    )(strat, along_y, back_y, *arrived)


def fold_kernel(count, table_ref, *refs):
    in_refs, out_ref = refs[:count], refs[count]
    blocks, _, depth, modes_x, lanes = out_ref.shape
    parts = [
        jnp.concatenate([ref[0, level] for ref in in_refs], axis=0) for level in range(depth)
    ]
    values = jnp.dot(
        table_ref[...], jnp.concatenate(parts, axis=1), preferred_element_type=F32
    ).astype(BF16)
    for level in range(depth):
        out_ref[:, 0, level] = values[:, level * lanes : (level + 1) * lanes].reshape(
            blocks, modes_x, lanes
        )


def fold(kernels, arrived, table, blocks):
    count = len(arrived)
    fields, depth, rows, lanes = arrived[0].shape
    modes_x = table.shape[0] // blocks
    if not kernels:
        values = jnp.einsum(
            "pax,fzxk->pfzak",
            table.reshape(blocks, modes_x, -1),
            jnp.concatenate(arrived, axis=2),
            preferred_element_type=F32,
        )
        return values.astype(BF16)
    step = largest_divisor(depth, 6)
    shape = (blocks, fields, depth, modes_x, lanes)
    return pl.pallas_call(
        lambda *refs: fold_kernel(count, *refs),
        grid=(fields, depth // step),
        in_specs=[whole(table.shape)]
        + [pl.BlockSpec((1, step, rows, lanes), lambda f, z: (f, z, 0, 0))] * count,
        out_specs=pl.BlockSpec((blocks, 1, step, modes_x, lanes), lambda f, z: (0, f, z, 0, 0)),
        out_shape=jax.ShapeDtypeStruct(shape, BF16),
        compiler_params=params(2),
        cost_estimate=pl.CostEstimate(
            flops=2 * fields * depth * lanes * table.size,
            bytes_accessed=2 * (count * arrived[0].size + math.prod(shape)),
            transcendentals=0,
        ),
        name="fold",
    )(table, *arrived)


def solve_modal(modal_buoy, modal_vel, wave, eig_val):
    lapl = wave + eig_val
    diag_buoy = 1.0 + diffuse_buoy * lapl
    diag_vel = 1.0 + diffuse_vel * lapl
    scale = 1.0 / (diag_buoy * diag_vel + couple_buoy * couple_vel)
    solved_buoy = ((diag_vel * modal_buoy - couple_buoy * modal_vel) * scale).astype(BF16)
    solved_vel = ((diag_buoy * modal_vel + couple_vel * modal_buoy) * scale).astype(BF16)
    return (solved_buoy, solved_vel)


def finish_kernel(
    wave_x_ref, wave_y_ref, eig_val_ref, left_ref, right_ref, proj_ref, buoy_ref, vel_ref, *refs
):
    in_refs, out_refs = refs[:-2], refs[-2:]
    span, lanes, degree = buoy_ref.shape
    modal = []
    for field, coeff_ref in enumerate((buoy_ref, vel_ref)):
        parts = []
        for ref in in_refs:
            part = ref[:, field]
            parts.append(part.reshape(part.shape[0] * part.shape[1], span, lanes))
        fluxes = jnp.concatenate(parts, axis=0).astype(F32)
        fluxes = jnp.swapaxes(fluxes, 0, 1).astype(BF16)
        rows = []
        for mode in range(span):
            tend = lax.dot_general(
                fluxes[mode], proj_ref[...], (((0,), (0,)), ((), ())), preferred_element_type=F32
            )
            rows.append((coeff_ref[mode].astype(F32) + explicit_step * tend).astype(BF16))
        modal.append(
            jnp.dot(jnp.concatenate(rows, axis=0), left_ref[...], preferred_element_type=F32)
        )
    first = pl.program_id(0) * span
    waves = [4.0 * (wave_x_ref[first + mode] + wave_y_ref[...]) for mode in range(span)]
    solved = solve_modal(modal[0], modal[1], jnp.concatenate(waves, axis=0), eig_val_ref[...])
    for values, out_ref in zip(solved, out_refs):
        result = jnp.dot(values, right_ref[...], preferred_element_type=F32).astype(BF16)
        out_ref[...] = result.reshape(span, lanes, degree)


def finish(kernels, folded, buoy, vel_w, projs, eig_val, eig_left, eig_right, wave_x, wave_y):
    modes_x, modes_y, degree = buoy.shape
    if not kernels:
        tend = 0.0
        for part, proj in zip(folded, projs):
            parts = jnp.transpose(part, (1, 0, 2, 3, 4)).reshape(2, -1, modes_x, modes_y)
            tend += jnp.einsum("fzak,zn->fakn", parts, proj, preferred_element_type=F32)
        modal = []
        for field, coeffs in enumerate((buoy, vel_w)):
            rhs = (coeffs.astype(F32) + explicit_step * tend[field]).astype(BF16)
            modal.append(jnp.einsum("akn,nj->akj", rhs, eig_left, preferred_element_type=F32))
        wave = 4.0 * (wave_x[:, None, None] + wave_y[None, :, None])
        solved = solve_modal(modal[0], modal[1], wave, eig_val)
        return tuple(
            jnp.einsum("akj,jn->akn", values, eig_right, preferred_element_type=F32).astype(BF16)
            for values in solved
        )
    span = 8
    proj = jnp.concatenate(projs, axis=0)
    field_block = pl.BlockSpec((span, modes_y, degree), lambda a: (a, 0, 0))
    result = jax.ShapeDtypeStruct(buoy.shape, BF16)
    return pl.pallas_call(
        finish_kernel,
        grid=(modes_x // span,),
        in_specs=[
            pl.BlockSpec(memory_space=pltpu.SMEM),
            whole((modes_y, 1)),
            whole((1, degree)),
            whole(eig_left.shape),
            whole(eig_right.shape),
            whole(proj.shape),
            field_block,
            field_block,
        ]
        + [
            pl.BlockSpec(
                (part.shape[0], 2, part.shape[2], span, modes_y), lambda a: (0, 0, 0, a, 0)
            )
            for part in folded
        ],
        out_specs=[field_block, field_block],
        out_shape=[result, result],
        compiler_params=params(1),
        cost_estimate=pl.CostEstimate(
            flops=4 * buoy.size * (proj.shape[0] + 2 * degree),
            bytes_accessed=8 * buoy.size + sum(2 * part.size for part in folded),
            transcendentals=buoy.size,
        ),
        name="finish",
    )(
        wave_x,
        wave_y[:, None],
        eig_val[None, :],
        eig_left,
        eig_right,
        proj,
        buoy,
        vel_w,
        *folded,
    )


def per_device(buoy, vel_w, strat, eig_val, eig_left, eig_right):
    row_count = lax.axis_size("row")
    col_count = lax.axis_size("col")
    modes_x, modes_y, degree = buoy.shape
    total_x, total_y = modes_x * row_count, modes_y * col_count
    grid_x, grid_y = 3 * total_x // 2, 3 * total_y // 2
    grid_z = strat.shape[0] * col_count
    own = grid_z // row_count
    rows_x = grid_x // col_count
    kernels = modes_y % 128 == 0 and modes_x % 16 == 0 and rows_x % 16 == 0 and degree % 128 == 0
    paired = col_count & (col_count - 1) == 0

    def partner(device, shift, sign):
        return device ^ shift if paired else (device + sign * shift) % col_count

    row = lax.axis_index("row")
    col = lax.axis_index("col")
    shifts = np.arange(col_count)
    sends = [[partner(c, s, 1) for s in shifts] for c in range(col_count)]
    receives = [[partner(c, s, -1) for s in shifts] for c in range(col_count)]
    send_order = jnp.asarray(np.array(sends, np.int32))[col]
    receive_order = jnp.asarray(np.array(receives, np.int32))[col]

    def exchange_col(blocks):
        arrived = [blocks[0]]
        for shift in range(1, col_count):
            pairs = [(c, int(partner(c, shift, 1))) for c in range(col_count)]
            arrived.append(lax.ppermute(blocks[shift], "col", pairs))
        return arrived

    def exchange_row(values):
        return lax.all_to_all(values, "row", split_axis=0, concat_axis=0, tiled=True)

    levels, slopes, projector = cheb_tables(degree, grid_z)
    forward_z = np.stack([levels.T, slopes.T]).reshape(2, row_count, own, degree)
    backward_z = projector.reshape(row_count, own, degree)
    along_x = jnp.asarray(fourier_eval(total_x, grid_x).T.reshape(col_count, rows_x, total_x))
    along_x = along_x[send_order].reshape(grid_x, total_x)
    back_x = jnp.asarray(fourier_proj(total_x, grid_x).T.reshape(total_x, col_count, rows_x))
    back_x = back_x[:, receive_order].reshape(total_x, grid_x)
    along_y = jnp.asarray(fourier_eval(total_y, grid_y).reshape(col_count, modes_y, grid_y))
    along_y = along_y[receive_order].reshape(total_y, grid_y)
    back_y = jnp.asarray(fourier_proj(total_y, grid_y).reshape(grid_y, col_count, modes_y))
    back_y = back_y[:, send_order].reshape(grid_y, total_y)
    strat_all = lax.all_gather(strat, "col", axis=0, tiled=True)
    strat_own = lax.dynamic_slice_in_dim(strat_all, row * own, own)

    depth = own // CHUNKS if own % CHUNKS == 0 else own
    starts = list(range(0, own, depth))
    folded, projs = [], []
    for start in starts:
        table = jnp.asarray(
            forward_z[:, :, start : start + depth].reshape(2, row_count * depth, degree)
        )
        projs.append(
            jnp.asarray(backward_z[:, start : start + depth].reshape(row_count * depth, degree))
        )
        lifted = exchange_row(lift(kernels, vel_w, buoy, table, row_count))
        arrived = exchange_col(spread(kernels, lifted, along_x, col_count))
        fluxes = make_fluxes(
            kernels, arrived, strat_own[start : start + depth], along_y, back_y
        )
        returned = exchange_col(fluxes)
        folded.append(exchange_row(fold(kernels, returned, back_x, row_count)))
    wave_x = wave_squares(total_x, row * modes_x, modes_x)
    wave_y = wave_squares(total_y, col * modes_y, modes_y)
    return finish(
        kernels, folded, buoy, vel_w, projs, eig_val, eig_left, eig_right, wave_x, wave_y
    )


def solution(mesh):
    in_specs = (P("row", "col", None), P("row", "col", None), P("col"), P(), P(), P())
    out_specs = (P("row", "col", None), P("row", "col", None))
    return jax.shard_map(
        per_device, mesh=mesh, in_specs=in_specs, out_specs=out_specs, check_vma=False
    )
```

time: 1940 us -> 1300 us (0.67)
  matrix products: 491 us -> 0 us
  local copies, waits for them, and re-layouts: 349 us -> 18.6 us
  Pallas kernels: 0 us -> 213 us
  waiting for transfers between devices: 1040 us -> 918 us
  blocking collectives: 0 us -> 76 us
  starting transfers between devices: 46.3 us -> 67.5 us
    all_to_all x8, waiting for transfers between devices: 1040 us -> 391 us  [exchange_row(): lax.all_to_all(values, 'row', split_axis=0, concat_axis=0, tiled=True)]
    ppermute x0 -> x24, waiting for transfers between devices: none -> 527 us  [exchange_col(): arrived.append(lax.ppermute(blocks[shift], 'col', pairs))]
    dot_general x13 -> x0, matrix products: 491 us -> none  [the longest x2 193 us: spread_rows(): jnp.einsum('fzcak,ckbi->fbaiz', parts, along_y, preferred_element_type=jn...]
    pallas_call x0 -> x17, Pallas kernels: none -> 213 us  [the longest x4 61.1 us: make_fluxes(): pl.pallas_call(lambda *refs: flux_kernel(count, *refs), grid=(depth // st...]
    another operation x5 -> x0, local copies, waits for them, and re-layouts: 118 us -> none
    reshape x4 -> x2, local copies, waits for them, and re-layouts: 104 us -> 2.16 us  [the longest x1 1.17 us: per_device(): back_x = back_x[:, receive_order].reshape(total_x, grid_x)]
    convert_element_type x4 -> x0, local copies, waits for them, and re-layouts: 84.8 us -> none  [the longest x2 58.1 us: spread_rows(): return result.astype(jnp.bfloat16).reshape(fields, row_count, modes_x, -1)]
    unnamed x0 -> x1, blocking collectives: none -> 76 us
  transfers between devices with their start and end apart: 8 -> 32, of which waited for: 7 -> 19; matrix products, arithmetic and copies ran while one was open for 36% -> 1% of each run, Pallas kernels for 0% -> 12%
where the time goes in v1:
time: 1300 us
  waiting for transfers between devices  918 us (71%)
  Pallas kernels  213 us (16%)
  blocking collectives  76 us (6%)
  starting transfers between devices  67.5 us (5%)
  local copies, waits for them, and re-layouts  18.6 us (1%)
    ppermute x24, waiting for transfers between devices, exchange_col(): arrived.append(lax.ppermute(blocks[shift], 'col', pairs))  527 us
    all_to_all x8, waiting for transfers between devices, exchange_row(): lax.all_to_all(values, 'row', split_axis=0, concat_axis=0, tiled=True)  391 us
    unnamed x1, blocking collectives  76 us
    pallas_call x4, Pallas kernels, make_fluxes(): pl.pallas_call(lambda *refs: flux_kernel(count, *refs), grid=(depth // st...  61.1 us
    pallas_call x1, Pallas kernels, finish(): pl.pallas_call(finish_kernel, grid=(modes_x // span,), in_specs=[pl.Block...  44.2 us
    all_to_all x8, starting transfers between devices, exchange_row(): lax.all_to_all(values, 'row', split_axis=0, concat_axis=0, tiled=True)  39 us
    pallas_call x4, Pallas kernels, lift(): pl.pallas_call(lift_kernel, grid=(modes_x // span,), in_specs=[pl.BlockSp...  37.5 us
    pallas_call x4, Pallas kernels, fold(): pl.pallas_call(lambda *refs: fold_kernel(count, *refs), grid=(fields, dep...  35.9 us
  transfers between devices with their start and end apart: 32, of which 19 were waited for; matrix products, arithmetic and copies ran while one was open for 1% of the time, Pallas kernels for 12%

profile of v1, /device:TPU:0, one launch (start us, length us, event | category | flops | bytes accessed | tf_op | source)
XLA Modules:
  0.0 1296.1 jit_solution(2648904742442361737)
XLA Ops:
  0.6 9.4 lift.4
  10.0 6.3 all-to-all-start
  16.3 9.4 lift.5
  25.7 96.0 %all-to-all-done.in_ref = bf16[8,2,18,64,128]{4,3,2,1,0:T(8,128)(2,1)} async-done(((bf16[8,2,18,64,128]{4,3,2,1,0:T(8,128)(2,1)}), bf16[8,2,18,64,128]{4,3,2,1,0:T(8,128)(2,1)}, u32[]{:S(2)}, u32[]{:S(2)}) %all-to-all-start) | async-done | bytes 4718624 | tf_op jit(solution)/shard_map/all_to_all | solution.py:400
  121.7 4.6 all-to-all-start.2
  126.3 9.4 lift.6
  135.7 95.9 %all-to-all-done.2.in_ref = bf16[8,2,18,64,128]{4,3,2,1,0:T(8,128)(2,1)} async-done(((bf16[8,2,18,64,128]{4,3,2,1,0:T(8,128)(2,1)}), bf16[8,2,18,64,128]{4,3,2,1,0:T(8,128)(2,1)}, u32[]{:S(2)}, u32[]{:S(2)}) %all-to-all-start.2) | async-done | bytes 4718624 | tf_op jit(solution)/shard_map/all_to_all | solution.py:400
  231.5 4.6 all-to-all-start.4
  236.2 9.4 lift.7
  245.5 95.9 %all-to-all-done.4.in_ref = bf16[8,2,18,64,128]{4,3,2,1,0:T(8,128)(2,1)} async-done(((bf16[8,2,18,64,128]{4,3,2,1,0:T(8,128)(2,1)}), bf16[8,2,18,64,128]{4,3,2,1,0:T(8,128)(2,1)}, u32[]{:S(2)}, u32[]{:S(2)}) %all-to-all-start.4) | async-done | bytes 4718624 | tf_op jit(solution)/shard_map/all_to_all | solution.py:400
  341.4 4.6 all-to-all-start.6
  346.8 1.6 gather_fusion.3
  348.3 8.6 spread.4
  356.9 1.6 collective-permute-start
  358.5 1.5 collective-permute-start.1
  361.2 1.5 gather_fusion.1
  364.2 76.0 %all-reduce = f32[576]{0:T(1024)S(1)} all-reduce(f32[576]{0:T(1024)S(1)} %dynamic-update-slice), channel_id=1, replica_groups=mesh['row'=8,'col'=4] {'col'}, use_global_device_ids=true, to_apply=%add | all-reduce | flops 576 | bytes 4608
  442.0 15.3 %fluxes.4 = (bf16[2,18,192,128]{3,2,1,0:T(8,128)(2,1)}, bf16[2,18,192,128]{3,2,1,0:T(8,128)(2,1)}, bf16[2,18,192,128]{3,2,1,0:T(8,128)(2,1)}, bf16[2,18,192,128]{3,2,1,0:T(8,128)(2,1)}) custom-call(f32[18]{0:T(128)} %get-tuple-element.69.refs_0_, bf16[512,768]{1,0:T(8,128)(2,1)} %bitcast.21, bf16[768,512]{1,0:T(8,128)(2,1)} %copy_bitcast_fusion.refs_2_, ...), custom_call_target="tpu_custom_call" | custom-call | flops 10871635968 | bytes 14155776 | tf_op jit(solution)/shard_map/fluxes/pallas_call | solution.py:204
  458.9 2.0 collective-permute-start.5
  461.5 1.2 copy.31.refs_0_
  462.6 36.6 %collective-permute-done.3.refs_2_ = bf16[2,18,192,128]{3,2,1,0:T(8,128)(2,1)} collective-permute-done((bf16[2,18,192,128]{3,2,1,0:T(8,128)(2,1)}, bf16[2,18,192,128]{3,2,1,0:T(8,128)(2,1)}, u32[]{:S(2)}, u32[]{:S(2)}) %collective-permute-start.3) | collective-permute-done | bytes 1769504 | tf_op jit(solution)/shard_map/ppermute | solution.py:396
  499.2 36.9 %collective-permute-done.5.refs_4_ = bf16[2,18,192,128]{3,2,1,0:T(8,128)(2,1)} collective-permute-done((bf16[2,18,192,128]{3,2,1,0:T(8,128)(2,1)}, bf16[2,18,192,128]{3,2,1,0:T(8,128)(2,1)}, u32[]{:S(2)}, u32[]{:S(2)}) %collective-permute-start.5) | collective-permute-done | bytes 1769504 | tf_op jit(solution)/shard_map/ppermute | solution.py:396
  536.1 9.0 fold.4
  545.1 4.8 all-to-all-start.1
  549.9 8.5 spread.5
  559.3 1.5 collective-permute-start.7
  561.9 38.2 %collective-permute-done.6.refs_4_ = bf16[2,18,192,128]{3,2,1,0:T(8,128)(2,1)S(1)} collective-permute-done((bf16[2,18,192,128]{3,2,1,0:T(8,128)(2,1)}, bf16[2,18,192,128]{3,2,1,0:T(8,128)(2,1)S(1)}, u32[]{:S(2)}, u32[]{:S(2)}) %collective-permute-start.6) | collective-permute-done | bytes 1769504 | tf_op jit(solution)/shard_map/ppermute | solution.py:396
  600.1 37.8 %collective-permute-done.7.refs_5_ = bf16[2,18,192,128]{3,2,1,0:T(8,128)(2,1)S(1)} collective-permute-done((bf16[2,18,192,128]{3,2,1,0:T(8,128)(2,1)}, bf16[2,18,192,128]{3,2,1,0:T(8,128)(2,1)S(1)}, u32[]{:S(2)}, u32[]{:S(2)}) %collective-permute-start.7) | collective-permute-done | bytes 1769504 | tf_op jit(solution)/shard_map/ppermute | solution.py:396
  637.9 1.2 copy-done.10
  639.8 15.3 %fluxes.5 = (bf16[2,18,192,128]{3,2,1,0:T(8,128)(2,1)}, bf16[2,18,192,128]{3,2,1,0:T(8,128)(2,1)}, bf16[2,18,192,128]{3,2,1,0:T(8,128)(2,1)}, bf16[2,18,192,128]{3,2,1,0:T(8,128)(2,1)}) custom-call(f32[18]{0:T(128)} %get-tuple-element.68.refs_0_, bf16[512,768]{1,0:T(8,128)(2,1)} %bitcast.22, bf16[768,512]{1,0:T(8,128)(2,1)} %copy_bitcast_fusion.refs_2_, ...), custom_call_target="tpu_custom_call" | custom-call | flops 10871635968 | bytes 14155776 | tf_op jit(solution)/shard_map/fluxes/pallas_call | solution.py:204
  656.6 1.9 collective-permute-start.11
  658.6 38.3 %collective-permute-done.9.refs_2_ = bf16[2,18,192,128]{3,2,1,0:T(8,128)(2,1)S(1)} collective-permute-done((bf16[2,18,192,128]{3,2,1,0:T(8,128)(2,1)}, bf16[2,18,192,128]{3,2,1,0:T(8,128)(2,1)S(1)}, u32[]{:S(2)}, u32[]{:S(2)}) %collective-permute-start.9) | collective-permute-done | bytes 1769504 | tf_op jit(solution)/shard_map/ppermute | solution.py:396
  696.8 36.7 %collective-permute-done.10.refs_3_ = bf16[2,18,192,128]{3,2,1,0:T(8,128)(2,1)S(1)} collective-permute-done((bf16[2,18,192,128]{3,2,1,0:T(8,128)(2,1)}, bf16[2,18,192,128]{3,2,1,0:T(8,128)(2,1)S(1)}, u32[]{:S(2)}, u32[]{:S(2)}) %collective-permute-start.10) | collective-permute-done | bytes 1769504 | tf_op jit(solution)/shard_map/ppermute | solution.py:396
  733.6 1.2 copy-done.19
  735.4 9.0 fold.5
  744.4 4.6 all-to-all-start.3
  749.0 8.5 spread.6
  758.6 2.3 collective-permute-start.14
  761.0 38.1 %collective-permute-done.12.refs_4_ = bf16[2,18,192,128]{3,2,1,0:T(8,128)(2,1)S(1)} collective-permute-done((bf16[2,18,192,128]{3,2,1,0:T(8,128)(2,1)}, bf16[2,18,192,128]{3,2,1,0:T(8,128)(2,1)S(1)}, u32[]{:S(2)}, u32[]{:S(2)}) %collective-permute-start.12) | collective-permute-done | bytes 1769504 | tf_op jit(solution)/shard_map/ppermute | solution.py:396
  799.1 37.5 %collective-permute-done.14.refs_6_ = bf16[2,18,192,128]{3,2,1,0:T(8,128)(2,1)S(1)} collective-permute-done((bf16[2,18,192,128]{3,2,1,0:T(8,128)(2,1)}, bf16[2,18,192,128]{3,2,1,0:T(8,128)(2,1)S(1)}, u32[]{:S(2)}, u32[]{:S(2)}) %collective-permute-start.14) | collective-permute-done | bytes 1769504 | tf_op jit(solution)/shard_map/ppermute | solution.py:396
  836.6 1.3 copy-done.17
  837.9 15.3 %fluxes.6 = (bf16[2,18,192,128]{3,2,1,0:T(8,128)(2,1)}, bf16[2,18,192,128]{3,2,1,0:T(8,128)(2,1)}, bf16[2,18,192,128]{3,2,1,0:T(8,128)(2,1)}, bf16[2,18,192,128]{3,2,1,0:T(8,128)(2,1)}) custom-call(f32[18]{0:T(128)} %get-tuple-element.67.refs_0_, bf16[512,768]{1,0:T(8,128)(2,1)} %bitcast.23, bf16[768,512]{1,0:T(8,128)(2,1)} %copy_bitcast_fusion.refs_2_, ...), custom_call_target="tpu_custom_call" | custom-call | flops 10871635968 | bytes 14155776 | tf_op jit(solution)/shard_map/fluxes/pallas_call | solution.py:204
  853.2 2.3 collective-permute-start.15
  857.0 38.2 %collective-permute-done.15.refs_2_ = bf16[2,18,192,128]{3,2,1,0:T(8,128)(2,1)S(1)} collective-permute-done((bf16[2,18,192,128]{3,2,1,0:T(8,128)(2,1)}, bf16[2,18,192,128]{3,2,1,0:T(8,128)(2,1)S(1)}, u32[]{:S(2)}, u32[]{:S(2)}) %collective-permute-start.15) | collective-permute-done | bytes 1769504 | tf_op jit(solution)/shard_map/ppermute | solution.py:396
  895.2 38.0 %collective-permute-done.16.refs_3_ = bf16[2,18,192,128]{3,2,1,0:T(8,128)(2,1)S(1)} collective-permute-done((bf16[2,18,192,128]{3,2,1,0:T(8,128)(2,1)}, bf16[2,18,192,128]{3,2,1,0:T(8,128)(2,1)S(1)}, u32[]{:S(2)}, u32[]{:S(2)}) %collective-permute-start.16) | collective-permute-done | bytes 1769504 | tf_op jit(solution)/shard_map/ppermute | solution.py:396
  933.2 1.3 copy-done.20
  935.0 9.0 fold.6
  943.9 4.6 all-to-all-start.5
  948.5 8.5 spread.7
  958.3 2.3 collective-permute-start.20
  960.6 38.1 %collective-permute-done.18.refs_4_ = bf16[2,18,192,128]{3,2,1,0:T(8,128)(2,1)S(1)} collective-permute-done((bf16[2,18,192,128]{3,2,1,0:T(8,128)(2,1)}, bf16[2,18,192,128]{3,2,1,0:T(8,128)(2,1)S(1)}, u32[]{:S(2)}, u32[]{:S(2)}) %collective-permute-start.18) | collective-permute-done | bytes 1769504 | tf_op jit(solution)/shard_map/ppermute | solution.py:396
  998.7 37.4 %collective-permute-done.19.refs_5_ = bf16[2,18,192,128]{3,2,1,0:T(8,128)(2,1)S(1)} collective-permute-done((bf16[2,18,192,128]{3,2,1,0:T(8,128)(2,1)}, bf16[2,18,192,128]{3,2,1,0:T(8,128)(2,1)S(1)}, u32[]{:S(2)}, u32[]{:S(2)}) %collective-permute-start.19) | collective-permute-done | bytes 1769504 | tf_op jit(solution)/shard_map/ppermute | solution.py:396
  1036.2 1.3 copy-done.9
  1038.0 15.3 %fluxes.7 = (bf16[2,18,192,128]{3,2,1,0:T(8,128)(2,1)}, bf16[2,18,192,128]{3,2,1,0:T(8,128)(2,1)}, bf16[2,18,192,128]{3,2,1,0:T(8,128)(2,1)}, bf16[2,18,192,128]{3,2,1,0:T(8,128)(2,1)}) custom-call(f32[18]{0:T(128)} %get-tuple-element.66.refs_0_, bf16[512,768]{1,0:T(8,128)(2,1)} %bitcast.24, bf16[768,512]{1,0:T(8,128)(2,1)} %copy_bitcast_fusion.refs_2_, ...), custom_call_target="tpu_custom_call" | custom-call | flops 10871635968 | bytes 14155776 | tf_op jit(solution)/shard_map/fluxes/pallas_call | solution.py:204
  1053.2 1.7 collective-permute-start.21
  1055.2 1.5 collective-permute-start.23
  1056.8 38.3 %collective-permute-done.21.refs_2_ = bf16[2,18,192,128]{3,2,1,0:T(8,128)(2,1)S(1)} collective-permute-done((bf16[2,18,192,128]{3,2,1,0:T(8,128)(2,1)}, bf16[2,18,192,128]{3,2,1,0:T(8,128)(2,1)S(1)}, u32[]{:S(2)}, u32[]{:S(2)}) %collective-permute-start.21) | collective-permute-done | bytes 1769504 | tf_op jit(solution)/shard_map/ppermute | solution.py:396
  1095.0 35.1 %collective-permute-done.22.refs_3_ = bf16[2,18,192,128]{3,2,1,0:T(8,128)(2,1)S(1)} collective-permute-done((bf16[2,18,192,128]{3,2,1,0:T(8,128)(2,1)}, bf16[2,18,192,128]{3,2,1,0:T(8,128)(2,1)S(1)}, u32[]{:S(2)}, u32[]{:S(2)}) %collective-permute-start.22) | collective-permute-done | bytes 1769504 | tf_op jit(solution)/shard_map/ppermute | solution.py:396
  1130.1 1.7 collective-permute-done.23.refs_4_
  1131.8 1.2 copy-done.21
  1133.0 9.0 fold.7
  1142.0 4.9 all-to-all-start.7
  1148.8 103.1 %all-to-all-done.7.refs_3_ = bf16[8,2,18,64,128]{4,3,2,1,0:T(8,128)(2,1)} async-done(((bf16[8,2,18,64,128]{4,3,2,1,0:T(8,128)(2,1)}), bf16[8,2,18,64,128]{4,3,2,1,0:T(8,128)(2,1)}, u32[]{:S(2)}, u32[]{:S(2)}) %all-to-all-start.7) | async-done | bytes 4718624 | tf_op jit(solution)/shard_map/all_to_all | solution.py:400
  1251.8 44.2 %finish.1 = (bf16[64,128,384]{2,1,0:T(8,128)(2,1)}, bf16[64,128,384]{2,1,0:T(8,128)(2,1)}) custom-call(f32[64]{0:T(128)} %multiply_multiply_fusion.wave_x_ref, f32[128,1]{1,0:T(8,128)} %mul.48.wave_y_ref, f32[1,384]{1,0:T(1,128)} %broadcast_in_dim.2.eig_val_ref, bf16[384,384]{1,0:T(8,128)(2,1)} %left_ref.1, bf16[384,384]{1,0:T(8,128)(2,1)} %right_ref.1, ...), custom_call_target="tpu_custom_call" | custom-call | flops 16911433728 | bytes 44040192 | tf_op jit(solution)/shard_map/finish/pallas_call | solution.py:328
  (86 shorter events, 18.8 us)
Async XLA Ops:
  10.0 111.7 %all-to-all-start = ((bf16[8,2,18,64,128]{4,3,2,1,0:T(8,128)(2,1)}), bf16[8,2,18,64,128]{4,3,2,1,0:T(8,128)(2,1)}, u32[]{:S(2)}, u32[]{:S(2)}) async-start(bf16[8,2,18,64,128]{4,3,2,1,0:T(8,128)(2,1)} %lift.4), calls=%async_computation | async-start | bytes 9437184 | tf_op jit(solution)/shard_map/all_to_all | solution.py:400
  121.7 109.9 %all-to-all-start.2 = ((bf16[8,2,18,64,128]{4,3,2,1,0:T(8,128)(2,1)}), bf16[8,2,18,64,128]{4,3,2,1,0:T(8,128)(2,1)}, u32[]{:S(2)}, u32[]{:S(2)}) async-start(bf16[8,2,18,64,128]{4,3,2,1,0:T(8,128)(2,1)} %lift.5), calls=%async_computation.2 | async-start | bytes 9437184 | tf_op jit(solution)/shard_map/all_to_all | solution.py:400
  231.5 109.9 %all-to-all-start.4 = ((bf16[8,2,18,64,128]{4,3,2,1,0:T(8,128)(2,1)}), bf16[8,2,18,64,128]{4,3,2,1,0:T(8,128)(2,1)}, u32[]{:S(2)}, u32[]{:S(2)}) async-start(bf16[8,2,18,64,128]{4,3,2,1,0:T(8,128)(2,1)} %lift.6), calls=%async_computation.4 | async-start | bytes 9437184 | tf_op jit(solution)/shard_map/all_to_all | solution.py:400
  245.5 101.2 %copy-start.3 = (bf16[4,192,512]{2,1,0:T(8,128)(2,1)S(1)}, bf16[4,192,512]{2,1,0:T(8,128)(2,1)}, u32[]{:S(2)}) copy-start(bf16[4,192,512]{2,1,0:T(8,128)(2,1)} %constant.77.clone) | copy-start | bytes 2359300
  341.4 203.7 %all-to-all-start.6 = ((bf16[8,2,18,64,128]{4,3,2,1,0:T(8,128)(2,1)}), bf16[8,2,18,64,128]{4,3,2,1,0:T(8,128)(2,1)}, u32[]{:S(2)}, u32[]{:S(2)}) async-start(bf16[8,2,18,64,128]{4,3,2,1,0:T(8,128)(2,1)} %lift.7), calls=%async_computation.6 | async-start | bytes 9437184 | tf_op jit(solution)/shard_map/all_to_all | solution.py:400
  348.3 12.1 copy-start.2
  356.9 4.3 copy-start.1
  356.9 5.8 copy-start.24
  356.9 7.1 copy-start.5
  356.9 85.1 %collective-permute-start = (bf16[2,18,192,128]{3,2,1,0:T(8,128)(2,1)}, bf16[2,18,192,128]{3,2,1,0:T(8,128)(2,1)}, u32[]{:S(2)}, u32[]{:S(2)}) collective-permute-start(bf16[2,18,192,128]{3,2,1,0:T(8,128)(2,1)} %get-tuple-element.35), channel_id=1, source_target_pairs={{0,1},{1,0},{2,3},{3,2},{4,5},{5,4},{6,7},{7,6},{8,9},{9,8},{10,11... | collective-permute-start | bytes 5308424 | tf_op jit(solution)/shard_map/ppermute | solution.py:396
  358.5 83.5 %collective-permute-start.1 = (bf16[2,18,192,128]{3,2,1,0:T(8,128)(2,1)}, bf16[2,18,192,128]{3,2,1,0:T(8,128)(2,1)}, u32[]{:S(2)}, u32[]{:S(2)}) collective-permute-start(bf16[2,18,192,128]{3,2,1,0:T(8,128)(2,1)} %get-tuple-element.36), channel_id=1, source_target_pairs={{0,2},{1,3},{2,0},{3,1},{4,6},{5,7},{6,4},{7,5},{8,10},{9,11},{10,... | collective-permute-start | bytes 5308424 | tf_op jit(solution)/shard_map/ppermute | solution.py:396
  360.0 82.0 %collective-permute-start.2 = (bf16[2,18,192,128]{3,2,1,0:T(8,128)(2,1)}, bf16[2,18,192,128]{3,2,1,0:T(8,128)(2,1)}, u32[]{:S(2)}, u32[]{:S(2)}) collective-permute-start(bf16[2,18,192,128]{3,2,1,0:T(8,128)(2,1)} %get-tuple-element.37), channel_id=1, source_target_pairs={{0,3},{1,2},{2,1},{3,0},{4,7},{5,6},{6,5},{7,4},{8,11},{9,10},{10,... | collective-permute-start | bytes 5308424 | tf_op jit(solution)/shard_map/ppermute | solution.py:396
  442.0 18.9 %copy-start = (bf16[512,4,192]{0,2,1:T(8,128)(2,1)S(1)}, bf16[512,4,192]{0,2,1:T(8,128)(2,1)}, u32[]{:S(2)}) copy-start(bf16[512,4,192]{0,2,1:T(8,128)(2,1)} %constant.78.clone) | copy-start | bytes 2359300
  457.3 41.9 %collective-permute-start.3 = (bf16[2,18,192,128]{3,2,1,0:T(8,128)(2,1)}, bf16[2,18,192,128]{3,2,1,0:T(8,128)(2,1)}, u32[]{:S(2)}, u32[]{:S(2)}) collective-permute-start(bf16[2,18,192,128]{3,2,1,0:T(8,128)(2,1)} %get-tuple-element.39), channel_id=1, source_target_pairs={{0,1},{1,0},{2,3},{3,2},{4,5},{5,4},{6,7},{7,6},{8,9},{9,8},{10,11... | collective-permute-start | bytes 5308424 | tf_op jit(solution)/shard_map/ppermute | solution.py:396
  457.9 41.3 %collective-permute-start.4 = (bf16[2,18,192,128]{3,2,1,0:T(8,128)(2,1)}, bf16[2,18,192,128]{3,2,1,0:T(8,128)(2,1)}, u32[]{:S(2)}, u32[]{:S(2)}) collective-permute-start(bf16[2,18,192,128]{3,2,1,0:T(8,128)(2,1)} %get-tuple-element.40), channel_id=1, source_target_pairs={{0,2},{1,3},{2,0},{3,1},{4,6},{5,7},{6,4},{7,5},{8,10},{9,11},{10,... | collective-permute-start | bytes 5308424 | tf_op jit(solution)/shard_map/ppermute | solution.py:396
  458.9 77.3 %collective-permute-start.5 = (bf16[2,18,192,128]{3,2,1,0:T(8,128)(2,1)}, bf16[2,18,192,128]{3,2,1,0:T(8,128)(2,1)}, u32[]{:S(2)}, u32[]{:S(2)}) collective-permute-start(bf16[2,18,192,128]{3,2,1,0:T(8,128)(2,1)} %get-tuple-element.41), channel_id=1, source_target_pairs={{0,3},{1,2},{2,1},{3,0},{4,7},{5,6},{6,5},{7,4},{8,11},{9,10},{10,... | collective-permute-start | bytes 5308424 | tf_op jit(solution)/shard_map/ppermute | solution.py:396
  545.1 199.3 %all-to-all-start.1 = ((bf16[8,2,18,64,128]{4,3,2,1,0:T(8,128)(2,1)}), bf16[8,2,18,64,128]{4,3,2,1,0:T(8,128)(2,1)}, u32[]{:S(2)}, u32[]{:S(2)}) async-start(bf16[8,2,18,64,128]{4,3,2,1,0:T(8,128)(2,1)} %fold.4), calls=%async_computation.1 | async-start | bytes 9437184 | tf_op jit(solution)/shard_map/all_to_all | solution.py:400
  558.4 41.6 %collective-permute-start.6 = (bf16[2,18,192,128]{3,2,1,0:T(8,128)(2,1)}, bf16[2,18,192,128]{3,2,1,0:T(8,128)(2,1)S(1)}, u32[]{:S(2)}, u32[]{:S(2)}) collective-permute-start(bf16[2,18,192,128]{3,2,1,0:T(8,128)(2,1)} %get-tuple-element.43), channel_id=1, source_target_pairs={{0,1},{1,0},{2,3},{3,2},{4,5},{5,4},{6,7},{7,6},{8,9},{9,8},{10,11... | collective-permute-start | bytes 5308424 | tf_op jit(solution)/shard_map/ppermute | solution.py:396
  559.3 78.6 %collective-permute-start.7 = (bf16[2,18,192,128]{3,2,1,0:T(8,128)(2,1)}, bf16[2,18,192,128]{3,2,1,0:T(8,128)(2,1)S(1)}, u32[]{:S(2)}, u32[]{:S(2)}) collective-permute-start(bf16[2,18,192,128]{3,2,1,0:T(8,128)(2,1)} %get-tuple-element.44), channel_id=1, source_target_pairs={{0,2},{1,3},{2,0},{3,1},{4,6},{5,7},{6,4},{7,5},{8,10},{9,11},{10,... | collective-permute-start | bytes 5308424 | tf_op jit(solution)/shard_map/ppermute | solution.py:396
  560.7 77.2 %collective-permute-start.8 = (bf16[2,18,192,128]{3,2,1,0:T(8,128)(2,1)}, bf16[2,18,192,128]{3,2,1,0:T(8,128)(2,1)S(1)}, u32[]{:S(2)}, u32[]{:S(2)}) collective-permute-start(bf16[2,18,192,128]{3,2,1,0:T(8,128)(2,1)} %get-tuple-element.45), channel_id=1, source_target_pairs={{0,3},{1,2},{2,1},{3,0},{4,7},{5,6},{6,5},{7,4},{8,11},{9,10},{10,... | collective-permute-start | bytes 5308424 | tf_op jit(solution)/shard_map/ppermute | solution.py:396
  600.1 37.9 %copy-start.7 = (bf16[2,18,192,128]{3,2,1,0:T(8,128)(2,1)}, bf16[2,18,192,128]{3,2,1,0:T(8,128)(2,1)S(1)}, u32[]{:S(2)}) copy-start(bf16[2,18,192,128]{3,2,1,0:T(8,128)(2,1)S(1)} %collective-permute-done.6.refs_4_) | copy-start | bytes 5308420
  637.9 1.2 copy-start.10
  637.9 1.9 copy-start.16
  655.0 41.8 %collective-permute-start.9 = (bf16[2,18,192,128]{3,2,1,0:T(8,128)(2,1)}, bf16[2,18,192,128]{3,2,1,0:T(8,128)(2,1)S(1)}, u32[]{:S(2)}, u32[]{:S(2)}) collective-permute-start(bf16[2,18,192,128]{3,2,1,0:T(8,128)(2,1)} %get-tuple-element.47), channel_id=1, source_target_pairs={{0,1},{1,0},{2,3},{3,2},{4,5},{5,4},{6,7},{7,6},{8,9},{9,8},{10,11... | collective-permute-start | bytes 5308424 | tf_op jit(solution)/shard_map/ppermute | solution.py:396
  655.7 77.8 %collective-permute-start.10 = (bf16[2,18,192,128]{3,2,1,0:T(8,128)(2,1)}, bf16[2,18,192,128]{3,2,1,0:T(8,128)(2,1)S(1)}, u32[]{:S(2)}, u32[]{:S(2)}) collective-permute-start(bf16[2,18,192,128]{3,2,1,0:T(8,128)(2,1)} %get-tuple-element.48), channel_id=1, source_target_pairs={{0,2},{1,3},{2,0},{3,1},{4,6},{5,7},{6,4},{7,5},{8,10},{9,11},{10,... | collective-permute-start | bytes 5308424 | tf_op jit(solution)/shard_map/ppermute | solution.py:396
  656.6 76.9 %collective-permute-start.11 = (bf16[2,18,192,128]{3,2,1,0:T(8,128)(2,1)}, bf16[2,18,192,128]{3,2,1,0:T(8,128)(2,1)S(1)}, u32[]{:S(2)}, u32[]{:S(2)}) collective-permute-start(bf16[2,18,192,128]{3,2,1,0:T(8,128)(2,1)} %get-tuple-element.49), channel_id=1, source_target_pairs={{0,3},{1,2},{2,1},{3,0},{4,7},{5,6},{6,5},{7,4},{8,11},{9,10},{10,... | collective-permute-start | bytes 5308424 | tf_op jit(solution)/shard_map/ppermute | solution.py:396
  696.8 36.7 %copy-start.14 = (bf16[2,18,192,128]{3,2,1,0:T(8,128)(2,1)}, bf16[2,18,192,128]{3,2,1,0:T(8,128)(2,1)S(1)}, u32[]{:S(2)}) copy-start(bf16[2,18,192,128]{3,2,1,0:T(8,128)(2,1)S(1)} %collective-permute-done.9.refs_2_) | copy-start | bytes 5308420
  733.5 1.2 copy-start.19
  733.6 1.8 copy-start.22
  744.4 199.6 %all-to-all-start.3 = ((bf16[8,2,18,64,128]{4,3,2,1,0:T(8,128)(2,1)}), bf16[8,2,18,64,128]{4,3,2,1,0:T(8,128)(2,1)}, u32[]{:S(2)}, u32[]{:S(2)}) async-start(bf16[8,2,18,64,128]{4,3,2,1,0:T(8,128)(2,1)} %fold.5), calls=%async_computation.3 | async-start | bytes 9437184 | tf_op jit(solution)/shard_map/all_to_all | solution.py:400
  757.5 41.6 %collective-permute-start.12 = (bf16[2,18,192,128]{3,2,1,0:T(8,128)(2,1)}, bf16[2,18,192,128]{3,2,1,0:T(8,128)(2,1)S(1)}, u32[]{:S(2)}, u32[]{:S(2)}) collective-permute-start(bf16[2,18,192,128]{3,2,1,0:T(8,128)(2,1)} %get-tuple-element.51), channel_id=1, source_target_pairs={{0,1},{1,0},{2,3},{3,2},{4,5},{5,4},{6,7},{7,6},{8,9},{9,8},{10,11... | collective-permute-start | bytes 5308424 | tf_op jit(solution)/shard_map/ppermute | solution.py:396
  757.9 41.2 %collective-permute-start.13 = (bf16[2,18,192,128]{3,2,1,0:T(8,128)(2,1)}, bf16[2,18,192,128]{3,2,1,0:T(8,128)(2,1)S(1)}, u32[]{:S(2)}, u32[]{:S(2)}) collective-permute-start(bf16[2,18,192,128]{3,2,1,0:T(8,128)(2,1)} %get-tuple-element.52), channel_id=1, source_target_pairs={{0,2},{1,3},{2,0},{3,1},{4,6},{5,7},{6,4},{7,5},{8,10},{9,11},{10,... | collective-permute-start | bytes 5308424 | tf_op jit(solution)/shard_map/ppermute | solution.py:396
  758.6 78.0 %collective-permute-start.14 = (bf16[2,18,192,128]{3,2,1,0:T(8,128)(2,1)}, bf16[2,18,192,128]{3,2,1,0:T(8,128)(2,1)S(1)}, u32[]{:S(2)}, u32[]{:S(2)}) collective-permute-start(bf16[2,18,192,128]{3,2,1,0:T(8,128)(2,1)} %get-tuple-element.53), channel_id=1, source_target_pairs={{0,3},{1,2},{2,1},{3,0},{4,7},{5,6},{6,5},{7,4},{8,11},{9,10},{10,... | collective-permute-start | bytes 5308424 | tf_op jit(solution)/shard_map/ppermute | solution.py:396
  799.1 37.5 %copy-start.8 = (bf16[2,18,192,128]{3,2,1,0:T(8,128)(2,1)}, bf16[2,18,192,128]{3,2,1,0:T(8,128)(2,1)S(1)}, u32[]{:S(2)}) copy-start(bf16[2,18,192,128]{3,2,1,0:T(8,128)(2,1)S(1)} %collective-permute-done.12.refs_4_) | copy-start | bytes 5308420
  799.1 37.5 %copy-start.11 = (bf16[2,18,192,128]{3,2,1,0:T(8,128)(2,1)}, bf16[2,18,192,128]{3,2,1,0:T(8,128)(2,1)S(1)}, u32[]{:S(2)}) copy-start(bf16[2,18,192,128]{3,2,1,0:T(8,128)(2,1)S(1)} %collective-permute-done.13.refs_5_) | copy-start | bytes 5308420
  836.6 1.3 copy-start.17
  853.2 42.0 %collective-permute-start.15 = (bf16[2,18,192,128]{3,2,1,0:T(8,128)(2,1)}, bf16[2,18,192,128]{3,2,1,0:T(8,128)(2,1)S(1)}, u32[]{:S(2)}, u32[]{:S(2)}) collective-permute-start(bf16[2,18,192,128]{3,2,1,0:T(8,128)(2,1)} %get-tuple-element.55), channel_id=1, source_target_pairs={{0,1},{1,0},{2,3},{3,2},{4,5},{5,4},{6,7},{7,6},{8,9},{9,8},{10,11... | collective-permute-start | bytes 5308424 | tf_op jit(solution)/shard_map/ppermute | solution.py:396
  855.5 77.7 %collective-permute-start.16 = (bf16[2,18,192,128]{3,2,1,0:T(8,128)(2,1)}, bf16[2,18,192,128]{3,2,1,0:T(8,128)(2,1)S(1)}, u32[]{:S(2)}, u32[]{:S(2)}) collective-permute-start(bf16[2,18,192,128]{3,2,1,0:T(8,128)(2,1)} %get-tuple-element.56), channel_id=1, source_target_pairs={{0,2},{1,3},{2,0},{3,1},{4,6},{5,7},{6,4},{7,5},{8,10},{9,11},{10,... | collective-permute-start | bytes 5308424 | tf_op jit(solution)/shard_map/ppermute | solution.py:396
  856.0 77.2 %collective-permute-start.17 = (bf16[2,18,192,128]{3,2,1,0:T(8,128)(2,1)}, bf16[2,18,192,128]{3,2,1,0:T(8,128)(2,1)S(1)}, u32[]{:S(2)}, u32[]{:S(2)}) collective-permute-start(bf16[2,18,192,128]{3,2,1,0:T(8,128)(2,1)} %get-tuple-element.57), channel_id=1, source_target_pairs={{0,3},{1,2},{2,1},{3,0},{4,7},{5,6},{6,5},{7,4},{8,11},{9,10},{10,... | collective-permute-start | bytes 5308424 | tf_op jit(solution)/shard_map/ppermute | solution.py:396
  895.2 38.0 %copy-start.15 = (bf16[2,18,192,128]{3,2,1,0:T(8,128)(2,1)}, bf16[2,18,192,128]{3,2,1,0:T(8,128)(2,1)S(1)}, u32[]{:S(2)}) copy-start(bf16[2,18,192,128]{3,2,1,0:T(8,128)(2,1)S(1)} %collective-permute-done.15.refs_2_) | copy-start | bytes 5308420
  933.2 1.3 copy-start.20
  933.2 1.8 copy-start.23
  943.9 198.0 %all-to-all-start.5 = ((bf16[8,2,18,64,128]{4,3,2,1,0:T(8,128)(2,1)}), bf16[8,2,18,64,128]{4,3,2,1,0:T(8,128)(2,1)}, u32[]{:S(2)}, u32[]{:S(2)}) async-start(bf16[8,2,18,64,128]{4,3,2,1,0:T(8,128)(2,1)} %fold.6), calls=%async_computation.5 | async-start | bytes 9437184 | tf_op jit(solution)/shard_map/all_to_all | solution.py:400
  957.1 41.6 %collective-permute-start.18 = (bf16[2,18,192,128]{3,2,1,0:T(8,128)(2,1)}, bf16[2,18,192,128]{3,2,1,0:T(8,128)(2,1)S(1)}, u32[]{:S(2)}, u32[]{:S(2)}) collective-permute-start(bf16[2,18,192,128]{3,2,1,0:T(8,128)(2,1)} %get-tuple-element.59), channel_id=1, source_target_pairs={{0,1},{1,0},{2,3},{3,2},{4,5},{5,4},{6,7},{7,6},{8,9},{9,8},{10,11... | collective-permute-start | bytes 5308424 | tf_op jit(solution)/shard_map/ppermute | solution.py:396
  957.4 78.7 %collective-permute-start.19 = (bf16[2,18,192,128]{3,2,1,0:T(8,128)(2,1)}, bf16[2,18,192,128]{3,2,1,0:T(8,128)(2,1)S(1)}, u32[]{:S(2)}, u32[]{:S(2)}) collective-permute-start(bf16[2,18,192,128]{3,2,1,0:T(8,128)(2,1)} %get-tuple-element.60), channel_id=1, source_target_pairs={{0,2},{1,3},{2,0},{3,1},{4,6},{5,7},{6,4},{7,5},{8,10},{9,11},{10,... | collective-permute-start | bytes 5308424 | tf_op jit(solution)/shard_map/ppermute | solution.py:396
  958.3 77.8 %collective-permute-start.20 = (bf16[2,18,192,128]{3,2,1,0:T(8,128)(2,1)}, bf16[2,18,192,128]{3,2,1,0:T(8,128)(2,1)S(1)}, u32[]{:S(2)}, u32[]{:S(2)}) collective-permute-start(bf16[2,18,192,128]{3,2,1,0:T(8,128)(2,1)} %get-tuple-element.61), channel_id=1, source_target_pairs={{0,3},{1,2},{2,1},{3,0},{4,7},{5,6},{6,5},{7,4},{8,11},{9,10},{10,... | collective-permute-start | bytes 5308424 | tf_op jit(solution)/shard_map/ppermute | solution.py:396
  998.7 37.5 %copy-start.6 = (bf16[2,18,192,128]{3,2,1,0:T(8,128)(2,1)}, bf16[2,18,192,128]{3,2,1,0:T(8,128)(2,1)S(1)}, u32[]{:S(2)}) copy-start(bf16[2,18,192,128]{3,2,1,0:T(8,128)(2,1)S(1)} %collective-permute-done.18.refs_4_) | copy-start | bytes 5308420
  1036.1 1.3 copy-start.9
  1036.2 1.8 copy-start.12
  1053.2 41.8 %collective-permute-start.21 = (bf16[2,18,192,128]{3,2,1,0:T(8,128)(2,1)}, bf16[2,18,192,128]{3,2,1,0:T(8,128)(2,1)S(1)}, u32[]{:S(2)}, u32[]{:S(2)}) collective-permute-start(bf16[2,18,192,128]{3,2,1,0:T(8,128)(2,1)} %get-tuple-element.63), channel_id=1, source_target_pairs={{0,1},{1,0},{2,3},{3,2},{4,5},{5,4},{6,7},{7,6},{8,9},{9,8},{10,11... | collective-permute-start | bytes 5308424 | tf_op jit(solution)/shard_map/ppermute | solution.py:396
  1054.9 75.1 %collective-permute-start.22 = (bf16[2,18,192,128]{3,2,1,0:T(8,128)(2,1)}, bf16[2,18,192,128]{3,2,1,0:T(8,128)(2,1)S(1)}, u32[]{:S(2)}, u32[]{:S(2)}) collective-permute-start(bf16[2,18,192,128]{3,2,1,0:T(8,128)(2,1)} %get-tuple-element.64), channel_id=1, source_target_pairs={{0,2},{1,3},{2,0},{3,1},{4,6},{5,7},{6,4},{7,5},{8,10},{9,11},{10,... | collective-permute-start | bytes 5308424 | tf_op jit(solution)/shard_map/ppermute | solution.py:396
  1055.2 76.5 %collective-permute-start.23 = (bf16[2,18,192,128]{3,2,1,0:T(8,128)(2,1)}, bf16[2,18,192,128]{3,2,1,0:T(8,128)(2,1)S(1)}, u32[]{:S(2)}, u32[]{:S(2)}) collective-permute-start(bf16[2,18,192,128]{3,2,1,0:T(8,128)(2,1)} %get-tuple-element.65), channel_id=1, source_target_pairs={{0,3},{1,2},{2,1},{3,0},{4,7},{5,6},{6,5},{7,4},{8,11},{9,10},{10,... | collective-permute-start | bytes 5308424 | tf_op jit(solution)/shard_map/ppermute | solution.py:396
  1095.0 36.7 %copy-start.13 = (bf16[2,18,192,128]{3,2,1,0:T(8,128)(2,1)}, bf16[2,18,192,128]{3,2,1,0:T(8,128)(2,1)S(1)}, u32[]{:S(2)}) copy-start(bf16[2,18,192,128]{3,2,1,0:T(8,128)(2,1)S(1)} %collective-permute-done.21.refs_2_) | copy-start | bytes 5308420
  1130.1 1.7 copy-start.18
  1131.8 1.2 copy-start.21
  1141.9 4.9 copy-start.4
  1142.0 109.9 %all-to-all-start.7 = ((bf16[8,2,18,64,128]{4,3,2,1,0:T(8,128)(2,1)}), bf16[8,2,18,64,128]{4,3,2,1,0:T(8,128)(2,1)}, u32[]{:S(2)}, u32[]{:S(2)}) async-start(bf16[8,2,18,64,128]{4,3,2,1,0:T(8,128)(2,1)} %fold.7), calls=%async_computation.7 | async-start | bytes 9437184 | tf_op jit(solution)/shard_map/all_to_all | solution.py:400

commit v2 on v1

v2 whole, which is shorter than its diff:
```python
import math

import jax
import jax.numpy as jnp
import numpy as np
from jax import lax
from jax.experimental import pallas as pl
from jax.experimental.pallas import tpu as pltpu
from jax.sharding import PartitionSpec as P

explicit_step = 0.5
diffuse_buoy = 0.5
diffuse_vel = 0.25
couple_buoy = 0.7
couple_vel = 0.7

BF16 = jnp.bfloat16
F32 = jnp.float32
VMEM_BYTES = 56 * 1024 * 1024


def fourier_trig(modes, points):
    order = np.arange(modes, dtype=np.int32)
    freq = ((order + 1) // 2).astype(np.float32)
    place = np.arange(points, dtype=np.float32)
    angle = np.float32(2.0 * math.pi / points) * freq[:, None] * place[None, :]
    return (order, np.where((order % 2 == 0)[:, None], np.cos(angle), np.sin(angle)))


def fourier_eval(modes, points):
    order, values = fourier_trig(modes, points)
    return (values * np.float32(math.sqrt(2.0 / modes))).astype(BF16)


def fourier_proj(modes, points):
    order, values = fourier_trig(modes, points)
    weight = np.where(order == 0, 1.0 / points, 2.0 / points).astype(np.float32)
    return np.transpose(values * weight[:, None] * np.float32(math.sqrt(modes / 2.0))).astype(BF16)


def cheb_tables(degree, points):
    order = np.arange(degree, dtype=np.float32)
    theta = np.float32(math.pi) * (np.arange(points, dtype=np.float32) + np.float32(0.5)) / np.float32(points)
    angle = order[:, None] * theta[None, :]
    norm = np.float32(math.sqrt(2.0 / degree))
    levels = np.cos(angle) * norm
    slopes = -(order[:, None] / np.float32(degree)) * np.sin(angle) * norm
    weight = np.where(order == 0, 1.0 / points, 2.0 / points).astype(np.float32)
    projector = np.transpose(np.cos(angle) * weight[:, None] * np.float32(math.sqrt(degree / 2.0)))
    return (levels.astype(BF16), slopes.astype(BF16), projector.astype(BF16))


def wave_squares(modes, offset, count):
    order = offset + jnp.arange(count, dtype=jnp.int32)
    freq = ((order + 1) // 2).astype(F32) * (2.0 / modes)
    return freq * freq


def params(grid_rank):
    return pltpu.CompilerParams(
        dimension_semantics=("arbitrary",) * grid_rank, vmem_limit_bytes=VMEM_BYTES
    )


def whole(shape):
    return pl.BlockSpec(shape, lambda *_: (0,) * len(shape))


def lift_kernel(vel_ref, buoy_ref, table_ref, out_ref):
    blocks, fields, depth, span, lanes = out_ref.shape
    for field, source in enumerate((vel_ref, buoy_ref)):
        coeffs = source[...].reshape(span * lanes, source.shape[-1])
        values = lax.dot_general(
            table_ref[field], coeffs, (((1,), (1,)), ((), ())), preferred_element_type=F32
        )
        values = values.reshape(blocks * depth, span, lanes).astype(BF16)
        out_ref[:, field] = values.reshape(blocks, depth, span, lanes)


def lift(kernels, vel_w, buoy, table, blocks):
    modes_x, modes_y, degree = vel_w.shape
    depth = table.shape[1] // blocks
    shape = (blocks, 2, depth, modes_x, modes_y)
    if not kernels:
        fields = jnp.stack([vel_w, buoy])
        values = jnp.einsum("fzn,fakn->fzak", table, fields, preferred_element_type=F32)
        values = values.astype(BF16).reshape(2, blocks, depth, modes_x, modes_y)
        return jnp.transpose(values, (1, 0, 2, 3, 4))
    span = 16
    return pl.pallas_call(
        lift_kernel,
        grid=(modes_x // span,),
        in_specs=[
            pl.BlockSpec((span, modes_y, degree), lambda a: (a, 0, 0)),
            pl.BlockSpec((span, modes_y, degree), lambda a: (a, 0, 0)),
            whole(table.shape),
        ],
        out_specs=pl.BlockSpec((blocks, 2, depth, span, modes_y), lambda a: (0, 0, 0, a, 0)),
        out_shape=jax.ShapeDtypeStruct(shape, BF16),
        compiler_params=params(1),
        cost_estimate=pl.CostEstimate(
            flops=2 * math.prod(shape) * degree,
            bytes_accessed=2 * (2 * vel_w.size + math.prod(shape)),
            transcendentals=0,
        ),
        name="lift",
    )(vel_w, buoy, table)


def plane_kernel(
    col_count, strat_ref, along_y_ref, along_x_ref, back_x_ref, back_y_ref, in_ref, out_ref
):
    blocks, _, depth, modes_x, lanes = in_ref.shape
    row_count = blocks // col_count
    for level in range(depth):
        grids = []
        for field in range(2):
            rows = []
            for row in range(row_count):
                parts = [in_ref[row * col_count + col, field, level] for col in range(col_count)]
                rows.append(jnp.concatenate(parts, axis=1))
            middle = jnp.dot(
                jnp.concatenate(rows, axis=0), along_y_ref[...], preferred_element_type=F32
            ).astype(BF16)
            grid = jnp.dot(along_x_ref[...], middle, preferred_element_type=F32)
            grids.append(grid.astype(BF16).astype(F32))
        velocity, gradient = grids
        strata = strat_ref[pl.program_id(0) * depth + level]
        flux_buoy = (-(velocity * gradient) - strata * velocity).astype(BF16)
        flux_vel = (-(velocity * jnp.abs(velocity))).astype(BF16)
        for field, flux in enumerate((flux_buoy, flux_vel)):
            folded = jnp.dot(back_x_ref[...], flux, preferred_element_type=F32).astype(BF16)
            values = jnp.dot(folded, back_y_ref[...], preferred_element_type=F32).astype(BF16)
            for row in range(row_count):
                for col in range(col_count):
                    out_ref[row * col_count + col, field, level] = values[
                        row * modes_x : (row + 1) * modes_x, col * lanes : (col + 1) * lanes
                    ]


def planes(kernels, arrived, strat, along_y, along_x, back_x, back_y, col_count):
    blocks, fields, depth, modes_x, modes_y = arrived.shape
    row_count = blocks // col_count
    if not kernels:
        parts = arrived.reshape(row_count, col_count, fields, depth, modes_x, modes_y)
        parts = jnp.transpose(parts, (2, 3, 0, 4, 1, 5))
        parts = parts.reshape(fields, depth, row_count * modes_x, col_count * modes_y)
        middle = jnp.einsum("fzak,ky->fzay", parts, along_y, preferred_element_type=F32)
        grids = jnp.einsum("xa,fzay->fzxy", along_x, middle.astype(BF16), preferred_element_type=F32)
        grids = grids.astype(BF16).astype(F32)
        flux_buoy = -(grids[0] * grids[1]) - strat[:, None, None] * grids[0]
        flux_vel = -(grids[0] * jnp.abs(grids[0]))
        fluxes = jnp.stack([flux_buoy, flux_vel]).astype(BF16)
        folded = jnp.einsum("ax,fzxy->fzay", back_x, fluxes, preferred_element_type=F32)
        values = jnp.einsum("fzay,yk->fzak", folded.astype(BF16), back_y, preferred_element_type=F32)
        values = values.astype(BF16).reshape(
            fields, depth, row_count, modes_x, col_count, modes_y
        )
        return jnp.transpose(values, (2, 4, 0, 1, 3, 5)).reshape(arrived.shape)
    block = pl.BlockSpec((blocks, fields, 1, modes_x, modes_y), lambda z: (0, 0, z, 0, 0))
    work = along_y.size * along_x.shape[1] + along_x.size * along_y.shape[1]
    return pl.pallas_call(
        lambda *refs: plane_kernel(col_count, *refs),
        grid=(depth,),
        in_specs=[
            pl.BlockSpec(memory_space=pltpu.SMEM),
            whole(along_y.shape),
            whole(along_x.shape),
            whole(back_x.shape),
            whole(back_y.shape),
            block,
        ],
        out_specs=block,
        out_shape=jax.ShapeDtypeStruct(arrived.shape, BF16),
        compiler_params=params(1),
        cost_estimate=pl.CostEstimate(
            flops=4 * fields * depth * work, bytes_accessed=4 * arrived.size, transcendentals=0
        ),
        name="planes",
    )(strat, along_y, along_x, back_x, back_y, arrived)


def solve_modal(modal_buoy, modal_vel, wave, eig_val):
    lapl = wave + eig_val
    diag_buoy = 1.0 + diffuse_buoy * lapl
    diag_vel = 1.0 + diffuse_vel * lapl
    scale = 1.0 / (diag_buoy * diag_vel + couple_buoy * couple_vel)
    solved_buoy = ((diag_vel * modal_buoy - couple_buoy * modal_vel) * scale).astype(BF16)
    solved_vel = ((diag_buoy * modal_vel + couple_vel * modal_buoy) * scale).astype(BF16)
    return (solved_buoy, solved_vel)


def finish_kernel(
    wave_x_ref, wave_y_ref, eig_val_ref, left_ref, right_ref, proj_ref, buoy_ref, vel_ref, *refs
):
    in_refs, out_refs = refs[:-2], refs[-2:]
    span, lanes, degree = buoy_ref.shape
    modal = []
    for field, coeff_ref in enumerate((buoy_ref, vel_ref)):
        parts = []
        for ref in in_refs:
            part = ref[:, field]
            parts.append(part.reshape(part.shape[0] * part.shape[1], span, lanes))
        fluxes = jnp.concatenate(parts, axis=0).astype(F32)
        fluxes = jnp.swapaxes(fluxes, 0, 1).astype(BF16)
        rows = []
        for mode in range(span):
            tend = lax.dot_general(
                fluxes[mode], proj_ref[...], (((0,), (0,)), ((), ())), preferred_element_type=F32
            )
            rows.append((coeff_ref[mode].astype(F32) + explicit_step * tend).astype(BF16))
        modal.append(
            jnp.dot(jnp.concatenate(rows, axis=0), left_ref[...], preferred_element_type=F32)
        )
    first = pl.program_id(0) * span
    waves = [4.0 * (wave_x_ref[first + mode] + wave_y_ref[...]) for mode in range(span)]
    solved = solve_modal(modal[0], modal[1], jnp.concatenate(waves, axis=0), eig_val_ref[...])
    for values, out_ref in zip(solved, out_refs):
        result = jnp.dot(values, right_ref[...], preferred_element_type=F32).astype(BF16)
        out_ref[...] = result.reshape(span, lanes, degree)


def finish(kernels, folded, buoy, vel_w, projs, eig_val, eig_left, eig_right, wave_x, wave_y):
    modes_x, modes_y, degree = buoy.shape
    if not kernels:
        tend = 0.0
        for part, proj in zip(folded, projs):
            parts = jnp.transpose(part, (1, 0, 2, 3, 4)).reshape(2, -1, modes_x, modes_y)
            tend += jnp.einsum("fzak,zn->fakn", parts, proj, preferred_element_type=F32)
        modal = []
        for field, coeffs in enumerate((buoy, vel_w)):
            rhs = (coeffs.astype(F32) + explicit_step * tend[field]).astype(BF16)
            modal.append(jnp.einsum("akn,nj->akj", rhs, eig_left, preferred_element_type=F32))
        wave = 4.0 * (wave_x[:, None, None] + wave_y[None, :, None])
        solved = solve_modal(modal[0], modal[1], wave, eig_val)
        return tuple(
            jnp.einsum("akj,jn->akn", values, eig_right, preferred_element_type=F32).astype(BF16)
            for values in solved
        )
    span = 8
    proj = jnp.concatenate(projs, axis=0)
    field_block = pl.BlockSpec((span, modes_y, degree), lambda a: (a, 0, 0))
    result = jax.ShapeDtypeStruct(buoy.shape, BF16)
    return pl.pallas_call(
        finish_kernel,
        grid=(modes_x // span,),
        in_specs=[
            pl.BlockSpec(memory_space=pltpu.SMEM),
            whole((modes_y, 1)),
            whole((1, degree)),
            whole(eig_left.shape),
            whole(eig_right.shape),
            whole(proj.shape),
            field_block,
            field_block,
        ]
        + [
            pl.BlockSpec(
                (part.shape[0], 2, part.shape[2], span, modes_y), lambda a: (0, 0, 0, a, 0)
            )
            for part in folded
        ],
        out_specs=[field_block, field_block],
        out_shape=[result, result],
        compiler_params=params(1),
        cost_estimate=pl.CostEstimate(
            flops=4 * buoy.size * (proj.shape[0] + 2 * degree),
            bytes_accessed=8 * buoy.size + sum(2 * part.size for part in folded),
            transcendentals=buoy.size,
        ),
        name="finish",
    )(
        wave_x,
        wave_y[:, None],
        eig_val[None, :],
        eig_left,
        eig_right,
        proj,
        buoy,
        vel_w,
        *folded,
    )


def chunk_sizes(own):
    first = min(own, max(1, own * 4 // 18))
    second = (own - first) // 2
    return [size for size in (first, second, own - first - second) if size]


def per_device(buoy, vel_w, strat, eig_val, eig_left, eig_right):
    row_count = lax.axis_size("row")
    col_count = lax.axis_size("col")
    blocks = row_count * col_count
    modes_x, modes_y, degree = buoy.shape
    total_x, total_y = modes_x * row_count, modes_y * col_count
    grid_x, grid_y = 3 * total_x // 2, 3 * total_y // 2
    shard = strat.shape[0]
    own = -(-shard // row_count)
    padding = own * row_count - shard
    kernels = modes_y % 128 == 0 and modes_x % 16 == 0 and degree % 128 == 0
    row = lax.axis_index("row")
    col = lax.axis_index("col")


    def by_device(table):
        table = table.reshape(col_count, shard, degree)
        table = np.pad(table, ((0, 0), (0, padding), (0, 0)))
        table = table.reshape(col_count, row_count, own, degree)
        return np.transpose(table, (1, 0, 2, 3)).reshape(blocks, own, degree)

    def exchange(values):
        return lax.all_to_all(values, ("row", "col"), split_axis=0, concat_axis=0, tiled=True)

    levels, slopes, projector = cheb_tables(degree, shard * col_count)
    forward_z = np.stack([by_device(levels.T), by_device(slopes.T)])
    backward_z = by_device(projector)
    along_x = jnp.asarray(np.ascontiguousarray(fourier_eval(total_x, grid_x).T))
    back_x = jnp.asarray(np.ascontiguousarray(fourier_proj(total_x, grid_x).T))
    along_y = jnp.asarray(fourier_eval(total_y, grid_y))
    back_y = jnp.asarray(np.ascontiguousarray(fourier_proj(total_y, grid_y)))
    strat_own = lax.dynamic_slice_in_dim(jnp.pad(strat, (0, padding)), row * own, own)

    folded, projs = [], []
    start = 0
    for depth in chunk_sizes(own):
        stop = start + depth
        table = jnp.asarray(forward_z[:, :, start:stop].reshape(2, blocks * depth, degree))
        projs.append(jnp.asarray(backward_z[:, start:stop].reshape(blocks * depth, degree)))
        arrived = exchange(lift(kernels, vel_w, buoy, table, blocks))
        fluxes = planes(
            kernels,
            arrived,
            strat_own[start:stop],
            along_y,
            along_x,
            back_x,
            back_y,
            col_count,
        )
        folded.append(exchange(fluxes))
        start = stop
    wave_x = wave_squares(total_x, row * modes_x, modes_x)
    wave_y = wave_squares(total_y, col * modes_y, modes_y)
    return finish(
        kernels, folded, buoy, vel_w, projs, eig_val, eig_left, eig_right, wave_x, wave_y
    )


def solution(mesh):
    in_specs = (P("row", "col", None), P("row", "col", None), P("col"), P(), P(), P())
    out_specs = (P("row", "col", None), P("row", "col", None))
    return jax.shard_map(
        per_device, mesh=mesh, in_specs=in_specs, out_specs=out_specs, check_vma=False
    )
```

time: 1300 us -> 938 us (0.72)
  waiting for transfers between devices: 918 us -> 731 us
  blocking collectives: 76 us -> 0 us
  Pallas kernels: 213 us -> 166 us
  starting transfers between devices: 67.5 us -> 36.4 us
  local copies, waits for them, and re-layouts: 18.6 us -> 1.97 us
    ppermute x24 -> x0, waiting for transfers between devices: 527 us -> none  [exchange_col(): arrived.append(lax.ppermute(blocks[shift], 'col', pairs))]
    all_to_all x8 -> x6, waiting for transfers between devices: 391 us -> 731 us  [exchange(): lax.all_to_all(values, ('row', 'col'), split_axis=0, concat_axis=0, tiled...]
    unnamed x1 -> x0, blocking collectives: 76 us -> none
    pallas_call x12 -> x3, Pallas kernels: 131 us -> 91.5 us  [planes(): pl.pallas_call(lambda *refs: plane_kernel(col_count, *refs), grid=(depth,...]
    ppermute x24 -> x0, starting transfers between devices: 28.4 us -> none  [exchange_col(): arrived.append(lax.ppermute(blocks[shift], 'col', pairs))]
    pallas_call x4 -> x3, Pallas kernels: 37.5 us -> 30.7 us  [lift(): pl.pallas_call(lift_kernel, grid=(modes_x // span,), in_specs=[pl.BlockSp...]
    all_to_all x8 -> x6, starting transfers between devices: 39 us -> 36.4 us  [exchange(): lax.all_to_all(values, ('row', 'col'), split_axis=0, concat_axis=0, tiled...]
  transfers between devices with their start and end apart: 32 -> 6, of which waited for: 19 -> 6; matrix products, arithmetic and copies ran while one was open for 1% -> 0% of each run, Pallas kernels for 12% -> 12%
where the time goes in v2:
time: 938 us
  waiting for transfers between devices  731 us (78%)
  Pallas kernels  166 us (18%)
  starting transfers between devices  36.4 us (4%)
    all_to_all x6, waiting for transfers between devices, exchange(): lax.all_to_all(values, ('row', 'col'), split_axis=0, concat_axis=0, tiled...  731 us
    pallas_call x3, Pallas kernels, planes(): pl.pallas_call(lambda *refs: plane_kernel(col_count, *refs), grid=(depth,...  91.5 us
    pallas_call x1, Pallas kernels, finish(): pl.pallas_call(finish_kernel, grid=(modes_x // span,), in_specs=[pl.Block...  44.1 us
    all_to_all x6, starting transfers between devices, exchange(): lax.all_to_all(values, ('row', 'col'), split_axis=0, concat_axis=0, tiled...  36.4 us
    pallas_call x3, Pallas kernels, lift(): pl.pallas_call(lift_kernel, grid=(modes_x // span,), in_specs=[pl.BlockSp...  30.7 us
  transfers between devices with their start and end apart: 6, of which 6 were waited for; matrix products, arithmetic and copies ran while one was open for 0% of the time, Pallas kernels for 12%

profile of v2, /device:TPU:0, one launch (start us, length us, event | category | flops | bytes accessed | tf_op | source)
XLA Modules:
  0.0 937.9 jit_solution(6575667008249390007)
XLA Ops:
  0.6 9.1 lift.3
  9.8 7.4 all-to-all-start
  17.2 10.8 %lift.4 = bf16[32,2,7,64,128]{4,3,2,1,0:T(8,128)(2,1)} custom-call(bf16[64,128,384]{2,1,0:T(8,128)(2,1)} %vel_ref.7, bf16[64,128,384]{2,1,0:T(8,128)(2,1)} %buoy_ref.7, bf16[2,224,384]{2,1,0:T(8,128)(2,1)} %constant.72.clone.table_ref), custom_call_target="tpu_custom_call" | custom-call | flops 2818572288 | bytes 19922944 | tf_op jit(solution)/shard_map/lift/pallas_call | solution.py:90
  28.0 83.5 %all-to-all-done.refs_5_ = bf16[32,2,4,64,128]{4,3,2,1,0:T(8,128)(2,1)} async-done(((bf16[32,2,4,64,128]{4,3,2,1,0:T(8,128)(2,1)}), bf16[32,2,4,64,128]{4,3,2,1,0:T(8,128)(2,1)}, u32[]{:S(2)}, u32[]{:S(2)}) %all-to-all-start) | async-done | bytes 4194336 | tf_op jit(solution)/shard_map/all_to_all | solution.py:313
  111.5 5.8 all-to-all-start.2
  117.4 10.8 %lift.5 = bf16[32,2,7,64,128]{4,3,2,1,0:T(8,128)(2,1)} custom-call(bf16[64,128,384]{2,1,0:T(8,128)(2,1)} %vel_ref.7, bf16[64,128,384]{2,1,0:T(8,128)(2,1)} %buoy_ref.7, bf16[2,224,384]{2,1,0:T(8,128)(2,1)} %constant.74.clone.table_ref), custom_call_target="tpu_custom_call" | custom-call | flops 2818572288 | bytes 19922944 | tf_op jit(solution)/shard_map/lift/pallas_call | solution.py:90
  128.2 0.0 copy-start.2
  128.2 154.1 %all-to-all-done.2.refs_5_ = bf16[32,2,7,64,128]{4,3,2,1,0:T(8,128)(2,1)} async-done(((bf16[32,2,7,64,128]{4,3,2,1,0:T(8,128)(2,1)}), bf16[32,2,7,64,128]{4,3,2,1,0:T(8,128)(2,1)}, u32[]{:S(2)}, u32[]{:S(2)}) %all-to-all-start.2) | async-done | bytes 7340064 | tf_op jit(solution)/shard_map/all_to_all | solution.py:313
  282.2 5.6 all-to-all-start.4
  287.9 0.0 copy-done.2
  287.9 0.6 dynamic_slice.3
  288.5 21.3 %planes.3 = bf16[32,2,4,64,128]{4,3,2,1,0:T(8,128)(2,1)} custom-call(f32[4]{0:T(128)} %bitcast.1, bf16[512,768]{1,0:T(8,128)(2,1)} %constant.68.clone.refs_1_, bf16[768,512]{1,0:T(8,128)(2,1)} %constant.66.clone.refs_2_, bf16[512,768]{1,0:T(8,128)(2,1)} %constant.67.clone.refs_3_, bf16[768,512]{1,0:T(8,128)(2,1)} %constant.69.clone.refs_4_, ...), custom_call_target="tpu_custom_call" | custom-call | flops 16106127360 | bytes 8388608 | tf_op jit(solution)/shard_map/planes/pallas_call | solution.py:162
  309.8 0.0 copy-start.1
  309.8 142.9 %all-to-all-done.4.refs_5_ = bf16[32,2,7,64,128]{4,3,2,1,0:T(8,128)(2,1)} async-done(((bf16[32,2,7,64,128]{4,3,2,1,0:T(8,128)(2,1)}), bf16[32,2,7,64,128]{4,3,2,1,0:T(8,128)(2,1)}, u32[]{:S(2)}, u32[]{:S(2)}) %all-to-all-start.4) | async-done | bytes 7340064 | tf_op jit(solution)/shard_map/all_to_all | solution.py:313
  452.7 5.8 all-to-all-start.1
  458.6 0.0 copy-done.1
  458.6 0.7 fusion
  459.2 35.1 %planes.4 = bf16[32,2,7,64,128]{4,3,2,1,0:T(8,128)(2,1)} custom-call(f32[7]{0:T(128)} %get-tuple-element.3.refs_0_, bf16[512,768]{1,0:T(8,128)(2,1)} %constant.68.clone.refs_1_, bf16[768,512]{1,0:T(8,128)(2,1)} %constant.66.clone.refs_2_, bf16[512,768]{1,0:T(8,128)(2,1)} %constant.67.clone.refs_3_, bf16[768,512]{1,0:T(8,128)(2,1)} %constant.69.clone.refs_4_, ...), custom_call_target="tpu_custom_call" | custom-call | flops 28185722880 | bytes 14680064 | tf_op jit(solution)/shard_map/planes/pallas_call | solution.py:162
  494.3 58.5 %all-to-all-done.1.refs_0_ = bf16[32,2,4,64,128]{4,3,2,1,0:T(8,128)(2,1)} async-done(((bf16[32,2,4,64,128]{4,3,2,1,0:T(8,128)(2,1)}), bf16[32,2,4,64,128]{4,3,2,1,0:T(8,128)(2,1)}, u32[]{:S(2)}, u32[]{:S(2)}) %all-to-all-start.1) | async-done | bytes 4194336 | tf_op jit(solution)/shard_map/all_to_all | solution.py:313
  552.8 5.8 all-to-all-start.3
  558.5 35.1 %planes.5 = bf16[32,2,7,64,128]{4,3,2,1,0:T(8,128)(2,1)} custom-call(f32[7]{0:T(128)} %get-tuple-element.2.refs_0_, bf16[512,768]{1,0:T(8,128)(2,1)} %constant.68.clone.refs_1_, bf16[768,512]{1,0:T(8,128)(2,1)} %constant.66.clone.refs_2_, bf16[512,768]{1,0:T(8,128)(2,1)} %constant.67.clone.refs_3_, bf16[768,512]{1,0:T(8,128)(2,1)} %constant.69.clone.refs_4_, ...), custom_call_target="tpu_custom_call" | custom-call | flops 28185722880 | bytes 14680064 | tf_op jit(solution)/shard_map/planes/pallas_call | solution.py:162
  593.6 0.0 copy-start
  593.6 129.8 %all-to-all-done.3.refs_1_ = bf16[32,2,7,64,128]{4,3,2,1,0:T(8,128)(2,1)} async-done(((bf16[32,2,7,64,128]{4,3,2,1,0:T(8,128)(2,1)}), bf16[32,2,7,64,128]{4,3,2,1,0:T(8,128)(2,1)}, u32[]{:S(2)}, u32[]{:S(2)}) %all-to-all-start.3) | async-done | bytes 7340064 | tf_op jit(solution)/shard_map/all_to_all | solution.py:313
  723.4 5.9 all-to-all-start.5
  729.3 0.0 copy-done
  729.3 0.6 broadcast_in_dim.4.eig_val_ref
  729.9 0.1 copy.19
  730.0 0.6 mul.48.wave_y_ref
  730.6 0.6 multiply_multiply_fusion.wave_x_ref
  731.2 162.5 %all-to-all-done.5.refs_2_ = bf16[32,2,7,64,128]{4,3,2,1,0:T(8,128)(2,1)} async-done(((bf16[32,2,7,64,128]{4,3,2,1,0:T(8,128)(2,1)}), bf16[32,2,7,64,128]{4,3,2,1,0:T(8,128)(2,1)}, u32[]{:S(2)}, u32[]{:S(2)}) %all-to-all-start.5) | async-done | bytes 7340064 | tf_op jit(solution)/shard_map/all_to_all | solution.py:313
  893.8 44.1 %finish.1 = (bf16[64,128,384]{2,1,0:T(8,128)(2,1)}, bf16[64,128,384]{2,1,0:T(8,128)(2,1)}) custom-call(f32[64]{0:T(128)} %multiply_multiply_fusion.wave_x_ref, f32[128,1]{1,0:T(8,128)} %mul.48.wave_y_ref, f32[1,384]{1,0:T(1,128)} %broadcast_in_dim.4.eig_val_ref, bf16[384,384]{1,0:T(8,128)(2,1)} %left_ref.1, bf16[384,384]{1,0:T(8,128)(2,1)} %right_ref.1, ...), custom_call_target="tpu_custom_call" | custom-call | flops 16911433728 | bytes 44040192 | tf_op jit(solution)/shard_map/finish/pallas_call | solution.py:244
  (1 shorter events, 0.0 us)
Async XLA Ops:
  9.8 101.8 %all-to-all-start = ((bf16[32,2,4,64,128]{4,3,2,1,0:T(8,128)(2,1)}), bf16[32,2,4,64,128]{4,3,2,1,0:T(8,128)(2,1)}, u32[]{:S(2)}, u32[]{:S(2)}) async-start(bf16[32,2,4,64,128]{4,3,2,1,0:T(8,128)(2,1)} %lift.3), calls=%async_computation | async-start | bytes 8388608 | tf_op jit(solution)/shard_map/all_to_all | solution.py:313
  111.5 170.7 %all-to-all-start.2 = ((bf16[32,2,7,64,128]{4,3,2,1,0:T(8,128)(2,1)}), bf16[32,2,7,64,128]{4,3,2,1,0:T(8,128)(2,1)}, u32[]{:S(2)}, u32[]{:S(2)}) async-start(bf16[32,2,7,64,128]{4,3,2,1,0:T(8,128)(2,1)} %lift.4), calls=%async_computation.2 | async-start | bytes 14680064 | tf_op jit(solution)/shard_map/all_to_all | solution.py:313
  128.2 159.7 %copy-start.2 = (f32[144]{0:T(256)S(1)}, f32[144]{0:T(256)}, u32[]{:S(2)}) copy-start(f32[144]{0:T(256)} %param.18) | copy-start | bytes 1732
  282.2 170.5 %all-to-all-start.4 = ((bf16[32,2,7,64,128]{4,3,2,1,0:T(8,128)(2,1)}), bf16[32,2,7,64,128]{4,3,2,1,0:T(8,128)(2,1)}, u32[]{:S(2)}, u32[]{:S(2)}) async-start(bf16[32,2,7,64,128]{4,3,2,1,0:T(8,128)(2,1)} %lift.5), calls=%async_computation.4 | async-start | bytes 14680064 | tf_op jit(solution)/shard_map/all_to_all | solution.py:313
  309.8 148.8 %copy-start.1 = (f32[18]{0:T(128)S(1)}, f32[18]{0:T(128)}, u32[]{:S(2)}) copy-start(f32[18]{0:T(128)} %dynamic_slice.3) | copy-start | bytes 220
  452.7 100.0 %all-to-all-start.1 = ((bf16[32,2,4,64,128]{4,3,2,1,0:T(8,128)(2,1)}), bf16[32,2,4,64,128]{4,3,2,1,0:T(8,128)(2,1)}, u32[]{:S(2)}, u32[]{:S(2)}) async-start(bf16[32,2,4,64,128]{4,3,2,1,0:T(8,128)(2,1)} %planes.3), calls=%async_computation.1 | async-start | bytes 8388608 | tf_op jit(solution)/shard_map/all_to_all | solution.py:313
  552.8 170.6 %all-to-all-start.3 = ((bf16[32,2,7,64,128]{4,3,2,1,0:T(8,128)(2,1)}), bf16[32,2,7,64,128]{4,3,2,1,0:T(8,128)(2,1)}, u32[]{:S(2)}, u32[]{:S(2)}) async-start(bf16[32,2,7,64,128]{4,3,2,1,0:T(8,128)(2,1)} %planes.4), calls=%async_computation.3 | async-start | bytes 14680064 | tf_op jit(solution)/shard_map/all_to_all | solution.py:313
  593.6 135.7 %copy-start = (f32[384]{0:T(512)S(1)}, f32[384]{0:T(512)}, u32[]{:S(2)}) copy-start(f32[384]{0:T(512)} %param.19) | copy-start | bytes 4612
  723.4 170.4 %all-to-all-start.5 = ((bf16[32,2,7,64,128]{4,3,2,1,0:T(8,128)(2,1)}), bf16[32,2,7,64,128]{4,3,2,1,0:T(8,128)(2,1)}, u32[]{:S(2)}, u32[]{:S(2)}) async-start(bf16[32,2,7,64,128]{4,3,2,1,0:T(8,128)(2,1)} %planes.5), calls=%async_computation.5 | async-start | bytes 14680064 | tf_op jit(solution)/shard_map/all_to_all | solution.py:313

commit v3 on v2

--- a/solution.py
+++ b/solution.py
@@ -108,8 +108,9 @@
 
 
 def plane_kernel(
-    col_count, strat_ref, along_y_ref, along_x_ref, back_x_ref, back_y_ref, in_ref, out_ref
+    col_count, strat_ref, along_y_ref, along_x_ref, back_x_ref, back_y_ref, in_ref, *refs
 ):
+    out_ref = refs[-1]
     blocks, _, depth, modes_x, lanes = in_ref.shape
     row_count = blocks // col_count
     for level in range(depth):
@@ -138,7 +139,7 @@
                     ]
 
 
-def planes(kernels, arrived, strat, along_y, along_x, back_x, back_y, col_count):
+def planes(kernels, arrived, strat, along_y, along_x, back_x, back_y, col_count, after):
     blocks, fields, depth, modes_x, modes_y = arrived.shape
     row_count = blocks // col_count
     if not kernels:
@@ -169,7 +170,8 @@
             whole(back_x.shape),
             whole(back_y.shape),
             block,
-        ],
+        ]
+        + [pl.BlockSpec(memory_space=pl.ANY)] * len(after),
         out_specs=block,
         out_shape=jax.ShapeDtypeStruct(arrived.shape, BF16),
         compiler_params=params(1),
@@ -177,7 +179,7 @@
             flops=4 * fields * depth * work, bytes_accessed=4 * arrived.size, transcendentals=0
         ),
         name="planes",
-    )(strat, along_y, along_x, back_x, back_y, arrived)
+    )(strat, along_y, along_x, back_x, back_y, arrived, *after)
 
 
 def solve_modal(modal_buoy, modal_vel, wave, eig_val):
@@ -190,28 +192,69 @@
     return (solved_buoy, solved_vel)
 
 
+def project(ref, field, proj_ref):
+    blocks, _, depth, span, lanes = ref.shape
+    fluxes = ref[:, field].reshape(blocks * depth, span, lanes).astype(F32)
+    fluxes = jnp.swapaxes(fluxes, 0, 1).astype(BF16)
+    rows = [jnp.transpose(fluxes[mode]) for mode in range(span)]
+    return jnp.dot(jnp.concatenate(rows, axis=0), proj_ref[...], preferred_element_type=F32)
+
+
+def gather_kernel(proj_ref, buoy_ref, vel_ref, in_ref, *out_refs):
+    span, lanes, degree = buoy_ref.shape
+    for field, (coeff_ref, out_ref) in enumerate(zip((buoy_ref, vel_ref), out_refs)):
+        tend = explicit_step * project(in_ref, field, proj_ref)
+        out_ref[...] = coeff_ref[...].astype(F32) + tend.reshape(span, lanes, degree)
+
+
+def gather(kernels, folded, proj, rhs):
+    modes_x, modes_y, degree = rhs[0].shape
+    blocks, fields, depth = folded.shape[:3]
+    if not kernels:
+        parts = jnp.transpose(folded, (1, 0, 2, 3, 4)).reshape(2, -1, modes_x, modes_y)
+        tend = jnp.einsum("fzak,zn->fakn", parts, proj, preferred_element_type=F32)
+        return [part.astype(F32) + explicit_step * tend[f] for f, part in enumerate(rhs)]
+    span = 8
+    block = pl.BlockSpec((span, modes_y, degree), lambda a: (a, 0, 0))
+    return pl.pallas_call(
+        gather_kernel,
+        grid=(modes_x // span,),
+        in_specs=[
+            whole(proj.shape),
+            block,
+            block,
+            pl.BlockSpec((blocks, fields, depth, span, modes_y), lambda a: (0, 0, 0, a, 0)),
+        ],
+        out_specs=[block, block],
+        out_shape=[jax.ShapeDtypeStruct(rhs[0].shape, F32)] * 2,
+        compiler_params=params(1),
+        cost_estimate=pl.CostEstimate(
+            flops=4 * rhs[0].size * proj.shape[0],
+            bytes_accessed=2 * folded.size + 14 * rhs[0].size,
+            transcendentals=0,
+        ),
+        name="gather",
+    )(proj, *rhs, folded)
+
+
 def finish_kernel(
-    wave_x_ref, wave_y_ref, eig_val_ref, left_ref, right_ref, proj_ref, buoy_ref, vel_ref, *refs
+    wave_x_ref,
+    wave_y_ref,
+    eig_val_ref,
+    left_ref,
+    right_ref,
+    proj_ref,
+    buoy_ref,
+    vel_ref,
+    in_ref,
+    *out_refs,
 ):
-    in_refs, out_refs = refs[:-2], refs[-2:]
     span, lanes, degree = buoy_ref.shape
     modal = []
-    for field, coeff_ref in enumerate((buoy_ref, vel_ref)):
-        parts = []
-        for ref in in_refs:
-            part = ref[:, field]
-            parts.append(part.reshape(part.shape[0] * part.shape[1], span, lanes))
-        fluxes = jnp.concatenate(parts, axis=0).astype(F32)
-        fluxes = jnp.swapaxes(fluxes, 0, 1).astype(BF16)
-        rows = []
-        for mode in range(span):
-            tend = lax.dot_general(
-                fluxes[mode], proj_ref[...], (((0,), (0,)), ((), ())), preferred_element_type=F32
-            )
-            rows.append((coeff_ref[mode].astype(F32) + explicit_step * tend).astype(BF16))
-        modal.append(
-            jnp.dot(jnp.concatenate(rows, axis=0), left_ref[...], preferred_element_type=F32)
-        )
+    for field, rhs_ref in enumerate((buoy_ref, vel_ref)):
+        tend = explicit_step * project(in_ref, field, proj_ref)
+        rhs = rhs_ref[...].reshape(span * lanes, degree).astype(F32) + tend
+        modal.append(jnp.dot(rhs.astype(BF16), left_ref[...], preferred_element_type=F32))
     first = pl.program_id(0) * span
     waves = [4.0 * (wave_x_ref[first + mode] + wave_y_ref[...]) for mode in range(span)]
     solved = solve_modal(modal[0], modal[1], jnp.concatenate(waves, axis=0), eig_val_ref[...])
@@ -220,17 +263,13 @@
         out_ref[...] = result.reshape(span, lanes, degree)
 
 
-def finish(kernels, folded, buoy, vel_w, projs, eig_val, eig_left, eig_right, wave_x, wave_y):
-    modes_x, modes_y, degree = buoy.shape
+def finish(kernels, folded, proj, rhs, eig_val, eig_left, eig_right, wave_x, wave_y):
+    modes_x, modes_y, degree = rhs[0].shape
     if not kernels:
-        tend = 0.0
-        for part, proj in zip(folded, projs):
-            parts = jnp.transpose(part, (1, 0, 2, 3, 4)).reshape(2, -1, modes_x, modes_y)
-            tend += jnp.einsum("fzak,zn->fakn", parts, proj, preferred_element_type=F32)
         modal = []
-        for field, coeffs in enumerate((buoy, vel_w)):
-            rhs = (coeffs.astype(F32) + explicit_step * tend[field]).astype(BF16)
-            modal.append(jnp.einsum("akn,nj->akj", rhs, eig_left, preferred_element_type=F32))
+        for part in gather(kernels, folded, proj, rhs):
+            part = part.astype(BF16)
+            modal.append(jnp.einsum("akn,nj->akj", part, eig_left, preferred_element_type=F32))
         wave = 4.0 * (wave_x[:, None, None] + wave_y[None, :, None])
         solved = solve_modal(modal[0], modal[1], wave, eig_val)
         return tuple(
@@ -238,9 +277,9 @@
             for values in solved
         )
     span = 8
-    proj = jnp.concatenate(projs, axis=0)
-    field_block = pl.BlockSpec((span, modes_y, degree), lambda a: (a, 0, 0))
-    result = jax.ShapeDtypeStruct(buoy.shape, BF16)
+    blocks, fields, depth = folded.shape[:3]
+    block = pl.BlockSpec((span, modes_y, degree), lambda a: (a, 0, 0))
+    result = jax.ShapeDtypeStruct(rhs[0].shape, BF16)
     return pl.pallas_call(
         finish_kernel,
         grid=(modes_x // span,),
@@ -251,22 +290,17 @@
             whole(eig_left.shape),
             whole(eig_right.shape),
             whole(proj.shape),
-            field_block,
-            field_block,
-        ]
-        + [
-            pl.BlockSpec(
-                (part.shape[0], 2, part.shape[2], span, modes_y), lambda a: (0, 0, 0, a, 0)
-            )
-            for part in folded
+            block,
+            block,
+            pl.BlockSpec((blocks, fields, depth, span, modes_y), lambda a: (0, 0, 0, a, 0)),
         ],
-        out_specs=[field_block, field_block],
+        out_specs=[block, block],
         out_shape=[result, result],
         compiler_params=params(1),
         cost_estimate=pl.CostEstimate(
-            flops=4 * buoy.size * (proj.shape[0] + 2 * degree),
-            bytes_accessed=8 * buoy.size + sum(2 * part.size for part in folded),
-            transcendentals=buoy.size,
+            flops=4 * rhs[0].size * (proj.shape[0] + 2 * degree),
+            bytes_accessed=12 * rhs[0].size + 2 * folded.size,
+            transcendentals=rhs[0].size,
         ),
         name="finish",
     )(
@@ -276,9 +310,8 @@
         eig_left,
         eig_right,
         proj,
-        buoy,
-        vel_w,
-        *folded,
+        *rhs,
+        folded,
     )
 
 
@@ -321,29 +354,41 @@
     back_y = jnp.asarray(np.ascontiguousarray(fourier_proj(total_y, grid_y)))
     strat_own = lax.dynamic_slice_in_dim(jnp.pad(strat, (0, padding)), row * own, own)
 
-    folded, projs = [], []
-    start = 0
-    for depth in chunk_sizes(own):
-        stop = start + depth
-        table = jnp.asarray(forward_z[:, :, start:stop].reshape(2, blocks * depth, degree))
-        projs.append(jnp.asarray(backward_z[:, start:stop].reshape(blocks * depth, degree)))
-        arrived = exchange(lift(kernels, vel_w, buoy, table, blocks))
+    sizes = chunk_sizes(own)
+    stops = np.cumsum(sizes)
+    pieces = [(int(stop - size), int(stop)) for size, stop in zip(sizes, stops)]
+    arrived = []
+    for start, stop in pieces:
+        table = forward_z[:, :, start:stop].reshape(2, blocks * (stop - start), degree)
+        arrived.append(exchange(lift(kernels, vel_w, buoy, jnp.asarray(table), blocks)))
+    order = list(range(1, len(pieces))) + [0]
+    folded, after = [], []
+    for piece in order:
+        start, stop = pieces[piece]
         fluxes = planes(
             kernels,
-            arrived,
+            arrived[piece],
             strat_own[start:stop],
             along_y,
             along_x,
             back_x,
             back_y,
             col_count,
+            after,
         )
+        after = [fluxes]
         folded.append(exchange(fluxes))
-        start = stop
+    projs = [
+        jnp.asarray(backward_z[:, start:stop].reshape(blocks * (stop - start), degree))
+        for start, stop in (pieces[piece] for piece in order)
+    ]
+    rhs = [buoy, vel_w]
+    for part, proj in zip(folded[:-1], projs[:-1]):
+        rhs = gather(kernels, part, proj, rhs)
     wave_x = wave_squares(total_x, row * modes_x, modes_x)
     wave_y = wave_squares(total_y, col * modes_y, modes_y)
     return finish(
-        kernels, folded, buoy, vel_w, projs, eig_val, eig_left, eig_right, wave_x, wave_y
+        kernels, folded[-1], projs[-1], rhs, eig_val, eig_left, eig_right, wave_x, wave_y
     )
 
 

time: 938 us -> 923 us (0.984)
  waiting for transfers between devices: 731 us -> 691 us
  Pallas kernels: 166 us -> 192 us
    pallas_call x0 -> x2, Pallas kernels: none -> 40.4 us  [gather(): pl.pallas_call(gather_kernel, grid=(modes_x // span,), in_specs=[whole(pr...]
    all_to_all x6, waiting for transfers between devices: 731 us -> 691 us  [exchange(): lax.all_to_all(values, ('row', 'col'), split_axis=0, concat_axis=0, tiled...]
    pallas_call x1, Pallas kernels: 44.1 us -> 29 us  [finish(): pl.pallas_call(finish_kernel, grid=(modes_x // span,), in_specs=[pl.Block...]
  transfers between devices with their start and end apart: 6 -> 6, of which waited for: 6 -> 6; matrix products, arithmetic and copies ran while one was open for 0% -> 0% of each run, Pallas kernels for 12% -> 17%
where the time goes in v3:
time: 923 us
  waiting for transfers between devices  691 us (75%)
  Pallas kernels  192 us (21%)
  starting transfers between devices  36.3 us (4%)
    all_to_all x6, waiting for transfers between devices, exchange(): lax.all_to_all(values, ('row', 'col'), split_axis=0, concat_axis=0, tiled...  691 us
    pallas_call x3, Pallas kernels, planes(): pl.pallas_call(lambda *refs: plane_kernel(col_count, *refs), grid=(depth,...  91.6 us
    pallas_call x2, Pallas kernels, gather(): pl.pallas_call(gather_kernel, grid=(modes_x // span,), in_specs=[whole(pr...  40.4 us
    all_to_all x6, starting transfers between devices, exchange(): lax.all_to_all(values, ('row', 'col'), split_axis=0, concat_axis=0, tiled...  36.3 us
    pallas_call x3, Pallas kernels, lift(): pl.pallas_call(lift_kernel, grid=(modes_x // span,), in_specs=[pl.BlockSp...  30.8 us
    pallas_call x1, Pallas kernels, finish(): pl.pallas_call(finish_kernel, grid=(modes_x // span,), in_specs=[pl.Block...  29 us
  transfers between devices with their start and end apart: 6, of which 6 were waited for; matrix products, arithmetic and copies ran while one was open for 0% of the time, Pallas kernels for 17%

profile of v3, /device:TPU:0, one launch (start us, length us, event | category | flops | bytes accessed | tf_op | source)
XLA Modules:
  0.0 922.8 jit_solution(3746929554840216811)
XLA Ops:
  0.6 9.1 lift.5
  9.8 7.4 all-to-all-start.4
  17.2 10.8 %lift.3 = bf16[32,2,7,64,128]{4,3,2,1,0:T(8,128)(2,1)} custom-call(bf16[64,128,384]{2,1,0:T(8,128)(2,1)} %vel_ref.7, bf16[64,128,384]{2,1,0:T(8,128)(2,1)} %buoy_ref.7, bf16[2,224,384]{2,1,0:T(8,128)(2,1)} %constant.71.clone.table_ref), custom_call_target="tpu_custom_call" | custom-call | flops 2818572288 | bytes 19922944 | tf_op jit(solution)/shard_map/lift/pallas_call | solution.py:90
  28.0 83.6 %all-to-all-done.4.refs_5_ = bf16[32,2,4,64,128]{4,3,2,1,0:T(8,128)(2,1)} async-done(((bf16[32,2,4,64,128]{4,3,2,1,0:T(8,128)(2,1)}), bf16[32,2,4,64,128]{4,3,2,1,0:T(8,128)(2,1)}, u32[]{:S(2)}, u32[]{:S(2)}) %all-to-all-start.4) | async-done | bytes 4194336 | tf_op jit(solution)/shard_map/all_to_all | solution.py:346
  111.5 5.8 all-to-all-start
  117.4 10.9 %lift.4 = bf16[32,2,7,64,128]{4,3,2,1,0:T(8,128)(2,1)} custom-call(bf16[64,128,384]{2,1,0:T(8,128)(2,1)} %vel_ref.7, bf16[64,128,384]{2,1,0:T(8,128)(2,1)} %buoy_ref.7, bf16[2,224,384]{2,1,0:T(8,128)(2,1)} %constant.72.clone.table_ref), custom_call_target="tpu_custom_call" | custom-call | flops 2818572288 | bytes 19922944 | tf_op jit(solution)/shard_map/lift/pallas_call | solution.py:90
  128.2 0.0 copy-start.2
  128.2 154.0 %all-to-all-done.refs_5_ = bf16[32,2,7,64,128]{4,3,2,1,0:T(8,128)(2,1)} async-done(((bf16[32,2,7,64,128]{4,3,2,1,0:T(8,128)(2,1)}), bf16[32,2,7,64,128]{4,3,2,1,0:T(8,128)(2,1)}, u32[]{:S(2)}, u32[]{:S(2)}) %all-to-all-start) | async-done | bytes 7340064 | tf_op jit(solution)/shard_map/all_to_all | solution.py:346
  282.2 5.6 all-to-all-start.2
  287.9 0.0 copy-done.2
  287.9 0.1 dynamic_slice.3
  288.0 0.0 copy-start.1
  288.0 0.6 fusion
  288.5 35.1 %planes.3.refs_6_ = bf16[32,2,7,64,128]{4,3,2,1,0:T(8,128)(2,1)} custom-call(f32[7]{0:T(128)} %get-tuple-element.11.refs_0_, bf16[512,768]{1,0:T(8,128)(2,1)} %constant.68.clone.refs_1_, bf16[768,512]{1,0:T(8,128)(2,1)} %constant.66.clone.refs_2_, bf16[512,768]{1,0:T(8,128)(2,1)} %constant.67.clone.refs_3_, bf16[768,512]{1,0:T(8,128)(2,1)} %constant.69.clone.refs_4_, ...), custom_call_target="tpu_custom_call" | custom-call | flops 28185722880 | bytes 14680064 | tf_op jit(solution)/shard_map/planes/pallas_call | solution.py:163
  323.7 0.0 copy-done.1
  323.7 129.0 %all-to-all-done.2.refs_5_ = bf16[32,2,7,64,128]{4,3,2,1,0:T(8,128)(2,1)} async-done(((bf16[32,2,7,64,128]{4,3,2,1,0:T(8,128)(2,1)}), bf16[32,2,7,64,128]{4,3,2,1,0:T(8,128)(2,1)}, u32[]{:S(2)}, u32[]{:S(2)}) %all-to-all-start.2) | async-done | bytes 7340064 | tf_op jit(solution)/shard_map/all_to_all | solution.py:346
  452.7 5.8 all-to-all-start.1
  458.5 35.1 %planes.4.refs_6_ = bf16[32,2,7,64,128]{4,3,2,1,0:T(8,128)(2,1)} custom-call(f32[7]{0:T(128)} %get-tuple-element.10.refs_0_, bf16[512,768]{1,0:T(8,128)(2,1)} %constant.68.clone.refs_1_, bf16[768,512]{1,0:T(8,128)(2,1)} %constant.66.clone.refs_2_, bf16[512,768]{1,0:T(8,128)(2,1)} %constant.67.clone.refs_3_, bf16[768,512]{1,0:T(8,128)(2,1)} %constant.69.clone.refs_4_, ...), custom_call_target="tpu_custom_call" | custom-call | flops 28185722880 | bytes 14680064 | tf_op jit(solution)/shard_map/planes/pallas_call | solution.py:163
  493.6 129.5 %all-to-all-done.1.in_ref = bf16[32,2,7,64,128]{4,3,2,1,0:T(8,128)(2,1)} async-done(((bf16[32,2,7,64,128]{4,3,2,1,0:T(8,128)(2,1)}), bf16[32,2,7,64,128]{4,3,2,1,0:T(8,128)(2,1)}, u32[]{:S(2)}, u32[]{:S(2)}) %all-to-all-start.1) | async-done | bytes 7340064 | tf_op jit(solution)/shard_map/all_to_all | solution.py:346
  623.2 5.7 all-to-all-start.3
  628.9 21.4 %planes.5 = bf16[32,2,4,64,128]{4,3,2,1,0:T(8,128)(2,1)} custom-call(f32[4]{0:T(128)} %bitcast.1, bf16[512,768]{1,0:T(8,128)(2,1)} %constant.68.clone.refs_1_, bf16[768,512]{1,0:T(8,128)(2,1)} %constant.66.clone.refs_2_, bf16[512,768]{1,0:T(8,128)(2,1)} %constant.67.clone.refs_3_, bf16[768,512]{1,0:T(8,128)(2,1)} %constant.69.clone.refs_4_, ...), custom_call_target="tpu_custom_call" | custom-call | flops 16106127360 | bytes 8388608 | tf_op jit(solution)/shard_map/planes/pallas_call | solution.py:163
  650.2 0.0 copy-start
  650.2 143.5 %all-to-all-done.3.in_ref = bf16[32,2,7,64,128]{4,3,2,1,0:T(8,128)(2,1)} async-done(((bf16[32,2,7,64,128]{4,3,2,1,0:T(8,128)(2,1)}), bf16[32,2,7,64,128]{4,3,2,1,0:T(8,128)(2,1)}, u32[]{:S(2)}, u32[]{:S(2)}) %all-to-all-start.3) | async-done | bytes 7340064 | tf_op jit(solution)/shard_map/all_to_all | solution.py:346
  793.7 5.9 all-to-all-start.5
  799.6 0.0 copy-done
  799.6 0.6 broadcast_in_dim.4.eig_val_ref
  800.2 0.1 copy.19
  800.3 0.6 mul.48.wave_y_ref
  801.0 0.5 multiply_multiply_fusion.wave_x_ref
  801.5 19.2 %gather.2 = (f32[64,128,384]{2,1,0:T(8,128)}, f32[64,128,384]{2,1,0:T(8,128)}) custom-call(bf16[224,384]{1,0:T(8,128)(2,1)} %constant.73.clone.proj_ref, bf16[64,128,384]{2,1,0:T(8,128)(2,1)} %buoy_ref.7, bf16[64,128,384]{2,1,0:T(8,128)(2,1)} %vel_ref.7, bf16[32,2,7,64,128]{4,3,2,1,0:T(8,128)(2,1)} %all-to-all-done.1.in_ref), custom_call_target="tpu_custom_call" | custom-call | flops 2818572288 | bytes 51380224 | tf_op jit(solution)/shard_map/gather/pallas_call | solution.py:219
  820.7 21.2 %gather.3 = (f32[64,128,384]{2,1,0:T(8,128)}, f32[64,128,384]{2,1,0:T(8,128)}) custom-call(bf16[224,384]{1,0:T(8,128)(2,1)} %constant.74.clone.proj_ref, f32[64,128,384]{2,1,0:T(8,128)} %get-tuple-element.6.buoy_ref, f32[64,128,384]{2,1,0:T(8,128)} %get-tuple-element.7.vel_ref, bf16[32,2,7,64,128]{4,3,2,1,0:T(8,128)(2,1)} %all-to-all-done.3.in_ref), custom_call_target="tpu_custom_call" | custom-call | flops 2818572288 | bytes 51380224 | tf_op jit(solution)/shard_map/gather/pallas_call | solution.py:219
  841.9 51.9 %all-to-all-done.5.in_ref = bf16[32,2,4,64,128]{4,3,2,1,0:T(8,128)(2,1)} async-done(((bf16[32,2,4,64,128]{4,3,2,1,0:T(8,128)(2,1)}), bf16[32,2,4,64,128]{4,3,2,1,0:T(8,128)(2,1)}, u32[]{:S(2)}, u32[]{:S(2)}) %all-to-all-start.5) | async-done | bytes 4194336 | tf_op jit(solution)/shard_map/all_to_all | solution.py:346
  893.8 29.0 %finish.1 = (bf16[64,128,384]{2,1,0:T(8,128)(2,1)}, bf16[64,128,384]{2,1,0:T(8,128)(2,1)}) custom-call(f32[64]{0:T(128)} %multiply_multiply_fusion.wave_x_ref, f32[128,1]{1,0:T(8,128)} %mul.48.wave_y_ref, f32[1,384]{1,0:T(1,128)} %broadcast_in_dim.4.eig_val_ref, bf16[384,384]{1,0:T(8,128)(2,1)} %left_ref.1, bf16[384,384]{1,0:T(8,128)(2,1)} %right_ref.1, ...), custom_call_target="tpu_custom_call" | custom-call | flops 11274289152 | bytes 41943040 | tf_op jit(solution)/shard_map/finish/pallas_call | solution.py:283
  (1 shorter events, 0.0 us)
Async XLA Ops:
  9.8 101.8 %all-to-all-start.4 = ((bf16[32,2,4,64,128]{4,3,2,1,0:T(8,128)(2,1)}), bf16[32,2,4,64,128]{4,3,2,1,0:T(8,128)(2,1)}, u32[]{:S(2)}, u32[]{:S(2)}) async-start(bf16[32,2,4,64,128]{4,3,2,1,0:T(8,128)(2,1)} %lift.5), calls=%async_computation.4 | async-start | bytes 8388608 | tf_op jit(solution)/shard_map/all_to_all | solution.py:346
  111.5 170.7 %all-to-all-start = ((bf16[32,2,7,64,128]{4,3,2,1,0:T(8,128)(2,1)}), bf16[32,2,7,64,128]{4,3,2,1,0:T(8,128)(2,1)}, u32[]{:S(2)}, u32[]{:S(2)}) async-start(bf16[32,2,7,64,128]{4,3,2,1,0:T(8,128)(2,1)} %lift.3), calls=%async_computation | async-start | bytes 14680064 | tf_op jit(solution)/shard_map/all_to_all | solution.py:346
  128.2 159.7 %copy-start.2 = (f32[144]{0:T(256)S(1)}, f32[144]{0:T(256)}, u32[]{:S(2)}) copy-start(f32[144]{0:T(256)} %param.18) | copy-start | bytes 1732
  282.2 170.5 %all-to-all-start.2 = ((bf16[32,2,7,64,128]{4,3,2,1,0:T(8,128)(2,1)}), bf16[32,2,7,64,128]{4,3,2,1,0:T(8,128)(2,1)}, u32[]{:S(2)}, u32[]{:S(2)}) async-start(bf16[32,2,7,64,128]{4,3,2,1,0:T(8,128)(2,1)} %lift.4), calls=%async_computation.2 | async-start | bytes 14680064 | tf_op jit(solution)/shard_map/all_to_all | solution.py:346
  288.0 35.7 %copy-start.1 = (f32[18]{0:T(128)}, f32[18]{0:T(128)S(1)}, u32[]{:S(2)}) copy-start(f32[18]{0:T(128)S(1)} %dynamic_slice.3) | copy-start | bytes 220
  452.7 170.4 %all-to-all-start.1 = ((bf16[32,2,7,64,128]{4,3,2,1,0:T(8,128)(2,1)}), bf16[32,2,7,64,128]{4,3,2,1,0:T(8,128)(2,1)}, u32[]{:S(2)}, u32[]{:S(2)}) async-start(bf16[32,2,7,64,128]{4,3,2,1,0:T(8,128)(2,1)} %planes.3.refs_6_), calls=%async_computation.1 | async-start | bytes 14680064 | tf_op jit(solution)/shard_map/all_to_all | solution.py:346
  623.2 170.6 %all-to-all-start.3 = ((bf16[32,2,7,64,128]{4,3,2,1,0:T(8,128)(2,1)}), bf16[32,2,7,64,128]{4,3,2,1,0:T(8,128)(2,1)}, u32[]{:S(2)}, u32[]{:S(2)}) async-start(bf16[32,2,7,64,128]{4,3,2,1,0:T(8,128)(2,1)} %planes.4.refs_6_), calls=%async_computation.3 | async-start | bytes 14680064 | tf_op jit(solution)/shard_map/all_to_all | solution.py:346
  650.2 149.4 %copy-start = (f32[384]{0:T(512)S(1)}, f32[384]{0:T(512)}, u32[]{:S(2)}) copy-start(f32[384]{0:T(512)} %param.19) | copy-start | bytes 4612
  793.7 100.0 %all-to-all-start.5 = ((bf16[32,2,4,64,128]{4,3,2,1,0:T(8,128)(2,1)}), bf16[32,2,4,64,128]{4,3,2,1,0:T(8,128)(2,1)}, u32[]{:S(2)}, u32[]{:S(2)}) async-start(bf16[32,2,4,64,128]{4,3,2,1,0:T(8,128)(2,1)} %planes.5), calls=%async_computation.5 | async-start | bytes 8388608 | tf_op jit(solution)/shard_map/all_to_all | solution.py:346

commit v4 on v3

--- a/solution.py
+++ b/solution.py
@@ -86,7 +86,7 @@
         values = jnp.einsum("fzn,fakn->fzak", table, fields, preferred_element_type=F32)
         values = values.astype(BF16).reshape(2, blocks, depth, modes_x, modes_y)
         return jnp.transpose(values, (1, 0, 2, 3, 4))
-    span = 16
+    span = 8
     return pl.pallas_call(
         lift_kernel,
         grid=(modes_x // span,),
@@ -183,12 +183,13 @@
 
 
 def solve_modal(modal_buoy, modal_vel, wave, eig_val):
-    lapl = wave + eig_val
-    diag_buoy = 1.0 + diffuse_buoy * lapl
-    diag_vel = 1.0 + diffuse_vel * lapl
+    diag_buoy = (1.0 + diffuse_buoy * wave) + diffuse_buoy * eig_val
+    diag_vel = (1.0 + diffuse_vel * wave) + diffuse_vel * eig_val
     scale = 1.0 / (diag_buoy * diag_vel + couple_buoy * couple_vel)
-    solved_buoy = ((diag_vel * modal_buoy - couple_buoy * modal_vel) * scale).astype(BF16)
-    solved_vel = ((diag_buoy * modal_vel + couple_vel * modal_buoy) * scale).astype(BF16)
+    modal_buoy = modal_buoy * scale
+    modal_vel = modal_vel * scale
+    solved_buoy = (diag_vel * modal_buoy - couple_buoy * modal_vel).astype(BF16)
+    solved_vel = (diag_buoy * modal_vel + couple_vel * modal_buoy).astype(BF16)
     return (solved_buoy, solved_vel)
 
 
@@ -200,20 +201,24 @@
     return jnp.dot(jnp.concatenate(rows, axis=0), proj_ref[...], preferred_element_type=F32)
 
 
-def gather_kernel(proj_ref, buoy_ref, vel_ref, in_ref, *out_refs):
+def gather_kernel(proj_ref, left_ref, buoy_ref, vel_ref, in_ref, *out_refs):
     span, lanes, degree = buoy_ref.shape
     for field, (coeff_ref, out_ref) in enumerate(zip((buoy_ref, vel_ref), out_refs)):
         tend = explicit_step * project(in_ref, field, proj_ref)
-        out_ref[...] = coeff_ref[...].astype(F32) + tend.reshape(span, lanes, degree)
-
-
-def gather(kernels, folded, proj, rhs):
-    modes_x, modes_y, degree = rhs[0].shape
-    blocks, fields, depth = folded.shape[:3]
+        rhs = coeff_ref[...].reshape(span * lanes, degree).astype(F32) + tend
+        modal = jnp.dot(rhs.astype(BF16), left_ref[...], preferred_element_type=F32)
+        out_ref[...] = modal.reshape(span, lanes, degree)
+
+
+def gather(kernels, folded, proj, eig_left, fields):
+    modes_x, modes_y, degree = fields[0].shape
+    blocks, count, depth = folded.shape[:3]
     if not kernels:
         parts = jnp.transpose(folded, (1, 0, 2, 3, 4)).reshape(2, -1, modes_x, modes_y)
         tend = jnp.einsum("fzak,zn->fakn", parts, proj, preferred_element_type=F32)
-        return [part.astype(F32) + explicit_step * tend[f] for f, part in enumerate(rhs)]
+        rhs = jnp.stack(fields).astype(F32) + explicit_step * tend
+        modal = jnp.einsum("fakn,nj->fakj", rhs.astype(BF16), eig_left, preferred_element_type=F32)
+        return [modal[0], modal[1]]
     span = 8
     block = pl.BlockSpec((span, modes_y, degree), lambda a: (a, 0, 0))
     return pl.pallas_call(
@@ -221,40 +226,31 @@
         grid=(modes_x // span,),
         in_specs=[
             whole(proj.shape),
-            block,
-            block,
-            pl.BlockSpec((blocks, fields, depth, span, modes_y), lambda a: (0, 0, 0, a, 0)),
+            whole(eig_left.shape),
+            block,
+            block,
+            pl.BlockSpec((blocks, count, depth, span, modes_y), lambda a: (0, 0, 0, a, 0)),
         ],
         out_specs=[block, block],
-        out_shape=[jax.ShapeDtypeStruct(rhs[0].shape, F32)] * 2,
+        out_shape=[jax.ShapeDtypeStruct(fields[0].shape, F32)] * 2,
         compiler_params=params(1),
         cost_estimate=pl.CostEstimate(
-            flops=4 * rhs[0].size * proj.shape[0],
-            bytes_accessed=2 * folded.size + 14 * rhs[0].size,
+            flops=4 * fields[0].size * (proj.shape[0] + degree),
+            bytes_accessed=2 * folded.size + 12 * fields[0].size,
             transcendentals=0,
         ),
         name="gather",
-    )(proj, *rhs, folded)
+    )(proj, eig_left, *fields, folded)
 
 
 def finish_kernel(
-    wave_x_ref,
-    wave_y_ref,
-    eig_val_ref,
-    left_ref,
-    right_ref,
-    proj_ref,
-    buoy_ref,
-    vel_ref,
-    in_ref,
-    *out_refs,
+    wave_x_ref, wave_y_ref, eig_val_ref, right_ref, proj_ref, buoy_ref, vel_ref, in_ref, *out_refs
 ):
     span, lanes, degree = buoy_ref.shape
     modal = []
-    for field, rhs_ref in enumerate((buoy_ref, vel_ref)):
-        tend = explicit_step * project(in_ref, field, proj_ref)
-        rhs = rhs_ref[...].reshape(span * lanes, degree).astype(F32) + tend
-        modal.append(jnp.dot(rhs.astype(BF16), left_ref[...], preferred_element_type=F32))
+    for field, part_ref in enumerate((buoy_ref, vel_ref)):
+        part = part_ref[...].reshape(span * lanes, degree)
+        modal.append(part + project(in_ref, field, proj_ref))
     first = pl.program_id(0) * span
     waves = [4.0 * (wave_x_ref[first + mode] + wave_y_ref[...]) for mode in range(span)]
     solved = solve_modal(modal[0], modal[1], jnp.concatenate(waves, axis=0), eig_val_ref[...])
@@ -263,15 +259,13 @@
         out_ref[...] = result.reshape(span, lanes, degree)
 
 
-def finish(kernels, folded, proj, rhs, eig_val, eig_left, eig_right, wave_x, wave_y):
-    modes_x, modes_y, degree = rhs[0].shape
+def finish(kernels, folded, proj, modal, eig_val, eig_right, wave_x, wave_y):
+    modes_x, modes_y, degree = modal[0].shape
     if not kernels:
-        modal = []
-        for part in gather(kernels, folded, proj, rhs):
-            part = part.astype(BF16)
-            modal.append(jnp.einsum("akn,nj->akj", part, eig_left, preferred_element_type=F32))
+        parts = jnp.transpose(folded, (1, 0, 2, 3, 4)).reshape(2, -1, modes_x, modes_y)
+        last = jnp.einsum("fzak,zn->fakn", parts, proj, preferred_element_type=F32)
         wave = 4.0 * (wave_x[:, None, None] + wave_y[None, :, None])
-        solved = solve_modal(modal[0], modal[1], wave, eig_val)
+        solved = solve_modal(modal[0] + last[0], modal[1] + last[1], wave, eig_val)
         return tuple(
             jnp.einsum("akj,jn->akn", values, eig_right, preferred_element_type=F32).astype(BF16)
             for values in solved
@@ -279,7 +273,7 @@
     span = 8
     blocks, fields, depth = folded.shape[:3]
     block = pl.BlockSpec((span, modes_y, degree), lambda a: (a, 0, 0))
-    result = jax.ShapeDtypeStruct(rhs[0].shape, BF16)
+    result = jax.ShapeDtypeStruct(modal[0].shape, BF16)
     return pl.pallas_call(
         finish_kernel,
         grid=(modes_x // span,),
@@ -287,7 +281,6 @@
             pl.BlockSpec(memory_space=pltpu.SMEM),
             whole((modes_y, 1)),
             whole((1, degree)),
-            whole(eig_left.shape),
             whole(eig_right.shape),
             whole(proj.shape),
             block,
@@ -298,27 +291,17 @@
         out_shape=[result, result],
         compiler_params=params(1),
         cost_estimate=pl.CostEstimate(
-            flops=4 * rhs[0].size * (proj.shape[0] + 2 * degree),
-            bytes_accessed=12 * rhs[0].size + 2 * folded.size,
-            transcendentals=rhs[0].size,
+            flops=4 * modal[0].size * (proj.shape[0] + degree),
+            bytes_accessed=12 * modal[0].size + 2 * folded.size,
+            transcendentals=modal[0].size,
         ),
         name="finish",
-    )(
-        wave_x,
-        wave_y[:, None],
-        eig_val[None, :],
-        eig_left,
-        eig_right,
-        proj,
-        *rhs,
-        folded,
-    )
+    )(wave_x, wave_y[:, None], eig_val[None, :], eig_right, proj, *modal, folded)
 
 
 def chunk_sizes(own):
-    first = min(own, max(1, own * 4 // 18))
-    second = (own - first) // 2
-    return [size for size in (first, second, own - first - second) if size]
+    second = -(-own * 4 // 18)
+    return [size for size in (own - second, second) if size]
 
 
 def per_device(buoy, vel_w, strat, eig_val, eig_left, eig_right):
@@ -361,13 +344,11 @@
     for start, stop in pieces:
         table = forward_z[:, :, start:stop].reshape(2, blocks * (stop - start), degree)
         arrived.append(exchange(lift(kernels, vel_w, buoy, jnp.asarray(table), blocks)))
-    order = list(range(1, len(pieces))) + [0]
     folded, after = [], []
-    for piece in order:
-        start, stop = pieces[piece]
+    for values, (start, stop) in zip(arrived, pieces):
         fluxes = planes(
             kernels,
-            arrived[piece],
+            values,
             strat_own[start:stop],
             along_y,
             along_x,
@@ -380,16 +361,20 @@
         folded.append(exchange(fluxes))
     projs = [
         jnp.asarray(backward_z[:, start:stop].reshape(blocks * (stop - start), degree))
-        for start, stop in (pieces[piece] for piece in order)
+        for start, stop in pieces
     ]
-    rhs = [buoy, vel_w]
-    for part, proj in zip(folded[:-1], projs[:-1]):
-        rhs = gather(kernels, part, proj, rhs)
+    if len(pieces) > 1:
+        modal = gather(kernels, folded[0], projs[0], eig_left, [buoy, vel_w])
+    else:
+        modal = [
+            jnp.einsum("akn,nj->akj", part, eig_left, preferred_element_type=F32)
+            for part in (buoy, vel_w)
+        ]
+    last = jnp.dot(projs[-1], eig_left, preferred_element_type=F32)
+    last = (explicit_step * last).astype(BF16)
     wave_x = wave_squares(total_x, row * modes_x, modes_x)
     wave_y = wave_squares(total_y, col * modes_y, modes_y)
-    return finish(
-        kernels, folded[-1], projs[-1], rhs, eig_val, eig_left, eig_right, wave_x, wave_y
-    )
+    return finish(kernels, folded[-1], last, modal, eig_val, eig_right, wave_x, wave_y)
 
 
 def solution(mesh):

time: 923 us -> 916 us (level)
  waiting for transfers between devices: 691 us -> 728 us
  Pallas kernels: 192 us -> 162 us
  starting transfers between devices: 36.3 us -> 20.4 us
    all_to_all x6 -> x4, waiting for transfers between devices: 691 us -> 728 us  [exchange(): lax.all_to_all(values, ('row', 'col'), split_axis=0, concat_axis=0, tiled...]
    all_to_all x6 -> x4, starting transfers between devices: 36.3 us -> 20.4 us  [exchange(): lax.all_to_all(values, ('row', 'col'), split_axis=0, concat_axis=0, tiled...]
    pallas_call x2 -> x1, Pallas kernels: 40.4 us -> 24.5 us  [gather(): pl.pallas_call(gather_kernel, grid=(modes_x // span,), in_specs=[whole(pr...]
    pallas_call x3 -> x2, Pallas kernels: 30.8 us -> 27.5 us  [lift(): pl.pallas_call(lift_kernel, grid=(modes_x // span,), in_specs=[pl.BlockSp...]
    pallas_call x3 -> x2, Pallas kernels: 91.6 us -> 88.3 us  [planes(): pl.pallas_call(lambda *refs: plane_kernel(col_count, *refs), grid=(depth,...]
  transfers between devices with their start and end apart: 6 -> 4, of which waited for: 6 -> 4; matrix products, arithmetic and copies ran while one was open for 0% -> 0% of each run, Pallas kernels for 17% -> 13%
where the time goes in v4:
time: 916 us
  waiting for transfers between devices  728 us (79%)
  Pallas kernels  162 us (18%)
  starting transfers between devices  20.4 us (2%)
    all_to_all x4, waiting for transfers between devices, exchange(): lax.all_to_all(values, ('row', 'col'), split_axis=0, concat_axis=0, tiled...  728 us
    pallas_call x2, Pallas kernels, planes(): pl.pallas_call(lambda *refs: plane_kernel(col_count, *refs), grid=(depth,...  88.3 us
    pallas_call x2, Pallas kernels, lift(): pl.pallas_call(lift_kernel, grid=(modes_x // span,), in_specs=[pl.BlockSp...  27.5 us
    pallas_call x1, Pallas kernels, gather(): pl.pallas_call(gather_kernel, grid=(modes_x // span,), in_specs=[whole(pr...  24.5 us
    pallas_call x1, Pallas kernels, finish(): pl.pallas_call(finish_kernel, grid=(modes_x // span,), in_specs=[pl.Block...  22.2 us
    all_to_all x4, starting transfers between devices, exchange(): lax.all_to_all(values, ('row', 'col'), split_axis=0, concat_axis=0, tiled...  20.4 us
  transfers between devices with their start and end apart: 4, of which 4 were waited for; matrix products, arithmetic and copies ran while one was open for 0% of the time, Pallas kernels for 13%

profile of v4, /device:TPU:0, one launch (start us, length us, event | category | flops | bytes accessed | tf_op | source)
XLA Modules:
  0.0 915.5 jit_solution(987076850198815243)
XLA Ops:
  0.6 16.8 %lift.2 = bf16[32,2,14,64,128]{4,3,2,1,0:T(8,128)(2,1)} custom-call(bf16[64,128,384]{2,1,0:T(8,128)(2,1)} %vel_ref.5, bf16[64,128,384]{2,1,0:T(8,128)(2,1)} %buoy_ref.5, bf16[2,448,384]{2,1,0:T(8,128)(2,1)} %constant.68.clone.table_ref), custom_call_target="tpu_custom_call" | custom-call | flops 5637144576 | bytes 27262976 | tf_op jit(solution)/shard_map/lift/pallas_call | solution.py:90
  17.4 7.4 all-to-all-start
  24.8 10.7 %lift.3 = bf16[32,2,4,64,128]{4,3,2,1,0:T(8,128)(2,1)} custom-call(bf16[64,128,384]{2,1,0:T(8,128)(2,1)} %vel_ref.5, bf16[64,128,384]{2,1,0:T(8,128)(2,1)} %buoy_ref.5, bf16[2,128,384]{2,1,0:T(8,128)(2,1)} %constant.69.clone.table_ref), custom_call_target="tpu_custom_call" | custom-call | flops 1610612736 | bytes 16777216 | tf_op jit(solution)/shard_map/lift/pallas_call | solution.py:90
  35.5 0.0 copy-start.3
  35.5 322.7 %all-to-all-done.refs_5_ = bf16[32,2,14,64,128]{4,3,2,1,0:T(8,128)(2,1)} async-done(((bf16[32,2,14,64,128]{4,3,2,1,0:T(8,128)(2,1)}), bf16[32,2,14,64,128]{4,3,2,1,0:T(8,128)(2,1)}, u32[]{:S(2)}, u32[]{:S(2)}) %all-to-all-start) | async-done | bytes 14680096 | tf_op jit(solution)/shard_map/all_to_all | solution.py:329
  358.3 3.6 all-to-all-start.2
  361.8 0.0 copy-done.3
  361.9 0.6 dynamic_slice.3
  362.4 67.0 %planes.2.refs_6_ = bf16[32,2,14,64,128]{4,3,2,1,0:T(8,128)(2,1)} custom-call(f32[14]{0:T(128)} %bitcast.3, bf16[512,768]{1,0:T(8,128)(2,1)} %constant.66.clone.refs_1_, bf16[768,512]{1,0:T(8,128)(2,1)} %constant.64.clone.refs_2_, bf16[512,768]{1,0:T(8,128)(2,1)} %constant.65.clone.refs_3_, bf16[768,512]{1,0:T(8,128)(2,1)} %constant.67.clone.refs_4_, ...), custom_call_target="tpu_custom_call" | custom-call | flops 56371445760 | bytes 29360128 | tf_op jit(solution)/shard_map/planes/pallas_call | solution.py:163
  429.4 0.0 copy-start.4
  429.4 26.8 %all-to-all-done.2.refs_5_ = bf16[32,2,4,64,128]{4,3,2,1,0:T(8,128)(2,1)} async-done(((bf16[32,2,4,64,128]{4,3,2,1,0:T(8,128)(2,1)}), bf16[32,2,4,64,128]{4,3,2,1,0:T(8,128)(2,1)}, u32[]{:S(2)}, u32[]{:S(2)}) %all-to-all-start.2) | async-done | bytes 4194336 | tf_op jit(solution)/shard_map/all_to_all | solution.py:329
  456.3 5.6 all-to-all-start.1
  461.9 0.0 copy-done.4
  461.9 0.6 slice.7.refs_0_
  462.5 21.3 %planes.3 = bf16[32,2,4,64,128]{4,3,2,1,0:T(8,128)(2,1)} custom-call(f32[4]{0:T(128)} %slice.7.refs_0_, bf16[512,768]{1,0:T(8,128)(2,1)} %constant.66.clone.refs_1_, bf16[768,512]{1,0:T(8,128)(2,1)} %constant.64.clone.refs_2_, bf16[512,768]{1,0:T(8,128)(2,1)} %constant.65.clone.refs_3_, bf16[768,512]{1,0:T(8,128)(2,1)} %constant.67.clone.refs_4_, ...), custom_call_target="tpu_custom_call" | custom-call | flops 16106127360 | bytes 8388608 | tf_op jit(solution)/shard_map/planes/pallas_call | solution.py:163
  483.8 0.0 copy-start.2
  483.8 0.0 copy-start
  483.8 0.0 copy-start.1
  483.8 311.5 %all-to-all-done.1.in_ref = bf16[32,2,14,64,128]{4,3,2,1,0:T(8,128)(2,1)} async-done(((bf16[32,2,14,64,128]{4,3,2,1,0:T(8,128)(2,1)}), bf16[32,2,14,64,128]{4,3,2,1,0:T(8,128)(2,1)}, u32[]{:S(2)}, u32[]{:S(2)}) %all-to-all-start.1) | async-done | bytes 14680096 | tf_op jit(solution)/shard_map/all_to_all | solution.py:329
  795.3 3.8 all-to-all-start.3
  799.1 0.1 copy.17
  799.2 0.6 mul.54.wave_y_ref
  799.8 0.0 copy-done.2
  799.9 0.5 broadcast_in_dim.4.eig_val_ref
  800.4 0.5 multiply_multiply_fusion.wave_x_ref
  800.9 0.0 copy-done
  800.9 0.0 copy-done.1
  800.9 0.8 fusion.proj_ref
  801.8 24.5 %gather.1 = (f32[64,128,384]{2,1,0:T(8,128)}, f32[64,128,384]{2,1,0:T(8,128)}) custom-call(bf16[448,384]{1,0:T(8,128)(2,1)} %constant.70.clone.proj_ref, bf16[384,384]{1,0:T(8,128)(2,1)} %left_ref.1, bf16[64,128,384]{2,1,0:T(8,128)(2,1)} %buoy_ref.5, bf16[64,128,384]{2,1,0:T(8,128)(2,1)} %vel_ref.5, bf16[32,2,14,64,128]{4,3,2,1,0:T(8,128)(2,1)} %all-to-all-done.1.in_ref), custom_call_target="tpu_custom_call" | custom-call | flops 10468982784 | bytes 52428800 | tf_op jit(solution)/shard_map/gather/pallas_call | solution.py:224
  826.3 67.1 %all-to-all-done.3.in_ref = bf16[32,2,4,64,128]{4,3,2,1,0:T(8,128)(2,1)} async-done(((bf16[32,2,4,64,128]{4,3,2,1,0:T(8,128)(2,1)}), bf16[32,2,4,64,128]{4,3,2,1,0:T(8,128)(2,1)}, u32[]{:S(2)}, u32[]{:S(2)}) %all-to-all-start.3) | async-done | bytes 4194336 | tf_op jit(solution)/shard_map/all_to_all | solution.py:329
  893.3 22.2 %finish.1 = (bf16[64,128,384]{2,1,0:T(8,128)(2,1)}, bf16[64,128,384]{2,1,0:T(8,128)(2,1)}) custom-call(f32[64]{0:T(128)} %multiply_multiply_fusion.wave_x_ref, f32[128,1]{1,0:T(8,128)} %mul.54.wave_y_ref, f32[1,384]{1,0:T(1,128)} %broadcast_in_dim.4.eig_val_ref, bf16[384,384]{1,0:T(8,128)(2,1)} %right_ref.1, bf16[128,384]{1,0:T(8,128)(2,1)} %fusion.proj_ref, ...), custom_call_target="tpu_custom_call" | custom-call | flops 6442450944 | bytes 41943040 | tf_op jit(solution)/shard_map/finish/pallas_call | solution.py:277
  (1 shorter events, 0.0 us)
Async XLA Ops:
  17.4 340.8 %all-to-all-start = ((bf16[32,2,14,64,128]{4,3,2,1,0:T(8,128)(2,1)}), bf16[32,2,14,64,128]{4,3,2,1,0:T(8,128)(2,1)}, u32[]{:S(2)}, u32[]{:S(2)}) async-start(bf16[32,2,14,64,128]{4,3,2,1,0:T(8,128)(2,1)} %lift.2), calls=%async_computation | async-start | bytes 29360128 | tf_op jit(solution)/shard_map/all_to_all | solution.py:329
  35.5 326.3 %copy-start.3 = (f32[144]{0:T(256)S(1)}, f32[144]{0:T(256)}, u32[]{:S(2)}) copy-start(f32[144]{0:T(256)} %param.16) | copy-start | bytes 1732
  358.3 98.0 %all-to-all-start.2 = ((bf16[32,2,4,64,128]{4,3,2,1,0:T(8,128)(2,1)}), bf16[32,2,4,64,128]{4,3,2,1,0:T(8,128)(2,1)}, u32[]{:S(2)}, u32[]{:S(2)}) async-start(bf16[32,2,4,64,128]{4,3,2,1,0:T(8,128)(2,1)} %lift.3), calls=%async_computation.2 | async-start | bytes 8388608 | tf_op jit(solution)/shard_map/all_to_all | solution.py:329
  429.4 32.5 %copy-start.4 = (f32[18]{0:T(128)S(1)}, f32[18]{0:T(128)}, u32[]{:S(2)}) copy-start(f32[18]{0:T(128)} %dynamic_slice.3) | copy-start | bytes 220
  456.3 339.0 %all-to-all-start.1 = ((bf16[32,2,14,64,128]{4,3,2,1,0:T(8,128)(2,1)}), bf16[32,2,14,64,128]{4,3,2,1,0:T(8,128)(2,1)}, u32[]{:S(2)}, u32[]{:S(2)}) async-start(bf16[32,2,14,64,128]{4,3,2,1,0:T(8,128)(2,1)} %planes.2.refs_6_), calls=%async_computation.1 | async-start | bytes 29360128 | tf_op jit(solution)/shard_map/all_to_all | solution.py:329
  483.8 316.0 %copy-start.2 = (f32[384]{0:T(512)S(1)}, f32[384]{0:T(512)}, u32[]{:S(2)}) copy-start(f32[384]{0:T(512)} %param.17) | copy-start | bytes 4612
  483.8 317.1 %copy-start = (bf16[384,384]{1,0:T(8,128)(2,1)S(1)}, bf16[384,384]{1,0:T(8,128)(2,1)}, u32[]{:S(2)}) copy-start(bf16[384,384]{1,0:T(8,128)(2,1)} %left_ref.1) | copy-start | bytes 884740
  483.8 317.1 %copy-start.1 = (bf16[128,384]{1,0:T(8,128)(2,1)S(1)}, bf16[128,384]{1,0:T(8,128)(2,1)}, u32[]{:S(2)}) copy-start(bf16[128,384]{1,0:T(8,128)(2,1)} %constant.71.clone) | copy-start | bytes 294916
  795.3 98.0 %all-to-all-start.3 = ((bf16[32,2,4,64,128]{4,3,2,1,0:T(8,128)(2,1)}), bf16[32,2,4,64,128]{4,3,2,1,0:T(8,128)(2,1)}, u32[]{:S(2)}, u32[]{:S(2)}) async-start(bf16[32,2,4,64,128]{4,3,2,1,0:T(8,128)(2,1)} %planes.3), calls=%async_computation.3 | async-start | bytes 8388608 | tf_op jit(solution)/shard_map/all_to_all | solution.py:329

commit v5 on v4

--- a/solution.py
+++ b/solution.py
@@ -118,7 +118,7 @@
         for field in range(2):
             rows = []
             for row in range(row_count):
-                parts = [in_ref[row * col_count + col, field, level] for col in range(col_count)]
+                parts = [in_ref[col * row_count + row, field, level] for col in range(col_count)]
                 rows.append(jnp.concatenate(parts, axis=1))
             middle = jnp.dot(
                 jnp.concatenate(rows, axis=0), along_y_ref[...], preferred_element_type=F32
@@ -134,7 +134,7 @@
             values = jnp.dot(folded, back_y_ref[...], preferred_element_type=F32).astype(BF16)
             for row in range(row_count):
                 for col in range(col_count):
-                    out_ref[row * col_count + col, field, level] = values[
+                    out_ref[col * row_count + row, field, level] = values[
                         row * modes_x : (row + 1) * modes_x, col * lanes : (col + 1) * lanes
                     ]
 
@@ -143,8 +143,8 @@
     blocks, fields, depth, modes_x, modes_y = arrived.shape
     row_count = blocks // col_count
     if not kernels:
-        parts = arrived.reshape(row_count, col_count, fields, depth, modes_x, modes_y)
-        parts = jnp.transpose(parts, (2, 3, 0, 4, 1, 5))
+        parts = arrived.reshape(col_count, row_count, fields, depth, modes_x, modes_y)
+        parts = jnp.transpose(parts, (2, 3, 1, 4, 0, 5))
         parts = parts.reshape(fields, depth, row_count * modes_x, col_count * modes_y)
         middle = jnp.einsum("fzak,ky->fzay", parts, along_y, preferred_element_type=F32)
         grids = jnp.einsum("xa,fzay->fzxy", along_x, middle.astype(BF16), preferred_element_type=F32)
@@ -157,7 +157,7 @@
         values = values.astype(BF16).reshape(
             fields, depth, row_count, modes_x, col_count, modes_y
         )
-        return jnp.transpose(values, (2, 4, 0, 1, 3, 5)).reshape(arrived.shape)
+        return jnp.transpose(values, (4, 2, 0, 1, 3, 5)).reshape(arrived.shape)
     block = pl.BlockSpec((blocks, fields, 1, modes_x, modes_y), lambda z: (0, 0, z, 0, 0))
     work = along_y.size * along_x.shape[1] + along_x.size * along_y.shape[1]
     return pl.pallas_call(
@@ -193,18 +193,20 @@
     return (solved_buoy, solved_vel)
 
 
-def project(ref, field, proj_ref):
-    blocks, _, depth, span, lanes = ref.shape
-    fluxes = ref[:, field].reshape(blocks * depth, span, lanes).astype(F32)
+def project(refs, field, proj_ref):
+    blocks, _, _, span, lanes = refs[0].shape
+    parts = [ref[:, field].reshape(blocks * ref.shape[2], span, lanes) for ref in refs]
+    fluxes = jnp.concatenate(parts, axis=0).astype(F32)
     fluxes = jnp.swapaxes(fluxes, 0, 1).astype(BF16)
     rows = [jnp.transpose(fluxes[mode]) for mode in range(span)]
     return jnp.dot(jnp.concatenate(rows, axis=0), proj_ref[...], preferred_element_type=F32)
 
 
-def gather_kernel(proj_ref, left_ref, buoy_ref, vel_ref, in_ref, *out_refs):
+def gather_kernel(proj_ref, left_ref, buoy_ref, vel_ref, *refs):
+    in_refs, out_refs = refs[:-2], refs[-2:]
     span, lanes, degree = buoy_ref.shape
     for field, (coeff_ref, out_ref) in enumerate(zip((buoy_ref, vel_ref), out_refs)):
-        tend = explicit_step * project(in_ref, field, proj_ref)
+        tend = explicit_step * project(in_refs, field, proj_ref)
         rhs = coeff_ref[...].reshape(span * lanes, degree).astype(F32) + tend
         modal = jnp.dot(rhs.astype(BF16), left_ref[...], preferred_element_type=F32)
         out_ref[...] = modal.reshape(span, lanes, degree)
@@ -212,9 +214,12 @@
 
 def gather(kernels, folded, proj, eig_left, fields):
     modes_x, modes_y, degree = fields[0].shape
-    blocks, count, depth = folded.shape[:3]
     if not kernels:
-        parts = jnp.transpose(folded, (1, 0, 2, 3, 4)).reshape(2, -1, modes_x, modes_y)
+        parts = [
+            jnp.transpose(part, (1, 0, 2, 3, 4)).reshape(2, -1, modes_x, modes_y)
+            for part in folded
+        ]
+        parts = jnp.concatenate(parts, axis=1)
         tend = jnp.einsum("fzak,zn->fakn", parts, proj, preferred_element_type=F32)
         rhs = jnp.stack(fields).astype(F32) + explicit_step * tend
         modal = jnp.einsum("fakn,nj->fakj", rhs.astype(BF16), eig_left, preferred_element_type=F32)
@@ -229,18 +234,21 @@
             whole(eig_left.shape),
             block,
             block,
-            pl.BlockSpec((blocks, count, depth, span, modes_y), lambda a: (0, 0, 0, a, 0)),
+        ]
+        + [
+            pl.BlockSpec((*part.shape[:3], span, modes_y), lambda a: (0, 0, 0, a, 0))
+            for part in folded
         ],
         out_specs=[block, block],
         out_shape=[jax.ShapeDtypeStruct(fields[0].shape, F32)] * 2,
         compiler_params=params(1),
         cost_estimate=pl.CostEstimate(
             flops=4 * fields[0].size * (proj.shape[0] + degree),
-            bytes_accessed=2 * folded.size + 12 * fields[0].size,
+            bytes_accessed=2 * sum(part.size for part in folded) + 12 * fields[0].size,
             transcendentals=0,
         ),
         name="gather",
-    )(proj, eig_left, *fields, folded)
+    )(proj, eig_left, *fields, *folded)
 
 
 def finish_kernel(
@@ -250,7 +258,7 @@
     modal = []
     for field, part_ref in enumerate((buoy_ref, vel_ref)):
         part = part_ref[...].reshape(span * lanes, degree)
-        modal.append(part + project(in_ref, field, proj_ref))
+        modal.append(part + project([in_ref], field, proj_ref))
     first = pl.program_id(0) * span
     waves = [4.0 * (wave_x_ref[first + mode] + wave_y_ref[...]) for mode in range(span)]
     solved = solve_modal(modal[0], modal[1], jnp.concatenate(waves, axis=0), eig_val_ref[...])
@@ -300,8 +308,9 @@
 
 
 def chunk_sizes(own):
-    second = -(-own * 4 // 18)
-    return [size for size in (own - second, second) if size]
+    first = -(-own * 3 // 18)
+    second = (own - first) // 2
+    return [size for size in (first, second, own - first - second) if size]
 
 
 def per_device(buoy, vel_w, strat, eig_val, eig_left, eig_right):
@@ -322,11 +331,10 @@
     def by_device(table):
         table = table.reshape(col_count, shard, degree)
         table = np.pad(table, ((0, 0), (0, padding), (0, 0)))
-        table = table.reshape(col_count, row_count, own, degree)
-        return np.transpose(table, (1, 0, 2, 3)).reshape(blocks, own, degree)
+        return table.reshape(blocks, own, degree)
 
     def exchange(values):
-        return lax.all_to_all(values, ("row", "col"), split_axis=0, concat_axis=0, tiled=True)
+        return lax.all_to_all(values, ("col", "row"), split_axis=0, concat_axis=0, tiled=True)
 
     levels, slopes, projector = cheb_tables(degree, shard * col_count)
     forward_z = np.stack([by_device(levels.T), by_device(slopes.T)])
@@ -344,11 +352,13 @@
     for start, stop in pieces:
         table = forward_z[:, :, start:stop].reshape(2, blocks * (stop - start), degree)
         arrived.append(exchange(lift(kernels, vel_w, buoy, jnp.asarray(table), blocks)))
+    order = list(range(1, len(pieces))) + [0]
     folded, after = [], []
-    for values, (start, stop) in zip(arrived, pieces):
+    for piece in order:
+        start, stop = pieces[piece]
         fluxes = planes(
             kernels,
-            values,
+            arrived[piece],
             strat_own[start:stop],
             along_y,
             along_x,
@@ -360,17 +370,18 @@
         after = [fluxes]
         folded.append(exchange(fluxes))
     projs = [
-        jnp.asarray(backward_z[:, start:stop].reshape(blocks * (stop - start), degree))
-        for start, stop in pieces
+        backward_z[:, start:stop].reshape(blocks * (stop - start), degree)
+        for start, stop in (pieces[piece] for piece in order)
     ]
     if len(pieces) > 1:
-        modal = gather(kernels, folded[0], projs[0], eig_left, [buoy, vel_w])
+        table = jnp.asarray(np.concatenate(projs[:-1], axis=0))
+        modal = gather(kernels, folded[:-1], table, eig_left, [buoy, vel_w])
     else:
         modal = [
             jnp.einsum("akn,nj->akj", part, eig_left, preferred_element_type=F32)
             for part in (buoy, vel_w)
         ]
-    last = jnp.dot(projs[-1], eig_left, preferred_element_type=F32)
+    last = jnp.dot(jnp.asarray(projs[-1]), eig_left, preferred_element_type=F32)
     last = (explicit_step * last).astype(BF16)
     wave_x = wave_squares(total_x, row * modes_x, modes_x)
     wave_y = wave_squares(total_y, col * modes_y, modes_y)

time: 916 us -> 902 us (0.985)
  waiting for transfers between devices: 728 us -> 694 us
  Pallas kernels: 162 us -> 173 us
    all_to_all x4 -> x6, waiting for transfers between devices: 728 us -> 694 us  [exchange(): lax.all_to_all(values, ('col', 'row'), split_axis=0, concat_axis=0, tiled...]
    pallas_call x2 -> x3, Pallas kernels: 27.5 us -> 35.1 us  [lift(): pl.pallas_call(lift_kernel, grid=(modes_x // span,), in_specs=[pl.BlockSp...]
    all_to_all x4 -> x6, starting transfers between devices: 20.4 us -> 24.9 us  [exchange(): lax.all_to_all(values, ('col', 'row'), split_axis=0, concat_axis=0, tiled...]
    pallas_call x2 -> x3, Pallas kernels: 88.3 us -> 91.5 us  [planes(): pl.pallas_call(lambda *refs: plane_kernel(col_count, *refs), grid=(depth,...]
  transfers between devices with their start and end apart: 4 -> 6, of which waited for: 4 -> 6; matrix products, arithmetic and copies ran while one was open for 0% -> 1% of each run, Pallas kernels for 13% -> 16%
where the time goes in v5:
time: 902 us; the launch traced here: 901 us
  waiting for transfers between devices  694 us (77%)
  Pallas kernels  173 us (19%)
  starting transfers between devices  24.9 us (3%)
    all_to_all x6, waiting for transfers between devices, exchange(): lax.all_to_all(values, ('col', 'row'), split_axis=0, concat_axis=0, tiled...  694 us
    pallas_call x3, Pallas kernels, planes(): pl.pallas_call(lambda *refs: plane_kernel(col_count, *refs), grid=(depth,...  91.5 us
    pallas_call x3, Pallas kernels, lift(): pl.pallas_call(lift_kernel, grid=(modes_x // span,), in_specs=[pl.BlockSp...  35.1 us
    pallas_call x1, Pallas kernels, gather(): pl.pallas_call(gather_kernel, grid=(modes_x // span,), in_specs=[whole(pr...  25 us
    all_to_all x6, starting transfers between devices, exchange(): lax.all_to_all(values, ('col', 'row'), split_axis=0, concat_axis=0, tiled...  24.9 us
    pallas_call x1, Pallas kernels, finish(): pl.pallas_call(finish_kernel, grid=(modes_x // span,), in_specs=[pl.Block...  21.7 us
  transfers between devices with their start and end apart: 6, of which 6 were waited for; matrix products, arithmetic and copies ran while one was open for 1% of the time, Pallas kernels for 16%

profile of v5, /device:TPU:0, one launch (start us, length us, event | category | flops | bytes accessed | tf_op | source)
XLA Modules:
  0.0 900.8 jit_solution(4649781725446022966)
XLA Ops:
  0.6 10.3 %lift.5 = bf16[32,2,3,64,128]{4,3,2,1,0:T(8,128)(2,1)} custom-call(bf16[64,128,384]{2,1,0:T(8,128)(2,1)} %vel_ref.7, bf16[64,128,384]{2,1,0:T(8,128)(2,1)} %buoy_ref.7, bf16[2,96,384]{2,1,0:T(8,128)(2,1)} %constant.70.clone.table_ref), custom_call_target="tpu_custom_call" | custom-call | flops 1207959552 | bytes 15728640 | tf_op jit(solution)/shard_map/lift/pallas_call | solution.py:90
  11.0 7.3 all-to-all-start.4
  18.3 12.2 %lift.3 = bf16[32,2,7,64,128]{4,3,2,1,0:T(8,128)(2,1)} custom-call(bf16[64,128,384]{2,1,0:T(8,128)(2,1)} %vel_ref.7, bf16[64,128,384]{2,1,0:T(8,128)(2,1)} %buoy_ref.7, bf16[2,224,384]{2,1,0:T(8,128)(2,1)} %constant.71.clone.table_ref), custom_call_target="tpu_custom_call" | custom-call | flops 2818572288 | bytes 19922944 | tf_op jit(solution)/shard_map/lift/pallas_call | solution.py:90
  30.5 60.4 %all-to-all-done.4.refs_5_ = bf16[32,2,3,64,128]{4,3,2,1,0:T(8,128)(2,1)S(1)} async-done(((bf16[32,2,3,64,128]{4,3,2,1,0:T(8,128)(2,1)}), bf16[32,2,3,64,128]{4,3,2,1,0:T(8,128)(2,1)S(1)}, u32[]{:S(2)}, u32[]{:S(2)}) %all-to-all-start.4) | async-done | bytes 3145760 | tf_op jit(solution)/shard_map/all_to_all | solution.py:337
  90.9 0.0 copy-start.1
  90.9 1.7 copy-done.1
  92.6 3.6 all-to-all-start
  96.2 12.6 %lift.4 = bf16[32,2,8,64,128]{4,3,2,1,0:T(8,128)(2,1)} custom-call(bf16[64,128,384]{2,1,0:T(8,128)(2,1)} %vel_ref.7, bf16[64,128,384]{2,1,0:T(8,128)(2,1)} %buoy_ref.7, bf16[2,256,384]{2,1,0:T(8,128)(2,1)} %constant.72.clone.table_ref), custom_call_target="tpu_custom_call" | custom-call | flops 3221225472 | bytes 20971520 | tf_op jit(solution)/shard_map/lift/pallas_call | solution.py:90
  108.8 0.0 copy-start.4
  108.8 149.9 %all-to-all-done.refs_5_ = bf16[32,2,7,64,128]{4,3,2,1,0:T(8,128)(2,1)} async-done(((bf16[32,2,7,64,128]{4,3,2,1,0:T(8,128)(2,1)}), bf16[32,2,7,64,128]{4,3,2,1,0:T(8,128)(2,1)}, u32[]{:S(2)}, u32[]{:S(2)}) %all-to-all-start) | async-done | bytes 7340064 | tf_op jit(solution)/shard_map/all_to_all | solution.py:337
  258.7 3.7 all-to-all-start.2
  262.4 0.0 copy-done.4
  262.4 0.1 dynamic_slice.3
  262.4 0.0 copy-start.5
  262.4 0.6 slice.9.refs_0_
  263.0 35.0 %planes.3.refs_6_ = bf16[32,2,7,64,128]{4,3,2,1,0:T(8,128)(2,1)} custom-call(f32[7]{0:T(128)} %slice.9.refs_0_, bf16[512,768]{1,0:T(8,128)(2,1)} %constant.68.clone.refs_1_, bf16[768,512]{1,0:T(8,128)(2,1)} %constant.66.clone.refs_2_, bf16[512,768]{1,0:T(8,128)(2,1)} %constant.67.clone.refs_3_, bf16[768,512]{1,0:T(8,128)(2,1)} %constant.69.clone.refs_4_, ...), custom_call_target="tpu_custom_call" | custom-call | flops 28185722880 | bytes 14680064 | tf_op jit(solution)/shard_map/planes/pallas_call | solution.py:163
  298.1 149.2 %all-to-all-done.2.refs_5_ = bf16[32,2,8,64,128]{4,3,2,1,0:T(8,128)(2,1)} async-done(((bf16[32,2,8,64,128]{4,3,2,1,0:T(8,128)(2,1)}), bf16[32,2,8,64,128]{4,3,2,1,0:T(8,128)(2,1)}, u32[]{:S(2)}, u32[]{:S(2)}) %all-to-all-start.2) | async-done | bytes 8388640 | tf_op jit(solution)/shard_map/all_to_all | solution.py:337
  447.2 3.6 all-to-all-start.1
  450.9 0.0 copy-done.5
  450.9 0.6 slice.10.refs_0_
  451.5 39.6 %planes.4.refs_6_ = bf16[32,2,8,64,128]{4,3,2,1,0:T(8,128)(2,1)} custom-call(f32[8]{0:T(128)} %slice.10.refs_0_, bf16[512,768]{1,0:T(8,128)(2,1)} %constant.68.clone.refs_1_, bf16[768,512]{1,0:T(8,128)(2,1)} %constant.66.clone.refs_2_, bf16[512,768]{1,0:T(8,128)(2,1)} %constant.67.clone.refs_3_, bf16[768,512]{1,0:T(8,128)(2,1)} %constant.69.clone.refs_4_, ...), custom_call_target="tpu_custom_call" | custom-call | flops 32212254720 | bytes 16777216 | tf_op jit(solution)/shard_map/planes/pallas_call | solution.py:163
  491.1 122.2 %all-to-all-done.1.refs_0_ = bf16[32,2,7,64,128]{4,3,2,1,0:T(8,128)(2,1)} async-done(((bf16[32,2,7,64,128]{4,3,2,1,0:T(8,128)(2,1)}), bf16[32,2,7,64,128]{4,3,2,1,0:T(8,128)(2,1)}, u32[]{:S(2)}, u32[]{:S(2)}) %all-to-all-start.1) | async-done | bytes 7340064 | tf_op jit(solution)/shard_map/all_to_all | solution.py:337
  613.3 3.9 all-to-all-start.3
  617.2 0.0 copy-start.3
  617.2 0.0 copy-start.2
  617.3 16.8 %planes.5 = bf16[32,2,3,64,128]{4,3,2,1,0:T(8,128)(2,1)} custom-call(f32[3]{0:T(128)} %bitcast.3, bf16[512,768]{1,0:T(8,128)(2,1)} %constant.68.clone.refs_1_, bf16[768,512]{1,0:T(8,128)(2,1)} %constant.66.clone.refs_2_, bf16[512,768]{1,0:T(8,128)(2,1)} %constant.67.clone.refs_3_, bf16[768,512]{1,0:T(8,128)(2,1)} %constant.69.clone.refs_4_, ...), custom_call_target="tpu_custom_call" | custom-call | flops 12079595520 | bytes 6291456 | tf_op jit(solution)/shard_map/planes/pallas_call | solution.py:163
  634.1 167.9 %all-to-all-done.3.refs_1_ = bf16[32,2,8,64,128]{4,3,2,1,0:T(8,128)(2,1)} async-done(((bf16[32,2,8,64,128]{4,3,2,1,0:T(8,128)(2,1)}), bf16[32,2,8,64,128]{4,3,2,1,0:T(8,128)(2,1)}, u32[]{:S(2)}, u32[]{:S(2)}) %all-to-all-start.3) | async-done | bytes 8388640 | tf_op jit(solution)/shard_map/all_to_all | solution.py:337
  801.9 2.8 all-to-all-start.5
  804.7 0.0 copy-done.3
  804.7 0.5 broadcast_in_dim.4.eig_val_ref
  805.3 0.1 copy.18
  805.4 0.6 mul.54.wave_y_ref
  806.0 0.5 multiply_multiply_fusion.wave_x_ref
  806.6 0.0 copy-done.2
  806.6 1.7 fusion.proj_ref
  808.3 25.0 %gather.1 = (f32[64,128,384]{2,1,0:T(8,128)}, f32[64,128,384]{2,1,0:T(8,128)}) custom-call(bf16[480,384]{1,0:T(8,128)(2,1)} %constant.73.clone.proj_ref, bf16[384,384]{1,0:T(8,128)(2,1)} %left_ref.1, bf16[64,128,384]{2,1,0:T(8,128)(2,1)} %buoy_ref.7, bf16[64,128,384]{2,1,0:T(8,128)(2,1)} %vel_ref.7, bf16[32,2,7,64,128]{4,3,2,1,0:T(8,128)(2,1)} %all-to-all-done.1.refs_0_, ...), custom_call_target="tpu_custom_call" | custom-call | flops 10871635968 | bytes 53477376 | tf_op jit(solution)/shard_map/gather/pallas_call | solution.py:229
  833.3 44.1 %all-to-all-done.5.in_ref = bf16[32,2,3,64,128]{4,3,2,1,0:T(8,128)(2,1)S(1)} async-done(((bf16[32,2,3,64,128]{4,3,2,1,0:T(8,128)(2,1)}), bf16[32,2,3,64,128]{4,3,2,1,0:T(8,128)(2,1)S(1)}, u32[]{:S(2)}, u32[]{:S(2)}) %all-to-all-start.5) | async-done | bytes 3145760 | tf_op jit(solution)/shard_map/all_to_all | solution.py:337
  877.4 0.0 copy-start
  877.4 1.7 copy-done
  879.1 21.7 %finish.1 = (bf16[64,128,384]{2,1,0:T(8,128)(2,1)}, bf16[64,128,384]{2,1,0:T(8,128)(2,1)}) custom-call(f32[64]{0:T(128)} %multiply_multiply_fusion.wave_x_ref, f32[128,1]{1,0:T(8,128)} %mul.54.wave_y_ref, f32[1,384]{1,0:T(1,128)} %broadcast_in_dim.4.eig_val_ref, bf16[384,384]{1,0:T(8,128)(2,1)} %right_ref.1, bf16[96,384]{1,0:T(8,128)(2,1)} %fusion.proj_ref, ...), custom_call_target="tpu_custom_call" | custom-call | flops 6039797760 | bytes 40894464 | tf_op jit(solution)/shard_map/finish/pallas_call | solution.py:285
  (1 shorter events, 0.0 us)
Async XLA Ops:
  11.0 79.9 %all-to-all-start.4 = ((bf16[32,2,3,64,128]{4,3,2,1,0:T(8,128)(2,1)}), bf16[32,2,3,64,128]{4,3,2,1,0:T(8,128)(2,1)S(1)}, u32[]{:S(2)}, u32[]{:S(2)}) async-start(bf16[32,2,3,64,128]{4,3,2,1,0:T(8,128)(2,1)} %lift.5), calls=%async_computation.4 | async-start | bytes 6291456 | tf_op jit(solution)/shard_map/all_to_all | solution.py:337
  90.9 1.7 copy-start.1
  92.6 166.1 %all-to-all-start = ((bf16[32,2,7,64,128]{4,3,2,1,0:T(8,128)(2,1)}), bf16[32,2,7,64,128]{4,3,2,1,0:T(8,128)(2,1)}, u32[]{:S(2)}, u32[]{:S(2)}) async-start(bf16[32,2,7,64,128]{4,3,2,1,0:T(8,128)(2,1)} %lift.3), calls=%async_computation | async-start | bytes 14680064 | tf_op jit(solution)/shard_map/all_to_all | solution.py:337
  108.8 153.6 %copy-start.4 = (f32[144]{0:T(256)S(1)}, f32[144]{0:T(256)}, u32[]{:S(2)}) copy-start(f32[144]{0:T(256)} %param.17) | copy-start | bytes 1732
  258.7 188.6 %all-to-all-start.2 = ((bf16[32,2,8,64,128]{4,3,2,1,0:T(8,128)(2,1)}), bf16[32,2,8,64,128]{4,3,2,1,0:T(8,128)(2,1)}, u32[]{:S(2)}, u32[]{:S(2)}) async-start(bf16[32,2,8,64,128]{4,3,2,1,0:T(8,128)(2,1)} %lift.4), calls=%async_computation.2 | async-start | bytes 16777216 | tf_op jit(solution)/shard_map/all_to_all | solution.py:337
  262.4 188.5 %copy-start.5 = (f32[18]{0:T(128)}, f32[18]{0:T(128)S(1)}, u32[]{:S(2)}) copy-start(f32[18]{0:T(128)S(1)} %dynamic_slice.3) | copy-start | bytes 220
  447.2 166.1 %all-to-all-start.1 = ((bf16[32,2,7,64,128]{4,3,2,1,0:T(8,128)(2,1)}), bf16[32,2,7,64,128]{4,3,2,1,0:T(8,128)(2,1)}, u32[]{:S(2)}, u32[]{:S(2)}) async-start(bf16[32,2,7,64,128]{4,3,2,1,0:T(8,128)(2,1)} %planes.3.refs_6_), calls=%async_computation.1 | async-start | bytes 14680064 | tf_op jit(solution)/shard_map/all_to_all | solution.py:337
  613.3 188.6 %all-to-all-start.3 = ((bf16[32,2,8,64,128]{4,3,2,1,0:T(8,128)(2,1)}), bf16[32,2,8,64,128]{4,3,2,1,0:T(8,128)(2,1)}, u32[]{:S(2)}, u32[]{:S(2)}) async-start(bf16[32,2,8,64,128]{4,3,2,1,0:T(8,128)(2,1)} %planes.4.refs_6_), calls=%async_computation.3 | async-start | bytes 16777216 | tf_op jit(solution)/shard_map/all_to_all | solution.py:337
  617.2 187.5 %copy-start.3 = (f32[384]{0:T(512)S(1)}, f32[384]{0:T(512)}, u32[]{:S(2)}) copy-start(f32[384]{0:T(512)} %param.18) | copy-start | bytes 4612
  617.2 189.3 %copy-start.2 = (bf16[384,384]{1,0:T(8,128)(2,1)S(1)}, bf16[384,384]{1,0:T(8,128)(2,1)}, u32[]{:S(2)}) copy-start(bf16[384,384]{1,0:T(8,128)(2,1)} %left_ref.1) | copy-start | bytes 884740
  801.9 75.4 %all-to-all-start.5 = ((bf16[32,2,3,64,128]{4,3,2,1,0:T(8,128)(2,1)}), bf16[32,2,3,64,128]{4,3,2,1,0:T(8,128)(2,1)S(1)}, u32[]{:S(2)}, u32[]{:S(2)}) async-start(bf16[32,2,3,64,128]{4,3,2,1,0:T(8,128)(2,1)} %planes.5), calls=%async_computation.5 | async-start | bytes 6291456 | tf_op jit(solution)/shard_map/all_to_all | solution.py:337
  877.4 1.7 copy-start

commit v6 on v5

--- a/solution.py
+++ b/solution.py
@@ -86,7 +86,7 @@
         values = jnp.einsum("fzn,fakn->fzak", table, fields, preferred_element_type=F32)
         values = values.astype(BF16).reshape(2, blocks, depth, modes_x, modes_y)
         return jnp.transpose(values, (1, 0, 2, 3, 4))
-    span = 8
+    span = 16
     return pl.pallas_call(
         lift_kernel,
         grid=(modes_x // span,),
@@ -108,9 +108,9 @@
 
 
 def plane_kernel(
-    col_count, strat_ref, along_y_ref, along_x_ref, back_x_ref, back_y_ref, in_ref, *refs
+    col_count, count, strat_ref, along_y_ref, along_x_ref, back_x_ref, back_y_ref, in_ref, *refs
 ):
-    out_ref = refs[-1]
+    out_refs = refs[-count:]
     blocks, _, depth, modes_x, lanes = in_ref.shape
     row_count = blocks // col_count
     for level in range(depth):
@@ -133,13 +133,17 @@
             folded = jnp.dot(back_x_ref[...], flux, preferred_element_type=F32).astype(BF16)
             values = jnp.dot(folded, back_y_ref[...], preferred_element_type=F32).astype(BF16)
             for row in range(row_count):
-                for col in range(col_count):
-                    out_ref[col * row_count + row, field, level] = values[
-                        row * modes_x : (row + 1) * modes_x, col * lanes : (col + 1) * lanes
-                    ]
-
-
-def planes(kernels, arrived, strat, along_y, along_x, back_x, back_y, col_count, after):
+                first = row * modes_x
+                for out_ref in out_refs:
+                    last = first + out_ref.shape[3]
+                    for col in range(col_count):
+                        out_ref[col * row_count + row, field, level] = values[
+                            first:last, col * lanes : (col + 1) * lanes
+                        ]
+                    first = last
+
+
+def planes(kernels, arrived, strat, along_y, along_x, back_x, back_y, col_count, splits, after):
     blocks, fields, depth, modes_x, modes_y = arrived.shape
     row_count = blocks // col_count
     if not kernels:
@@ -157,11 +161,12 @@
         values = values.astype(BF16).reshape(
             fields, depth, row_count, modes_x, col_count, modes_y
         )
-        return jnp.transpose(values, (4, 2, 0, 1, 3, 5)).reshape(arrived.shape)
+        values = jnp.transpose(values, (4, 2, 0, 1, 3, 5)).reshape(arrived.shape)
+        return jnp.split(values, np.cumsum(splits)[:-1], axis=3)
     block = pl.BlockSpec((blocks, fields, 1, modes_x, modes_y), lambda z: (0, 0, z, 0, 0))
     work = along_y.size * along_x.shape[1] + along_x.size * along_y.shape[1]
     return pl.pallas_call(
-        lambda *refs: plane_kernel(col_count, *refs),
+        lambda *refs: plane_kernel(col_count, len(splits), *refs),
         grid=(depth,),
         in_specs=[
             pl.BlockSpec(memory_space=pltpu.SMEM),
@@ -172,8 +177,13 @@
             block,
         ]
         + [pl.BlockSpec(memory_space=pl.ANY)] * len(after),
-        out_specs=block,
-        out_shape=jax.ShapeDtypeStruct(arrived.shape, BF16),
+        out_specs=[
+            pl.BlockSpec((blocks, fields, 1, size, modes_y), lambda z: (0, 0, z, 0, 0))
+            for size in splits
+        ],
+        out_shape=[
+            jax.ShapeDtypeStruct((blocks, fields, depth, size, modes_y), BF16) for size in splits
+        ],
         compiler_params=params(1),
         cost_estimate=pl.CostEstimate(
             flops=4 * fields * depth * work, bytes_accessed=4 * arrived.size, transcendentals=0
@@ -202,63 +212,25 @@
     return jnp.dot(jnp.concatenate(rows, axis=0), proj_ref[...], preferred_element_type=F32)
 
 
-def gather_kernel(proj_ref, left_ref, buoy_ref, vel_ref, *refs):
-    in_refs, out_refs = refs[:-2], refs[-2:]
+def finish_kernel(
+    count,
+    wave_x_ref,
+    wave_y_ref,
+    eig_val_ref,
+    left_ref,
+    right_ref,
+    proj_ref,
+    buoy_ref,
+    vel_ref,
+    *refs,
+):
+    in_refs, out_refs = refs[:count], refs[-2:]
     span, lanes, degree = buoy_ref.shape
-    for field, (coeff_ref, out_ref) in enumerate(zip((buoy_ref, vel_ref), out_refs)):
+    modal = []
+    for field, coeff_ref in enumerate((buoy_ref, vel_ref)):
         tend = explicit_step * project(in_refs, field, proj_ref)
         rhs = coeff_ref[...].reshape(span * lanes, degree).astype(F32) + tend
-        modal = jnp.dot(rhs.astype(BF16), left_ref[...], preferred_element_type=F32)
-        out_ref[...] = modal.reshape(span, lanes, degree)
-
-
-def gather(kernels, folded, proj, eig_left, fields):
-    modes_x, modes_y, degree = fields[0].shape
-    if not kernels:
-        parts = [
-            jnp.transpose(part, (1, 0, 2, 3, 4)).reshape(2, -1, modes_x, modes_y)
-            for part in folded
-        ]
-        parts = jnp.concatenate(parts, axis=1)
-        tend = jnp.einsum("fzak,zn->fakn", parts, proj, preferred_element_type=F32)
-        rhs = jnp.stack(fields).astype(F32) + explicit_step * tend
-        modal = jnp.einsum("fakn,nj->fakj", rhs.astype(BF16), eig_left, preferred_element_type=F32)
-        return [modal[0], modal[1]]
-    span = 8
-    block = pl.BlockSpec((span, modes_y, degree), lambda a: (a, 0, 0))
-    return pl.pallas_call(
-        gather_kernel,
-        grid=(modes_x // span,),
-        in_specs=[
-            whole(proj.shape),
-            whole(eig_left.shape),
-            block,
-            block,
-        ]
-        + [
-            pl.BlockSpec((*part.shape[:3], span, modes_y), lambda a: (0, 0, 0, a, 0))
-            for part in folded
-        ],
-        out_specs=[block, block],
-        out_shape=[jax.ShapeDtypeStruct(fields[0].shape, F32)] * 2,
-        compiler_params=params(1),
-        cost_estimate=pl.CostEstimate(
-            flops=4 * fields[0].size * (proj.shape[0] + degree),
-            bytes_accessed=2 * sum(part.size for part in folded) + 12 * fields[0].size,
-            transcendentals=0,
-        ),
-        name="gather",
-    )(proj, eig_left, *fields, *folded)
-
-
-def finish_kernel(
-    wave_x_ref, wave_y_ref, eig_val_ref, right_ref, proj_ref, buoy_ref, vel_ref, in_ref, *out_refs
-):
-    span, lanes, degree = buoy_ref.shape
-    modal = []
-    for field, part_ref in enumerate((buoy_ref, vel_ref)):
-        part = part_ref[...].reshape(span * lanes, degree)
-        modal.append(part + project([in_ref], field, proj_ref))
+        modal.append(jnp.dot(rhs.astype(BF16), left_ref[...], preferred_element_type=F32))
     first = pl.program_id(0) * span
     waves = [4.0 * (wave_x_ref[first + mode] + wave_y_ref[...]) for mode in range(span)]
     solved = solve_modal(modal[0], modal[1], jnp.concatenate(waves, axis=0), eig_val_ref[...])
@@ -267,50 +239,73 @@
         out_ref[...] = result.reshape(span, lanes, degree)
 
 
-def finish(kernels, folded, proj, modal, eig_val, eig_right, wave_x, wave_y):
-    modes_x, modes_y, degree = modal[0].shape
+def finish(
+    kernels, start, size, parts, proj, buoy, vel_w, eigen, wave_x, wave_y, earlier
+):
+    eig_val, eig_left, eig_right = eigen
+    modes_y, degree = buoy.shape[1:]
+    wave_x = wave_x[start : start + size]
     if not kernels:
-        parts = jnp.transpose(folded, (1, 0, 2, 3, 4)).reshape(2, -1, modes_x, modes_y)
-        last = jnp.einsum("fzak,zn->fakn", parts, proj, preferred_element_type=F32)
+        taken = [part[:, :, :, start - first :][:, :, :, :size] for first, part in parts]
+        taken = [
+            jnp.transpose(part, (1, 0, 2, 3, 4)).reshape(2, -1, size, modes_y) for part in taken
+        ]
+        tend = jnp.einsum(
+            "fzak,zn->fakn", jnp.concatenate(taken, axis=1), proj, preferred_element_type=F32
+        )
+        fields = jnp.stack([buoy, vel_w])[:, start : start + size].astype(F32)
+        rhs = (fields + explicit_step * tend).astype(BF16)
+        modal = jnp.einsum("fakn,nj->fakj", rhs, eig_left, preferred_element_type=F32)
         wave = 4.0 * (wave_x[:, None, None] + wave_y[None, :, None])
-        solved = solve_modal(modal[0] + last[0], modal[1] + last[1], wave, eig_val)
-        return tuple(
+        results = [
             jnp.einsum("akj,jn->akn", values, eig_right, preferred_element_type=F32).astype(BF16)
-            for values in solved
-        )
+            for values in solve_modal(modal[0], modal[1], wave, eig_val)
+        ]
+        if earlier:
+            results = [jnp.concatenate(pair, axis=0) for pair in zip(earlier, results)]
+        return results
     span = 8
-    blocks, fields, depth = folded.shape[:3]
-    block = pl.BlockSpec((span, modes_y, degree), lambda a: (a, 0, 0))
-    result = jax.ShapeDtypeStruct(modal[0].shape, BF16)
+    block = pl.BlockSpec((span, modes_y, degree), lambda a: (a + start // span, 0, 0))
+
+    def part_spec(first, part):
+        return pl.BlockSpec(
+            (*part.shape[:3], span, modes_y), lambda a: (0, 0, 0, a + (start - first) // span, 0)
+        )
+
+    result = jax.ShapeDtypeStruct(buoy.shape, BF16)
+    operands = [wave_x, wave_y[:, None], eig_val[None, :], eig_left, eig_right, proj, buoy, vel_w]
+    operands += [part for _, part in parts]
     return pl.pallas_call(
-        finish_kernel,
-        grid=(modes_x // span,),
+        lambda *refs: finish_kernel(len(parts), *refs),
+        grid=(size // span,),
         in_specs=[
             pl.BlockSpec(memory_space=pltpu.SMEM),
             whole((modes_y, 1)),
             whole((1, degree)),
+            whole(eig_left.shape),
             whole(eig_right.shape),
             whole(proj.shape),
             block,
             block,
-            pl.BlockSpec((blocks, fields, depth, span, modes_y), lambda a: (0, 0, 0, a, 0)),
-        ],
+        ]
+        + [part_spec(first, part) for first, part in parts]
+        + [pl.BlockSpec(memory_space=pl.ANY)] * len(earlier),
         out_specs=[block, block],
         out_shape=[result, result],
+        input_output_aliases={len(operands) + item: item for item in range(len(earlier))},
         compiler_params=params(1),
         cost_estimate=pl.CostEstimate(
-            flops=4 * modal[0].size * (proj.shape[0] + degree),
-            bytes_accessed=12 * modal[0].size + 2 * folded.size,
-            transcendentals=modal[0].size,
+            flops=4 * size * modes_y * degree * (proj.shape[0] + 2 * degree),
+            bytes_accessed=size * modes_y * (8 * degree + 4 * proj.shape[0]),
+            transcendentals=size * modes_y * degree,
         ),
         name="finish",
-    )(wave_x, wave_y[:, None], eig_val[None, :], eig_right, proj, *modal, folded)
+    )(*operands, *earlier)
 
 
 def chunk_sizes(own):
-    first = -(-own * 3 // 18)
-    second = (own - first) // 2
-    return [size for size in (first, second, own - first - second) if size]
+    first = -(-own * 4 // 18)
+    return [size for size in (first, own - first) if size]
 
 
 def per_device(buoy, vel_w, strat, eig_val, eig_left, eig_right):
@@ -323,7 +318,7 @@
     shard = strat.shape[0]
     own = -(-shard // row_count)
     padding = own * row_count - shard
-    kernels = modes_y % 128 == 0 and modes_x % 16 == 0 and degree % 128 == 0
+    kernels = modes_y % 128 == 0 and modes_x % 64 == 0 and degree % 128 == 0
     row = lax.axis_index("row")
     col = lax.axis_index("col")
 
@@ -352,40 +347,38 @@
     for start, stop in pieces:
         table = forward_z[:, :, start:stop].reshape(2, blocks * (stop - start), degree)
         arrived.append(exchange(lift(kernels, vel_w, buoy, jnp.asarray(table), blocks)))
-    order = list(range(1, len(pieces))) + [0]
-    folded, after = [], []
-    for piece in order:
-        start, stop = pieces[piece]
-        fluxes = planes(
+    split = modes_x - modes_x // 4
+    parts, after = [], []
+    for values, (start, stop) in zip(arrived, pieces):
+        splits = [split, modes_x - split] if stop == own else [modes_x]
+        after = planes(
             kernels,
-            arrived[piece],
+            values,
             strat_own[start:stop],
             along_y,
             along_x,
             back_x,
             back_y,
             col_count,
+            splits,
             after,
         )
-        after = [fluxes]
-        folded.append(exchange(fluxes))
-    projs = [
+        parts.append([exchange(fluxes) for fluxes in after])
+    proj = [
         backward_z[:, start:stop].reshape(blocks * (stop - start), degree)
-        for start, stop in (pieces[piece] for piece in order)
+        for start, stop in pieces
     ]
-    if len(pieces) > 1:
-        table = jnp.asarray(np.concatenate(projs[:-1], axis=0))
-        modal = gather(kernels, folded[:-1], table, eig_left, [buoy, vel_w])
-    else:
-        modal = [
-            jnp.einsum("akn,nj->akj", part, eig_left, preferred_element_type=F32)
-            for part in (buoy, vel_w)
-        ]
-    last = jnp.dot(jnp.asarray(projs[-1]), eig_left, preferred_element_type=F32)
-    last = (explicit_step * last).astype(BF16)
+    proj = jnp.asarray(np.concatenate(proj, axis=0))
     wave_x = wave_squares(total_x, row * modes_x, modes_x)
     wave_y = wave_squares(total_y, col * modes_y, modes_y)
-    return finish(kernels, folded[-1], last, modal, eig_val, eig_right, wave_x, wave_y)
+    eigen = (eig_val, eig_left, eig_right)
+    results = []
+    for start, size, fluxes in ((0, split, parts[-1][0]), (split, modes_x - split, parts[-1][1])):
+        held = [(0, part[0]) for part in parts[:-1]] + [(start, fluxes)]
+        results = finish(
+            kernels, start, size, held, proj, buoy, vel_w, eigen, wave_x, wave_y, results
+        )
+    return tuple(results)
 
 
 def solution(mesh):

time: 902 us -> 880 us (0.976)
  blocking collectives: 0 us -> 245 us
  waiting for transfers between devices: 694 us -> 456 us
  Pallas kernels: 173 us -> 156 us
    all_to_all x0 -> x1, blocking collectives: none -> 245 us  [exchange(): lax.all_to_all(values, ('col', 'row'), split_axis=0, concat_axis=0, tiled...]
    all_to_all x6 -> x4, waiting for transfers between devices: 694 us -> 456 us  [exchange(): lax.all_to_all(values, ('col', 'row'), split_axis=0, concat_axis=0, tiled...]
    pallas_call x3 -> x2, Pallas kernels: 35.1 us -> 25 us  [lift(): pl.pallas_call(lift_kernel, grid=(modes_x // span,), in_specs=[pl.BlockSp...]
    pallas_call x5 -> x4, Pallas kernels: 138 us -> 131 us  [the longest x2 88.4 us: planes(): pl.pallas_call(lambda *refs: plane_kernel(col_count, len(splits), *refs),...]
    all_to_all x6 -> x4, starting transfers between devices: 24.9 us -> 18.7 us  [exchange(): lax.all_to_all(values, ('col', 'row'), split_axis=0, concat_axis=0, tiled...]
  transfers between devices with their start and end apart: 6 -> 4, of which waited for: 6 -> 4; matrix products, arithmetic and copies ran while one was open for 1% -> 0% of each run, Pallas kernels for 16% -> 15%
where the time goes in v6:
time: 880 us; the launch traced here: 879 us
  waiting for transfers between devices  456 us (52%)
  blocking collectives  245 us (28%)
  Pallas kernels  156 us (18%)
  starting transfers between devices  18.7 us (2%)
    all_to_all x4, waiting for transfers between devices, exchange(): lax.all_to_all(values, ('col', 'row'), split_axis=0, concat_axis=0, tiled...  456 us
    all_to_all x1, blocking collectives, exchange(): lax.all_to_all(values, ('col', 'row'), split_axis=0, concat_axis=0, tiled...  245 us
    pallas_call x2, Pallas kernels, planes(): pl.pallas_call(lambda *refs: plane_kernel(col_count, len(splits), *refs),...  88.4 us
    pallas_call x2, Pallas kernels, finish(): pl.pallas_call(lambda *refs: finish_kernel(len(parts), *refs), grid=(size...  43.1 us
    pallas_call x2, Pallas kernels, lift(): pl.pallas_call(lift_kernel, grid=(modes_x // span,), in_specs=[pl.BlockSp...  25 us
    all_to_all x4, starting transfers between devices, exchange(): lax.all_to_all(values, ('col', 'row'), split_axis=0, concat_axis=0, tiled...  18.7 us
  transfers between devices with their start and end apart: 4, of which 4 were waited for; matrix products, arithmetic and copies ran while one was open for 0% of the time, Pallas kernels for 15%

profile of v6, /device:TPU:0, one launch (start us, length us, event | category | flops | bytes accessed | tf_op | source)
XLA Modules:
  0.0 879.3 jit_solution(8886366428952702216)
XLA Ops:
  0.6 9.1 %lift.2 = bf16[32,2,4,64,128]{4,3,2,1,0:T(8,128)(2,1)} custom-call(bf16[64,128,384]{2,1,0:T(8,128)(2,1)} %refs_7_.3, bf16[64,128,384]{2,1,0:T(8,128)(2,1)} %refs_6_.3, bf16[2,128,384]{2,1,0:T(8,128)(2,1)} %constant.64.clone.table_ref), custom_call_target="tpu_custom_call" | custom-call | flops 1610612736 | bytes 16777216 | tf_op jit(solution)/shard_map/lift/pallas_call | solution.py:90
  9.8 7.4 all-to-all-start
  17.2 15.8 %lift.3 = bf16[32,2,14,64,128]{4,3,2,1,0:T(8,128)(2,1)} custom-call(bf16[64,128,384]{2,1,0:T(8,128)(2,1)} %refs_7_.3, bf16[64,128,384]{2,1,0:T(8,128)(2,1)} %refs_6_.3, bf16[2,448,384]{2,1,0:T(8,128)(2,1)} %constant.65.clone.table_ref), custom_call_target="tpu_custom_call" | custom-call | flops 5637144576 | bytes 27262976 | tf_op jit(solution)/shard_map/lift/pallas_call | solution.py:90
  33.0 0.0 copy-start.1
  33.0 79.2 %all-to-all-done.refs_5_ = bf16[32,2,4,64,128]{4,3,2,1,0:T(8,128)(2,1)} async-done(((bf16[32,2,4,64,128]{4,3,2,1,0:T(8,128)(2,1)}), bf16[32,2,4,64,128]{4,3,2,1,0:T(8,128)(2,1)}, u32[]{:S(2)}, u32[]{:S(2)}) %all-to-all-start) | async-done | bytes 4194336 | tf_op jit(solution)/shard_map/all_to_all | solution.py:332
  112.3 3.8 all-to-all-start.2
  116.1 0.0 copy-done.1
  116.1 0.6 dynamic_slice.3
  116.7 21.3 %planes.2.refs_6_ = bf16[32,2,4,64,128]{4,3,2,1,0:T(8,128)(2,1)} custom-call(f32[4]{0:T(128)} %bitcast.2, bf16[512,768]{1,0:T(8,128)(2,1)} %constant.62.clone.refs_1_, bf16[768,512]{1,0:T(8,128)(2,1)} %constant.60.clone.refs_2_, bf16[512,768]{1,0:T(8,128)(2,1)} %constant.61.clone.refs_3_, bf16[768,512]{1,0:T(8,128)(2,1)} %constant.63.clone.refs_4_, ...), custom_call_target="tpu_custom_call" | custom-call | flops 16106127360 | bytes 8388608 | tf_op jit(solution)/shard_map/planes/pallas_call | solution.py:168
  138.0 0.0 copy-start.2
  138.0 297.8 %all-to-all-done.2.refs_5_ = bf16[32,2,14,64,128]{4,3,2,1,0:T(8,128)(2,1)} async-done(((bf16[32,2,14,64,128]{4,3,2,1,0:T(8,128)(2,1)}), bf16[32,2,14,64,128]{4,3,2,1,0:T(8,128)(2,1)}, u32[]{:S(2)}, u32[]{:S(2)}) %all-to-all-start.2) | async-done | bytes 14680096 | tf_op jit(solution)/shard_map/all_to_all | solution.py:332
  435.8 3.8 all-to-all-start.1
  439.6 0.0 copy-done.2
  439.6 0.6 slice.14.refs_0_
  440.2 67.1 %planes.3 = (bf16[32,2,14,48,128]{4,3,2,1,0:T(8,128)(2,1)}, bf16[32,2,14,16,128]{4,3,2,1,0:T(8,128)(2,1)}) custom-call(f32[14]{0:T(128)} %slice.14.refs_0_, bf16[512,768]{1,0:T(8,128)(2,1)} %constant.62.clone.refs_1_, bf16[768,512]{1,0:T(8,128)(2,1)} %constant.60.clone.refs_2_, bf16[512,768]{1,0:T(8,128)(2,1)} %constant.61.clone.refs_3_, ...), custom_call_target="tpu_custom_call" | custom-call | flops 56371445760 | bytes 29360128 | tf_op jit(solution)/shard_map/planes/pallas_call | solution.py:168
  507.3 27.2 %all-to-all-done.1.refs_8_ = bf16[32,2,4,64,128]{4,3,2,1,0:T(8,128)(2,1)} async-done(((bf16[32,2,4,64,128]{4,3,2,1,0:T(8,128)(2,1)}), bf16[32,2,4,64,128]{4,3,2,1,0:T(8,128)(2,1)}, u32[]{:S(2)}, u32[]{:S(2)}) %all-to-all-start.1) | async-done | bytes 4194336 | tf_op jit(solution)/shard_map/all_to_all | solution.py:332
  534.5 244.8 %all_to_all.25.refs_9_ = bf16[32,2,14,48,128]{4,3,2,1,0:T(8,128)(2,1)} all-to-all(bf16[32,2,14,48,128]{4,3,2,1,0:T(8,128)(2,1)} %get-tuple-element.7), channel_id=1, replica_groups=mesh['row'=8,'col'=4] {'col','row'}, dimensions={0} | all-to-all | bytes 22020096 | tf_op jit(solution)/shard_map/all_to_all | solution.py:332
  779.3 0.0 copy-start
  779.3 3.7 all-to-all-start.3
  783.0 0.0 copy-done
  783.0 0.6 broadcast_in_dim.2.refs_2_
  783.6 0.0 copy-start.3
  783.6 0.7 slice.12.refs_0_
  784.2 0.7 fusion.3.refs_1_
  784.9 0.0 copy-done.3
  784.9 30.5 %finish.2 = (bf16[64,128,384]{2,1,0:T(8,128)(2,1)}, bf16[64,128,384]{2,1,0:T(8,128)(2,1)}) custom-call(f32[48]{0:T(128)} %bitcast.3, f32[128,1]{1,0:T(8,128)} %fusion.3.refs_1_, f32[1,384]{1,0:T(1,128)} %broadcast_in_dim.2.refs_2_, bf16[384,384]{1,0:T(8,128)(2,1)} %refs_3_.5, bf16[384,384]{1,0:T(8,128)(2,1)} %refs_4_.5, ...), custom_call_target="tpu_custom_call" | custom-call | flops 12683575296 | bytes 33030144 | tf_op jit(solution)/shard_map/finish/pallas_call | solution.py:278
  815.5 51.3 %all-to-all-done.3.refs_9_ = bf16[32,2,14,16,128]{4,3,2,1,0:T(8,128)(2,1)} async-done(((bf16[32,2,14,16,128]{4,3,2,1,0:T(8,128)(2,1)}), bf16[32,2,14,16,128]{4,3,2,1,0:T(8,128)(2,1)}, u32[]{:S(2)}, u32[]{:S(2)}) %all-to-all-start.3) | async-done | bytes 3670048 | tf_op jit(solution)/shard_map/all_to_all | solution.py:332
  866.8 12.5 %finish.3 = (bf16[64,128,384]{2,1,0:T(8,128)(2,1)}, bf16[64,128,384]{2,1,0:T(8,128)(2,1)}) custom-call(f32[16]{0:T(128)} %slice.12.refs_0_, f32[128,1]{1,0:T(8,128)} %fusion.3.refs_1_, f32[1,384]{1,0:T(1,128)} %broadcast_in_dim.2.refs_2_, bf16[384,384]{1,0:T(8,128)(2,1)} %refs_3_.5, ...), custom_call_target="tpu_custom_call", output_to_operand_aliasing={{0}: (10, {}), {1}: (11, {})} | custom-call | flops 4227858432 | bytes 11010048 | tf_op jit(solution)/shard_map/finish/pallas_call | solution.py:278
  (1 shorter events, 0.0 us)
Async XLA Ops:
  9.8 102.5 %all-to-all-start = ((bf16[32,2,4,64,128]{4,3,2,1,0:T(8,128)(2,1)}), bf16[32,2,4,64,128]{4,3,2,1,0:T(8,128)(2,1)}, u32[]{:S(2)}, u32[]{:S(2)}) async-start(bf16[32,2,4,64,128]{4,3,2,1,0:T(8,128)(2,1)} %lift.2), calls=%async_computation | async-start | bytes 8388608 | tf_op jit(solution)/shard_map/all_to_all | solution.py:332
  33.0 83.1 %copy-start.1 = (f32[144]{0:T(256)S(1)}, f32[144]{0:T(256)}, u32[]{:S(2)}) copy-start(f32[144]{0:T(256)} %param.15) | copy-start | bytes 1732
  112.3 323.6 %all-to-all-start.2 = ((bf16[32,2,14,64,128]{4,3,2,1,0:T(8,128)(2,1)}), bf16[32,2,14,64,128]{4,3,2,1,0:T(8,128)(2,1)}, u32[]{:S(2)}, u32[]{:S(2)}) async-start(bf16[32,2,14,64,128]{4,3,2,1,0:T(8,128)(2,1)} %lift.3), calls=%async_computation.2 | async-start | bytes 29360128 | tf_op jit(solution)/shard_map/all_to_all | solution.py:332
  138.0 301.6 %copy-start.2 = (f32[18]{0:T(128)S(1)}, f32[18]{0:T(128)}, u32[]{:S(2)}) copy-start(f32[18]{0:T(128)} %dynamic_slice.3) | copy-start | bytes 220
  435.8 98.7 %all-to-all-start.1 = ((bf16[32,2,4,64,128]{4,3,2,1,0:T(8,128)(2,1)}), bf16[32,2,4,64,128]{4,3,2,1,0:T(8,128)(2,1)}, u32[]{:S(2)}, u32[]{:S(2)}) async-start(bf16[32,2,4,64,128]{4,3,2,1,0:T(8,128)(2,1)} %planes.2.refs_6_), calls=%async_computation.1 | async-start | bytes 8388608 | tf_op jit(solution)/shard_map/all_to_all | solution.py:332
  779.3 3.7 copy-start
  779.3 87.5 %all-to-all-start.3 = ((bf16[32,2,14,16,128]{4,3,2,1,0:T(8,128)(2,1)}), bf16[32,2,14,16,128]{4,3,2,1,0:T(8,128)(2,1)}, u32[]{:S(2)}, u32[]{:S(2)}) async-start(bf16[32,2,14,16,128]{4,3,2,1,0:T(8,128)(2,1)} %get-tuple-element.6), calls=%async_computation.3 | async-start | bytes 7340032 | tf_op jit(solution)/shard_map/all_to_all | solution.py:332
  783.6 1.4 copy-start.3

commit v7 on v6

--- a/solution.py
+++ b/solution.py
@@ -16,7 +16,7 @@
 
 BF16 = jnp.bfloat16
 F32 = jnp.float32
-VMEM_BYTES = 56 * 1024 * 1024
+VMEM_BYTES = 63 * 1024 * 1024
 
 
 def fourier_trig(modes, points):
@@ -347,7 +347,7 @@
     for start, stop in pieces:
         table = forward_z[:, :, start:stop].reshape(2, blocks * (stop - start), degree)
         arrived.append(exchange(lift(kernels, vel_w, buoy, jnp.asarray(table), blocks)))
-    split = modes_x - modes_x // 4
+    split = modes_x - modes_x // 8
     parts, after = [], []
     for values, (start, stop) in zip(arrived, pieces):
         splits = [split, modes_x - split] if stop == own else [modes_x]

time: 880 us -> 875 us (level)
  waiting for transfers between devices: 456 us -> 412 us
  blocking collectives: 245 us -> 284 us
    all_to_all x4, waiting for transfers between devices: 456 us -> 412 us  [exchange(): lax.all_to_all(values, ('col', 'row'), split_axis=0, concat_axis=0, tiled...]
    all_to_all x1, blocking collectives: 245 us -> 284 us  [exchange(): lax.all_to_all(values, ('col', 'row'), split_axis=0, concat_axis=0, tiled...]
  transfers between devices with their start and end apart: 4 -> 4, of which waited for: 4 -> 4; matrix products, arithmetic and copies ran while one was open for 0% -> 0% of each run, Pallas kernels for 15% -> 16%
where the time goes in v7:
time: 875 us
  waiting for transfers between devices  412 us (47%)
  blocking collectives  284 us (32%)
  Pallas kernels  156 us (18%)
  starting transfers between devices  18.4 us (2%)
    all_to_all x4, waiting for transfers between devices, exchange(): lax.all_to_all(values, ('col', 'row'), split_axis=0, concat_axis=0, tiled...  412 us
    all_to_all x1, blocking collectives, exchange(): lax.all_to_all(values, ('col', 'row'), split_axis=0, concat_axis=0, tiled...  284 us
    pallas_call x2, Pallas kernels, planes(): pl.pallas_call(lambda *refs: plane_kernel(col_count, len(splits), *refs),...  88.4 us
    pallas_call x2, Pallas kernels, finish(): pl.pallas_call(lambda *refs: finish_kernel(len(parts), *refs), grid=(size...  42.9 us
    pallas_call x2, Pallas kernels, lift(): pl.pallas_call(lift_kernel, grid=(modes_x // span,), in_specs=[pl.BlockSp...  25 us
    all_to_all x4, starting transfers between devices, exchange(): lax.all_to_all(values, ('col', 'row'), split_axis=0, concat_axis=0, tiled...  18.4 us
  transfers between devices with their start and end apart: 4, of which 4 were waited for; matrix products, arithmetic and copies ran while one was open for 0% of the time, Pallas kernels for 16%

profile of v7, /device:TPU:0, one launch (start us, length us, event | category | flops | bytes accessed | tf_op | source)
XLA Modules:
  0.0 874.5 jit_solution(7653830208658614126)
XLA Ops:
  0.6 9.1 %lift.2 = bf16[32,2,4,64,128]{4,3,2,1,0:T(8,128)(2,1)} custom-call(bf16[64,128,384]{2,1,0:T(8,128)(2,1)} %refs_7_.3, bf16[64,128,384]{2,1,0:T(8,128)(2,1)} %refs_6_.3, bf16[2,128,384]{2,1,0:T(8,128)(2,1)} %constant.64.clone.table_ref), custom_call_target="tpu_custom_call" | custom-call | flops 1610612736 | bytes 16777216 | tf_op jit(solution)/shard_map/lift/pallas_call | solution.py:90
  9.8 7.4 all-to-all-start
  17.2 15.8 %lift.3 = bf16[32,2,14,64,128]{4,3,2,1,0:T(8,128)(2,1)} custom-call(bf16[64,128,384]{2,1,0:T(8,128)(2,1)} %refs_7_.3, bf16[64,128,384]{2,1,0:T(8,128)(2,1)} %refs_6_.3, bf16[2,448,384]{2,1,0:T(8,128)(2,1)} %constant.65.clone.table_ref), custom_call_target="tpu_custom_call" | custom-call | flops 5637144576 | bytes 27262976 | tf_op jit(solution)/shard_map/lift/pallas_call | solution.py:90
  33.0 0.0 copy-start.1
  33.0 79.2 %all-to-all-done.refs_5_ = bf16[32,2,4,64,128]{4,3,2,1,0:T(8,128)(2,1)} async-done(((bf16[32,2,4,64,128]{4,3,2,1,0:T(8,128)(2,1)}), bf16[32,2,4,64,128]{4,3,2,1,0:T(8,128)(2,1)}, u32[]{:S(2)}, u32[]{:S(2)}) %all-to-all-start) | async-done | bytes 4194336 | tf_op jit(solution)/shard_map/all_to_all | solution.py:332
  112.3 3.8 all-to-all-start.2
  116.1 0.0 copy-done.1
  116.1 0.6 dynamic_slice.3
  116.7 21.3 %planes.2.refs_6_ = bf16[32,2,4,64,128]{4,3,2,1,0:T(8,128)(2,1)} custom-call(f32[4]{0:T(128)} %bitcast.2, bf16[512,768]{1,0:T(8,128)(2,1)} %constant.62.clone.refs_1_, bf16[768,512]{1,0:T(8,128)(2,1)} %constant.60.clone.refs_2_, bf16[512,768]{1,0:T(8,128)(2,1)} %constant.61.clone.refs_3_, bf16[768,512]{1,0:T(8,128)(2,1)} %constant.63.clone.refs_4_, ...), custom_call_target="tpu_custom_call" | custom-call | flops 16106127360 | bytes 8388608 | tf_op jit(solution)/shard_map/planes/pallas_call | solution.py:168
  138.0 0.0 copy-start.2
  138.0 297.8 %all-to-all-done.2.refs_5_ = bf16[32,2,14,64,128]{4,3,2,1,0:T(8,128)(2,1)} async-done(((bf16[32,2,14,64,128]{4,3,2,1,0:T(8,128)(2,1)}), bf16[32,2,14,64,128]{4,3,2,1,0:T(8,128)(2,1)}, u32[]{:S(2)}, u32[]{:S(2)}) %all-to-all-start.2) | async-done | bytes 14680096 | tf_op jit(solution)/shard_map/all_to_all | solution.py:332
  435.8 3.8 all-to-all-start.1
  439.6 0.0 copy-done.2
  439.6 0.6 slice.14.refs_0_
  440.2 67.0 %planes.3 = (bf16[32,2,14,56,128]{4,3,2,1,0:T(8,128)(2,1)}, bf16[32,2,14,8,128]{4,3,2,1,0:T(8,128)(2,1)}) custom-call(f32[14]{0:T(128)} %slice.14.refs_0_, bf16[512,768]{1,0:T(8,128)(2,1)} %constant.62.clone.refs_1_, bf16[768,512]{1,0:T(8,128)(2,1)} %constant.60.clone.refs_2_, bf16[512,768]{1,0:T(8,128)(2,1)} %constant.61.clone.refs_3_, ...), custom_call_target="tpu_custom_call" | custom-call | flops 56371445760 | bytes 29360128 | tf_op jit(solution)/shard_map/planes/pallas_call | solution.py:168
  507.2 27.3 %all-to-all-done.1.refs_8_ = bf16[32,2,4,64,128]{4,3,2,1,0:T(8,128)(2,1)} async-done(((bf16[32,2,4,64,128]{4,3,2,1,0:T(8,128)(2,1)}), bf16[32,2,4,64,128]{4,3,2,1,0:T(8,128)(2,1)}, u32[]{:S(2)}, u32[]{:S(2)}) %all-to-all-start.1) | async-done | bytes 4194336 | tf_op jit(solution)/shard_map/all_to_all | solution.py:332
  534.5 0.0 copy-start
  534.5 284.3 %all_to_all.25.refs_9_ = bf16[32,2,14,56,128]{4,3,2,1,0:T(8,128)(2,1)} all-to-all(bf16[32,2,14,56,128]{4,3,2,1,0:T(8,128)(2,1)} %get-tuple-element.7), channel_id=1, replica_groups=mesh['row'=8,'col'=4] {'col','row'}, dimensions={0} | all-to-all | bytes 25690112 | tf_op jit(solution)/shard_map/all_to_all | solution.py:332
  818.7 3.4 all-to-all-start.3
  822.2 0.0 copy-done
  822.2 0.6 broadcast_in_dim.2.refs_2_
  822.8 0.0 copy-start.3
  822.8 0.7 slice.12.refs_0_
  823.5 0.7 fusion.3.refs_1_
  824.2 0.0 copy-done.3
  824.2 35.1 %finish.2 = (bf16[64,128,384]{2,1,0:T(8,128)(2,1)}, bf16[64,128,384]{2,1,0:T(8,128)(2,1)}) custom-call(f32[56]{0:T(128)} %bitcast.3, f32[128,1]{1,0:T(8,128)} %fusion.3.refs_1_, f32[1,384]{1,0:T(1,128)} %broadcast_in_dim.2.refs_2_, bf16[384,384]{1,0:T(8,128)(2,1)} %refs_3_.5, bf16[384,384]{1,0:T(8,128)(2,1)} %refs_4_.5, ...), custom_call_target="tpu_custom_call" | custom-call | flops 14797504512 | bytes 38535168 | tf_op jit(solution)/shard_map/finish/pallas_call | solution.py:278
  859.2 7.4 all-to-all-done.3.refs_9_
  866.7 7.8 finish.3
  (1 shorter events, 0.0 us)
Async XLA Ops:
  9.8 102.5 %all-to-all-start = ((bf16[32,2,4,64,128]{4,3,2,1,0:T(8,128)(2,1)}), bf16[32,2,4,64,128]{4,3,2,1,0:T(8,128)(2,1)}, u32[]{:S(2)}, u32[]{:S(2)}) async-start(bf16[32,2,4,64,128]{4,3,2,1,0:T(8,128)(2,1)} %lift.2), calls=%async_computation | async-start | bytes 8388608 | tf_op jit(solution)/shard_map/all_to_all | solution.py:332
  33.0 83.1 %copy-start.1 = (f32[144]{0:T(256)S(1)}, f32[144]{0:T(256)}, u32[]{:S(2)}) copy-start(f32[144]{0:T(256)} %param.15) | copy-start | bytes 1732
  112.3 323.6 %all-to-all-start.2 = ((bf16[32,2,14,64,128]{4,3,2,1,0:T(8,128)(2,1)}), bf16[32,2,14,64,128]{4,3,2,1,0:T(8,128)(2,1)}, u32[]{:S(2)}, u32[]{:S(2)}) async-start(bf16[32,2,14,64,128]{4,3,2,1,0:T(8,128)(2,1)} %lift.3), calls=%async_computation.2 | async-start | bytes 29360128 | tf_op jit(solution)/shard_map/all_to_all | solution.py:332
  138.0 301.6 %copy-start.2 = (f32[18]{0:T(128)S(1)}, f32[18]{0:T(128)}, u32[]{:S(2)}) copy-start(f32[18]{0:T(128)} %dynamic_slice.3) | copy-start | bytes 220
  435.8 98.7 %all-to-all-start.1 = ((bf16[32,2,4,64,128]{4,3,2,1,0:T(8,128)(2,1)}), bf16[32,2,4,64,128]{4,3,2,1,0:T(8,128)(2,1)}, u32[]{:S(2)}, u32[]{:S(2)}) async-start(bf16[32,2,4,64,128]{4,3,2,1,0:T(8,128)(2,1)} %planes.2.refs_6_), calls=%async_computation.1 | async-start | bytes 8388608 | tf_op jit(solution)/shard_map/all_to_all | solution.py:332
  534.5 287.7 %copy-start = (f32[384]{0:T(512)S(1)}, f32[384]{0:T(512)}, u32[]{:S(2)}) copy-start(f32[384]{0:T(512)} %param.16) | copy-start | bytes 4612
  818.7 47.9 %all-to-all-start.3 = ((bf16[32,2,14,8,128]{4,3,2,1,0:T(8,128)(2,1)}), bf16[32,2,14,8,128]{4,3,2,1,0:T(8,128)(2,1)}, u32[]{:S(2)}, u32[]{:S(2)}) async-start(bf16[32,2,14,8,128]{4,3,2,1,0:T(8,128)(2,1)} %get-tuple-element.6), calls=%async_computation.3 | async-start | bytes 3670016 | tf_op jit(solution)/shard_map/all_to_all | solution.py:332
  822.8 1.4 copy-start.3

commit v8 on v7

--- a/solution.py
+++ b/solution.py
@@ -108,17 +108,16 @@
 
 
 def plane_kernel(
-    col_count, count, strat_ref, along_y_ref, along_x_ref, back_x_ref, back_y_ref, in_ref, *refs
+    slots, count, strat_ref, along_y_ref, along_x_ref, back_x_ref, back_y_ref, in_ref, *refs
 ):
     out_refs = refs[-count:]
-    blocks, _, depth, modes_x, lanes = in_ref.shape
-    row_count = blocks // col_count
+    _, _, depth, modes_x, lanes = in_ref.shape
     for level in range(depth):
         grids = []
         for field in range(2):
             rows = []
-            for row in range(row_count):
-                parts = [in_ref[col * row_count + row, field, level] for col in range(col_count)]
+            for cols in slots:
+                parts = [in_ref[slot, field, level] for slot in cols]
                 rows.append(jnp.concatenate(parts, axis=1))
             middle = jnp.dot(
                 jnp.concatenate(rows, axis=0), along_y_ref[...], preferred_element_type=F32
@@ -132,23 +131,24 @@
         for field, flux in enumerate((flux_buoy, flux_vel)):
             folded = jnp.dot(back_x_ref[...], flux, preferred_element_type=F32).astype(BF16)
             values = jnp.dot(folded, back_y_ref[...], preferred_element_type=F32).astype(BF16)
-            for row in range(row_count):
+            for row, cols in enumerate(slots):
                 first = row * modes_x
                 for out_ref in out_refs:
                     last = first + out_ref.shape[3]
-                    for col in range(col_count):
-                        out_ref[col * row_count + row, field, level] = values[
+                    for col, slot in enumerate(cols):
+                        out_ref[slot, field, level] = values[
                             first:last, col * lanes : (col + 1) * lanes
                         ]
                     first = last
 
 
-def planes(kernels, arrived, strat, along_y, along_x, back_x, back_y, col_count, splits, after):
+def planes(kernels, arrived, strat, along_y, along_x, back_x, back_y, slots, splits, after):
     blocks, fields, depth, modes_x, modes_y = arrived.shape
-    row_count = blocks // col_count
+    row_count, col_count = len(slots), len(slots[0])
     if not kernels:
-        parts = arrived.reshape(col_count, row_count, fields, depth, modes_x, modes_y)
-        parts = jnp.transpose(parts, (2, 3, 1, 4, 0, 5))
+        parts = arrived[np.array(slots).reshape(-1)]
+        parts = parts.reshape(row_count, col_count, fields, depth, modes_x, modes_y)
+        parts = jnp.transpose(parts, (2, 3, 0, 4, 1, 5))
         parts = parts.reshape(fields, depth, row_count * modes_x, col_count * modes_y)
         middle = jnp.einsum("fzak,ky->fzay", parts, along_y, preferred_element_type=F32)
         grids = jnp.einsum("xa,fzay->fzxy", along_x, middle.astype(BF16), preferred_element_type=F32)
@@ -161,12 +161,13 @@
         values = values.astype(BF16).reshape(
             fields, depth, row_count, modes_x, col_count, modes_y
         )
-        values = jnp.transpose(values, (4, 2, 0, 1, 3, 5)).reshape(arrived.shape)
+        values = jnp.transpose(values, (2, 4, 0, 1, 3, 5)).reshape(arrived.shape)
+        values = values[np.argsort(np.array(slots).reshape(-1))]
         return jnp.split(values, np.cumsum(splits)[:-1], axis=3)
     block = pl.BlockSpec((blocks, fields, 1, modes_x, modes_y), lambda z: (0, 0, z, 0, 0))
     work = along_y.size * along_x.shape[1] + along_x.size * along_y.shape[1]
     return pl.pallas_call(
-        lambda *refs: plane_kernel(col_count, len(splits), *refs),
+        lambda *refs: plane_kernel(slots, len(splits), *refs),
         grid=(depth,),
         in_specs=[
             pl.BlockSpec(memory_space=pltpu.SMEM),
@@ -326,10 +327,27 @@
     def by_device(table):
         table = table.reshape(col_count, shard, degree)
         table = np.pad(table, ((0, 0), (0, padding), (0, 0)))
-        return table.reshape(blocks, own, degree)
+        table = table.reshape(col_count, row_count // pair, pair, own, degree)
+        return np.transpose(table, (2, 0, 1, 3, 4)).reshape(blocks, own, degree)
+
+
+    pair = 2 if row_count % 2 == 0 else 1
+
+    def slot_of(row, col):
+        return (row % pair * col_count + col) * (row_count // pair) + row // pair
+
+    slots = [[slot_of(row, col) for col in range(col_count)] for row in range(row_count)]
+    group = np.argsort(np.array(slots).reshape(-1)).tolist()
 
     def exchange(values):
-        return lax.all_to_all(values, ("col", "row"), split_axis=0, concat_axis=0, tiled=True)
+        return lax.all_to_all(
+            values,
+            ("row", "col"),
+            split_axis=0,
+            concat_axis=0,
+            axis_index_groups=[group],
+            tiled=True,
+        )
 
     levels, slopes, projector = cheb_tables(degree, shard * col_count)
     forward_z = np.stack([by_device(levels.T), by_device(slopes.T)])
@@ -359,7 +377,7 @@
             along_x,
             back_x,
             back_y,
-            col_count,
+            slots,
             splits,
             after,
         )

time: 875 us -> 878 us (level)
  starting transfers between devices: 18.4 us -> 33 us
  waiting for transfers between devices: 412 us -> 400 us
    all_to_all x4, starting transfers between devices: 18.4 us -> 33 us  [exchange(): lax.all_to_all(values, ('row', 'col'), split_axis=0, concat_axis=0, axis_...]
    all_to_all x4, waiting for transfers between devices: 412 us -> 400 us  [exchange(): lax.all_to_all(values, ('row', 'col'), split_axis=0, concat_axis=0, axis_...]
where the time goes in v8:
time: 878 us
  waiting for transfers between devices  400 us (46%)
  blocking collectives  285 us (32%)
  Pallas kernels  156 us (18%)
  starting transfers between devices  33 us (4%)
    all_to_all x4, waiting for transfers between devices, exchange(): lax.all_to_all(values, ('row', 'col'), split_axis=0, concat_axis=0, axis_...  400 us
    all_to_all x1, blocking collectives, exchange(): lax.all_to_all(values, ('row', 'col'), split_axis=0, concat_axis=0, axis_...  285 us
    pallas_call x2, Pallas kernels, planes(): pl.pallas_call(lambda *refs: plane_kernel(slots, len(splits), *refs), gri...  88.4 us
    pallas_call x2, Pallas kernels, finish(): pl.pallas_call(lambda *refs: finish_kernel(len(parts), *refs), grid=(size...  42.9 us
    all_to_all x4, starting transfers between devices, exchange(): lax.all_to_all(values, ('row', 'col'), split_axis=0, concat_axis=0, axis_...  33 us
    pallas_call x2, Pallas kernels, lift(): pl.pallas_call(lift_kernel, grid=(modes_x // span,), in_specs=[pl.BlockSp...  25 us
  transfers between devices with their start and end apart: 4, of which 4 were waited for; matrix products, arithmetic and copies ran while one was open for 0% of the time, Pallas kernels for 16%

profile of v8, /device:TPU:0, one launch (start us, length us, event | category | flops | bytes accessed | tf_op | source)
XLA Modules:
  0.0 878.0 jit_solution(10287736691557342221)
XLA Ops:
  0.6 9.1 %lift.2 = bf16[32,2,4,64,128]{4,3,2,1,0:T(8,128)(2,1)} custom-call(bf16[64,128,384]{2,1,0:T(8,128)(2,1)} %refs_7_.3, bf16[64,128,384]{2,1,0:T(8,128)(2,1)} %refs_6_.3, bf16[2,128,384]{2,1,0:T(8,128)(2,1)} %constant.64.clone.table_ref), custom_call_target="tpu_custom_call" | custom-call | flops 1610612736 | bytes 16777216 | tf_op jit(solution)/shard_map/lift/pallas_call | solution.py:90
  9.8 7.4 all-to-all-start
  17.2 15.8 %lift.3 = bf16[32,2,14,64,128]{4,3,2,1,0:T(8,128)(2,1)} custom-call(bf16[64,128,384]{2,1,0:T(8,128)(2,1)} %refs_7_.3, bf16[64,128,384]{2,1,0:T(8,128)(2,1)} %refs_6_.3, bf16[2,448,384]{2,1,0:T(8,128)(2,1)} %constant.65.clone.table_ref), custom_call_target="tpu_custom_call" | custom-call | flops 5637144576 | bytes 27262976 | tf_op jit(solution)/shard_map/lift/pallas_call | solution.py:90
  33.0 0.0 copy-start.1
  33.0 76.6 %all-to-all-done.refs_5_ = bf16[32,2,4,64,128]{4,3,2,1,0:T(8,128)(2,1)} async-done(((bf16[32,2,4,64,128]{4,3,2,1,0:T(8,128)(2,1)}), bf16[32,2,4,64,128]{4,3,2,1,0:T(8,128)(2,1)}, u32[]{:S(2)}, u32[]{:S(2)}) %all-to-all-start) | async-done | bytes 4194336 | tf_op jit(solution)/shard_map/all_to_all | solution.py:343
  109.7 4.7 all-to-all-start.2
  114.3 0.0 copy-done.1
  114.4 0.6 dynamic_slice.3
  114.9 21.3 %planes.2.refs_6_ = bf16[32,2,4,64,128]{4,3,2,1,0:T(8,128)(2,1)} custom-call(f32[4]{0:T(128)} %bitcast.2, bf16[512,768]{1,0:T(8,128)(2,1)} %constant.62.clone.refs_1_, bf16[768,512]{1,0:T(8,128)(2,1)} %constant.60.clone.refs_2_, bf16[512,768]{1,0:T(8,128)(2,1)} %constant.61.clone.refs_3_, bf16[768,512]{1,0:T(8,128)(2,1)} %constant.63.clone.refs_4_, ...), custom_call_target="tpu_custom_call" | custom-call | flops 16106127360 | bytes 8388608 | tf_op jit(solution)/shard_map/planes/pallas_call | solution.py:169
  136.3 0.0 copy-start.2
  136.3 292.1 %all-to-all-done.2.refs_5_ = bf16[32,2,14,64,128]{4,3,2,1,0:T(8,128)(2,1)} async-done(((bf16[32,2,14,64,128]{4,3,2,1,0:T(8,128)(2,1)}), bf16[32,2,14,64,128]{4,3,2,1,0:T(8,128)(2,1)}, u32[]{:S(2)}, u32[]{:S(2)}) %all-to-all-start.2) | async-done | bytes 14680096 | tf_op jit(solution)/shard_map/all_to_all | solution.py:343
  428.4 17.5 %all-to-all-start.1 = ((bf16[32,2,4,64,128]{4,3,2,1,0:T(8,128)(2,1)}), bf16[32,2,4,64,128]{4,3,2,1,0:T(8,128)(2,1)}, u32[]{:S(2)}, u32[]{:S(2)}) async-start(bf16[32,2,4,64,128]{4,3,2,1,0:T(8,128)(2,1)} %planes.2.refs_6_), calls=%async_computation.1 | async-start | bytes 8388608 | tf_op jit(solution)/shard_map/all_to_all | solution.py:343
  445.9 0.0 copy-done.2
  445.9 0.6 slice.14.refs_0_
  446.5 67.0 %planes.3 = (bf16[32,2,14,56,128]{4,3,2,1,0:T(8,128)(2,1)}, bf16[32,2,14,8,128]{4,3,2,1,0:T(8,128)(2,1)}) custom-call(f32[14]{0:T(128)} %slice.14.refs_0_, bf16[512,768]{1,0:T(8,128)(2,1)} %constant.62.clone.refs_1_, bf16[768,512]{1,0:T(8,128)(2,1)} %constant.60.clone.refs_2_, bf16[512,768]{1,0:T(8,128)(2,1)} %constant.61.clone.refs_3_, ...), custom_call_target="tpu_custom_call" | custom-call | flops 56371445760 | bytes 29360128 | tf_op jit(solution)/shard_map/planes/pallas_call | solution.py:169
  513.5 24.7 %all-to-all-done.1.refs_8_ = bf16[32,2,4,64,128]{4,3,2,1,0:T(8,128)(2,1)} async-done(((bf16[32,2,4,64,128]{4,3,2,1,0:T(8,128)(2,1)}), bf16[32,2,4,64,128]{4,3,2,1,0:T(8,128)(2,1)}, u32[]{:S(2)}, u32[]{:S(2)}) %all-to-all-start.1) | async-done | bytes 4194336 | tf_op jit(solution)/shard_map/all_to_all | solution.py:343
  538.3 0.0 copy-start
  538.3 285.2 %all_to_all.25.refs_9_ = bf16[32,2,14,56,128]{4,3,2,1,0:T(8,128)(2,1)} all-to-all(bf16[32,2,14,56,128]{4,3,2,1,0:T(8,128)(2,1)} %get-tuple-element.7), channel_id=1, replica_groups={{0,8,16,24,1,9,17,25,2,10,18,26,3,11,19,27,4,12,20,28,5,13,21,29,6,14,2..., dimensions={0} | all-to-all | bytes 25690112 | tf_op jit(solution)/shard_map/all_to_all | solution.py:343
  823.5 3.4 all-to-all-start.3
  826.9 0.0 copy-done
  826.9 0.6 broadcast_in_dim.2.refs_2_
  827.6 0.0 copy-start.3
  827.6 0.7 slice.12.refs_0_
  828.2 0.7 fusion.3.refs_1_
  828.9 0.0 copy-done.3
  828.9 35.1 %finish.2 = (bf16[64,128,384]{2,1,0:T(8,128)(2,1)}, bf16[64,128,384]{2,1,0:T(8,128)(2,1)}) custom-call(f32[56]{0:T(128)} %bitcast.3, f32[128,1]{1,0:T(8,128)} %fusion.3.refs_1_, f32[1,384]{1,0:T(1,128)} %broadcast_in_dim.2.refs_2_, bf16[384,384]{1,0:T(8,128)(2,1)} %refs_3_.5, bf16[384,384]{1,0:T(8,128)(2,1)} %refs_4_.5, ...), custom_call_target="tpu_custom_call" | custom-call | flops 14797504512 | bytes 38535168 | tf_op jit(solution)/shard_map/finish/pallas_call | solution.py:279
  864.0 6.2 all-to-all-done.3.refs_9_
  870.2 7.8 finish.3
  (1 shorter events, 0.0 us)
Async XLA Ops:
  9.8 99.9 %all-to-all-start = ((bf16[32,2,4,64,128]{4,3,2,1,0:T(8,128)(2,1)}), bf16[32,2,4,64,128]{4,3,2,1,0:T(8,128)(2,1)}, u32[]{:S(2)}, u32[]{:S(2)}) async-start(bf16[32,2,4,64,128]{4,3,2,1,0:T(8,128)(2,1)} %lift.2), calls=%async_computation | async-start | bytes 8388608 | tf_op jit(solution)/shard_map/all_to_all | solution.py:343
  33.0 81.3 %copy-start.1 = (f32[144]{0:T(256)S(1)}, f32[144]{0:T(256)}, u32[]{:S(2)}) copy-start(f32[144]{0:T(256)} %param.15) | copy-start | bytes 1732
  109.7 318.8 %all-to-all-start.2 = ((bf16[32,2,14,64,128]{4,3,2,1,0:T(8,128)(2,1)}), bf16[32,2,14,64,128]{4,3,2,1,0:T(8,128)(2,1)}, u32[]{:S(2)}, u32[]{:S(2)}) async-start(bf16[32,2,14,64,128]{4,3,2,1,0:T(8,128)(2,1)} %lift.3), calls=%async_computation.2 | async-start | bytes 29360128 | tf_op jit(solution)/shard_map/all_to_all | solution.py:343
  136.3 309.6 %copy-start.2 = (f32[18]{0:T(128)S(1)}, f32[18]{0:T(128)}, u32[]{:S(2)}) copy-start(f32[18]{0:T(128)} %dynamic_slice.3) | copy-start | bytes 220
  428.4 109.9 %all-to-all-start.1 = ((bf16[32,2,4,64,128]{4,3,2,1,0:T(8,128)(2,1)}), bf16[32,2,4,64,128]{4,3,2,1,0:T(8,128)(2,1)}, u32[]{:S(2)}, u32[]{:S(2)}) async-start(bf16[32,2,4,64,128]{4,3,2,1,0:T(8,128)(2,1)} %planes.2.refs_6_), calls=%async_computation.1 | async-start | bytes 8388608 | tf_op jit(solution)/shard_map/all_to_all | solution.py:343
  538.3 288.7 %copy-start = (f32[384]{0:T(512)S(1)}, f32[384]{0:T(512)}, u32[]{:S(2)}) copy-start(f32[384]{0:T(512)} %param.16) | copy-start | bytes 4612
  823.5 46.7 %all-to-all-start.3 = ((bf16[32,2,14,8,128]{4,3,2,1,0:T(8,128)(2,1)}), bf16[32,2,14,8,128]{4,3,2,1,0:T(8,128)(2,1)}, u32[]{:S(2)}, u32[]{:S(2)}) async-start(bf16[32,2,14,8,128]{4,3,2,1,0:T(8,128)(2,1)} %get-tuple-element.6), calls=%async_computation.3 | async-start | bytes 3670016 | tf_op jit(solution)/shard_map/all_to_all | solution.py:343
  827.6 1.4 copy-start.3

commit v9 on v7

--- a/solution.py
+++ b/solution.py
@@ -73,7 +73,7 @@
         values = lax.dot_general(
             table_ref[field], coeffs, (((1,), (1,)), ((), ())), preferred_element_type=F32
         )
-        values = values.reshape(blocks * depth, span, lanes).astype(BF16)
+        values = values.astype(BF16).reshape(blocks * depth, span, lanes)
         out_ref[:, field] = values.reshape(blocks, depth, span, lanes)
 
 
@@ -206,8 +206,7 @@
 def project(refs, field, proj_ref):
     blocks, _, _, span, lanes = refs[0].shape
     parts = [ref[:, field].reshape(blocks * ref.shape[2], span, lanes) for ref in refs]
-    fluxes = jnp.concatenate(parts, axis=0).astype(F32)
-    fluxes = jnp.swapaxes(fluxes, 0, 1).astype(BF16)
+    fluxes = jnp.swapaxes(jnp.concatenate(parts, axis=0), 0, 1)
     rows = [jnp.transpose(fluxes[mode]) for mode in range(span)]
     return jnp.dot(jnp.concatenate(rows, axis=0), proj_ref[...], preferred_element_type=F32)
 

time: 875 us -> 874 us (level)
  transfers between devices with their start and end apart: 4 -> 4, of which waited for: 4 -> 4; matrix products, arithmetic and copies ran while one was open for 0% -> 0% of each run, Pallas kernels for 16% -> 15%
where the time goes in v9:
time: 874 us
  waiting for transfers between devices  416 us (48%)
  blocking collectives  284 us (32%)
  Pallas kernels  151 us (17%)
  starting transfers between devices  18.4 us (2%)
    all_to_all x4, waiting for transfers between devices, exchange(): lax.all_to_all(values, ('col', 'row'), split_axis=0, concat_axis=0, tiled...  416 us
    all_to_all x1, blocking collectives, exchange(): lax.all_to_all(values, ('col', 'row'), split_axis=0, concat_axis=0, tiled...  284 us
    pallas_call x2, Pallas kernels, planes(): pl.pallas_call(lambda *refs: plane_kernel(col_count, len(splits), *refs),...  88.4 us
    pallas_call x2, Pallas kernels, finish(): pl.pallas_call(lambda *refs: finish_kernel(len(parts), *refs), grid=(size...  40 us
    pallas_call x2, Pallas kernels, lift(): pl.pallas_call(lift_kernel, grid=(modes_x // span,), in_specs=[pl.BlockSp...  23.1 us
    all_to_all x4, starting transfers between devices, exchange(): lax.all_to_all(values, ('col', 'row'), split_axis=0, concat_axis=0, tiled...  18.4 us
  transfers between devices with their start and end apart: 4, of which 4 were waited for; matrix products, arithmetic and copies ran while one was open for 0% of the time, Pallas kernels for 15%

profile of v9, /device:TPU:0, one launch (start us, length us, event | category | flops | bytes accessed | tf_op | source)
XLA Modules:
  0.0 874.1 jit_solution(1470529609380538208)
XLA Ops:
  0.6 8.9 %lift.2 = bf16[32,2,4,64,128]{4,3,2,1,0:T(8,128)(2,1)} custom-call(bf16[64,128,384]{2,1,0:T(8,128)(2,1)} %refs_7_.3, bf16[64,128,384]{2,1,0:T(8,128)(2,1)} %refs_6_.3, bf16[2,128,384]{2,1,0:T(8,128)(2,1)} %constant.64.clone.table_ref), custom_call_target="tpu_custom_call" | custom-call | flops 1610612736 | bytes 16777216 | tf_op jit(solution)/shard_map/lift/pallas_call | solution.py:90
  9.5 7.4 all-to-all-start
  16.9 14.2 %lift.3 = bf16[32,2,14,64,128]{4,3,2,1,0:T(8,128)(2,1)} custom-call(bf16[64,128,384]{2,1,0:T(8,128)(2,1)} %refs_7_.3, bf16[64,128,384]{2,1,0:T(8,128)(2,1)} %refs_6_.3, bf16[2,448,384]{2,1,0:T(8,128)(2,1)} %constant.65.clone.table_ref), custom_call_target="tpu_custom_call" | custom-call | flops 5637144576 | bytes 27262976 | tf_op jit(solution)/shard_map/lift/pallas_call | solution.py:90
  31.1 0.0 copy-start.1
  31.1 80.8 %all-to-all-done.refs_5_ = bf16[32,2,4,64,128]{4,3,2,1,0:T(8,128)(2,1)} async-done(((bf16[32,2,4,64,128]{4,3,2,1,0:T(8,128)(2,1)}), bf16[32,2,4,64,128]{4,3,2,1,0:T(8,128)(2,1)}, u32[]{:S(2)}, u32[]{:S(2)}) %all-to-all-start) | async-done | bytes 4194336 | tf_op jit(solution)/shard_map/all_to_all | solution.py:331
  112.0 3.8 all-to-all-start.2
  115.8 0.0 copy-done.1
  115.8 0.6 dynamic_slice.3
  116.4 21.3 %planes.2.refs_6_ = bf16[32,2,4,64,128]{4,3,2,1,0:T(8,128)(2,1)} custom-call(f32[4]{0:T(128)} %bitcast.2, bf16[512,768]{1,0:T(8,128)(2,1)} %constant.62.clone.refs_1_, bf16[768,512]{1,0:T(8,128)(2,1)} %constant.60.clone.refs_2_, bf16[512,768]{1,0:T(8,128)(2,1)} %constant.61.clone.refs_3_, bf16[768,512]{1,0:T(8,128)(2,1)} %constant.63.clone.refs_4_, ...), custom_call_target="tpu_custom_call" | custom-call | flops 16106127360 | bytes 8388608 | tf_op jit(solution)/shard_map/planes/pallas_call | solution.py:168
  137.8 0.0 copy-start.2
  137.8 297.8 %all-to-all-done.2.refs_5_ = bf16[32,2,14,64,128]{4,3,2,1,0:T(8,128)(2,1)} async-done(((bf16[32,2,14,64,128]{4,3,2,1,0:T(8,128)(2,1)}), bf16[32,2,14,64,128]{4,3,2,1,0:T(8,128)(2,1)}, u32[]{:S(2)}, u32[]{:S(2)}) %all-to-all-start.2) | async-done | bytes 14680096 | tf_op jit(solution)/shard_map/all_to_all | solution.py:331
  435.6 3.6 all-to-all-start.1
  439.1 0.0 copy-done.2
  439.1 0.6 slice.14.refs_0_
  439.7 67.0 %planes.3 = (bf16[32,2,14,56,128]{4,3,2,1,0:T(8,128)(2,1)}, bf16[32,2,14,8,128]{4,3,2,1,0:T(8,128)(2,1)}) custom-call(f32[14]{0:T(128)} %slice.14.refs_0_, bf16[512,768]{1,0:T(8,128)(2,1)} %constant.62.clone.refs_1_, bf16[768,512]{1,0:T(8,128)(2,1)} %constant.60.clone.refs_2_, bf16[512,768]{1,0:T(8,128)(2,1)} %constant.61.clone.refs_3_, ...), custom_call_target="tpu_custom_call" | custom-call | flops 56371445760 | bytes 29360128 | tf_op jit(solution)/shard_map/planes/pallas_call | solution.py:168
  506.8 27.4 %all-to-all-done.1.refs_8_ = bf16[32,2,4,64,128]{4,3,2,1,0:T(8,128)(2,1)} async-done(((bf16[32,2,4,64,128]{4,3,2,1,0:T(8,128)(2,1)}), bf16[32,2,4,64,128]{4,3,2,1,0:T(8,128)(2,1)}, u32[]{:S(2)}, u32[]{:S(2)}) %all-to-all-start.1) | async-done | bytes 4194336 | tf_op jit(solution)/shard_map/all_to_all | solution.py:331
  534.2 0.0 copy-start
  534.2 284.3 %all_to_all.25.refs_9_ = bf16[32,2,14,56,128]{4,3,2,1,0:T(8,128)(2,1)} all-to-all(bf16[32,2,14,56,128]{4,3,2,1,0:T(8,128)(2,1)} %get-tuple-element.7), channel_id=1, replica_groups=mesh['row'=8,'col'=4] {'col','row'}, dimensions={0} | all-to-all | bytes 25690112 | tf_op jit(solution)/shard_map/all_to_all | solution.py:331
  818.5 3.6 all-to-all-start.3
  822.1 0.0 copy-done
  822.1 0.6 broadcast_in_dim.2.refs_2_
  822.7 0.0 copy-start.3
  822.7 0.7 slice.12.refs_0_
  823.4 0.7 fusion.3.refs_1_
  824.1 0.0 copy-done.3
  824.1 32.5 %finish.2 = (bf16[64,128,384]{2,1,0:T(8,128)(2,1)}, bf16[64,128,384]{2,1,0:T(8,128)(2,1)}) custom-call(f32[56]{0:T(128)} %bitcast.3, f32[128,1]{1,0:T(8,128)} %fusion.3.refs_1_, f32[1,384]{1,0:T(1,128)} %broadcast_in_dim.2.refs_2_, bf16[384,384]{1,0:T(8,128)(2,1)} %refs_3_.5, bf16[384,384]{1,0:T(8,128)(2,1)} %refs_4_.5, ...), custom_call_target="tpu_custom_call" | custom-call | flops 14797504512 | bytes 38535168 | tf_op jit(solution)/shard_map/finish/pallas_call | solution.py:277
  856.6 10.0 %all-to-all-done.3.refs_9_ = bf16[32,2,14,8,128]{4,3,2,1,0:T(8,128)(2,1)} async-done(((bf16[32,2,14,8,128]{4,3,2,1,0:T(8,128)(2,1)}), bf16[32,2,14,8,128]{4,3,2,1,0:T(8,128)(2,1)}, u32[]{:S(2)}, u32[]{:S(2)}) %all-to-all-start.3) | async-done | bytes 1835040 | tf_op jit(solution)/shard_map/all_to_all | solution.py:331
  866.6 7.5 finish.3
  (1 shorter events, 0.0 us)
Async XLA Ops:
  9.5 102.5 %all-to-all-start = ((bf16[32,2,4,64,128]{4,3,2,1,0:T(8,128)(2,1)}), bf16[32,2,4,64,128]{4,3,2,1,0:T(8,128)(2,1)}, u32[]{:S(2)}, u32[]{:S(2)}) async-start(bf16[32,2,4,64,128]{4,3,2,1,0:T(8,128)(2,1)} %lift.2), calls=%async_computation | async-start | bytes 8388608 | tf_op jit(solution)/shard_map/all_to_all | solution.py:331
  31.1 84.7 %copy-start.1 = (f32[144]{0:T(256)S(1)}, f32[144]{0:T(256)}, u32[]{:S(2)}) copy-start(f32[144]{0:T(256)} %param.15) | copy-start | bytes 1732
  112.0 323.6 %all-to-all-start.2 = ((bf16[32,2,14,64,128]{4,3,2,1,0:T(8,128)(2,1)}), bf16[32,2,14,64,128]{4,3,2,1,0:T(8,128)(2,1)}, u32[]{:S(2)}, u32[]{:S(2)}) async-start(bf16[32,2,14,64,128]{4,3,2,1,0:T(8,128)(2,1)} %lift.3), calls=%async_computation.2 | async-start | bytes 29360128 | tf_op jit(solution)/shard_map/all_to_all | solution.py:331
  137.8 301.4 %copy-start.2 = (f32[18]{0:T(128)S(1)}, f32[18]{0:T(128)}, u32[]{:S(2)}) copy-start(f32[18]{0:T(128)} %dynamic_slice.3) | copy-start | bytes 220
  435.6 98.6 %all-to-all-start.1 = ((bf16[32,2,4,64,128]{4,3,2,1,0:T(8,128)(2,1)}), bf16[32,2,4,64,128]{4,3,2,1,0:T(8,128)(2,1)}, u32[]{:S(2)}, u32[]{:S(2)}) async-start(bf16[32,2,4,64,128]{4,3,2,1,0:T(8,128)(2,1)} %planes.2.refs_6_), calls=%async_computation.1 | async-start | bytes 8388608 | tf_op jit(solution)/shard_map/all_to_all | solution.py:331
  534.2 287.9 %copy-start = (f32[384]{0:T(512)S(1)}, f32[384]{0:T(512)}, u32[]{:S(2)}) copy-start(f32[384]{0:T(512)} %param.16) | copy-start | bytes 4612
  818.5 48.1 %all-to-all-start.3 = ((bf16[32,2,14,8,128]{4,3,2,1,0:T(8,128)(2,1)}), bf16[32,2,14,8,128]{4,3,2,1,0:T(8,128)(2,1)}, u32[]{:S(2)}, u32[]{:S(2)}) async-start(bf16[32,2,14,8,128]{4,3,2,1,0:T(8,128)(2,1)} %get-tuple-element.6), calls=%async_computation.3 | async-start | bytes 3670016 | tf_op jit(solution)/shard_map/all_to_all | solution.py:331
  822.7 1.4 copy-start.3
